TPU v7x, 256 devices: a whole 4x4x8 slice. The times are simulated.
256 devices in a mesh: dp: 32 (over z, y_lo, core), tensor: 8 (over y_hi, x).
Axes of the slice: x: 4, y: 4 (y_hi: 2, y_lo: 2; y = y_hi * 2 + y_lo), z: 8, core: 2. Of those that a mesh axis runs over, the one named last changes fastest.
Arguments:
- rollout_q: bfloat16 [34048, 4096], P('dp', 'tensor'), may hold values from -60 to 60
- rollout_k: bfloat16 [34048, 1024], P('dp', 'tensor'), may hold values from -8 to 8
- rollout_value_rows: bfloat16 [34048, 1024], P('dp', 'tensor'), may hold values from -6 to 6
- q_gain: float32 [128], replicated, may hold values from 0.5 to 6
- k_gain: float32 [128], replicated, may hold values from 0.5 to 6
- out_weight: bfloat16 [5120, 4096], P('dp', 'tensor'), may hold values from -0.09375 to 0.09375
- cotangent: bfloat16 [21504, 5120], P('dp', 'tensor'), may hold values from -6 to 6
- seq_lengths: int32 [192], replicated, may hold values from 28 to 196, as said below
- seq_source: int32 [192], replicated, may hold values from 0 to 31, as said below
Outputs:
- layer_out: bfloat16 [21504, 5120], P('dp', 'tensor')
- query_grad: bfloat16 [21504, 4096], P('dp', 'tensor')
- key_grad: bfloat16 [21504, 1024], P('dp', 'tensor')
- packed_value_gradient: bfloat16 [21504, 1024], P('dp', 'tensor')
- weight_grad: float32 [5120, 4096], P('dp', 'tensor')
Inputs may be any that keep to these rules, and one draw needn't show every extreme that they name: `seq_lengths`: the 6 rollouts of each data shard hold exactly 672 tokens together. `seq_source`: never falling along the rollouts. A source holds the rollouts of its own shard and at most the last rollout of the shard before it and the first of the shard after it; its rollouts lie end to end from its first row in order, and at least one source holds exactly 1064 tokens in every draw.
All inputs are finite; a program needn't handle non-finite values.
Results may differ from a plain program's by a relative error of at most 0.029.
The roundings to bfloat16 on the way count: a program that leaves them out, or rounds other values in their place, can miss the bound.
Values may be sent and summed in bfloat16 or wider, within the bound.
No kernel may reach another device: no remote copies, remote signals or barrier semaphores. Data moves between devices by JAX's collectives and lax.ppermute only.
A program may use at most 128 MiB of HBM per device.

v0:
```python
import math

import jax
import jax.numpy as jnp
from jax import lax
from jax.sharding import PartitionSpec as P

NORM_EPS = 1e-06


def passed_along(value, axis, steps):
    count = lax.axis_size(axis)
    initial, last = (max(0, -steps), min(count, count - steps))
    return lax.ppermute(value, axis, [(source, source + steps) for source in range(initial, last)])


def rms_norm(entries, gain):
    mean_sq = jnp.mean(entries * entries, axis=-1, keepdims=True)
    return entries * lax.rsqrt(mean_sq + NORM_EPS) * gain


def elementwise_result(form, left, right):
    return jnp.einsum(form, left, right, preferred_element_type=jnp.float32)


def attend(q_rows, k_rows, v_rows, grad_rows, segment, position, q_gain, k_gain):
    head_dim = q_gain.shape[0]
    row_sum_total = q_rows.shape[0]
    kv_heads = k_rows.shape[1] // head_dim
    queries_per_group = q_rows.shape[1] // k_rows.shape[1]
    query_f32 = q_rows.astype(jnp.float32).reshape(
        row_sum_total, kv_heads, queries_per_group, head_dim
    )
    key_f32 = k_rows.astype(jnp.float32).reshape(row_sum_total, kv_heads, head_dim)
    normalized_queries = rms_norm(query_f32, q_gain).astype(jnp.bfloat16)
    normalized_keys = rms_norm(key_f32, k_gain).astype(jnp.bfloat16)
    value_rows = v_rows.reshape(row_sum_total, kv_heads, head_dim)
    logit_scale = 1.0 / math.sqrt(head_dim)
    allowed = (segment[:, None] == segment[None, :]) & (position[None, :] <= position[:, None])
    attention_logits = (
        elementwise_result("yepz,jez->epyj", normalized_queries, normalized_keys) * logit_scale
    )
    attention_logits = jnp.where(allowed, attention_logits, -jnp.inf)
    row_max = jnp.max(attention_logits, axis=-1, keepdims=True)
    exp_scores = jnp.exp(attention_logits - row_max)
    attn_probs = exp_scores / jnp.sum(exp_scores, axis=-1, keepdims=True)
    probability_lower = attn_probs.astype(jnp.bfloat16)
    attention_lower = elementwise_result("qecz,zqo->cqeo", probability_lower, value_rows).astype(
        jnp.bfloat16
    )
    output_gradient = grad_rows.reshape(row_sum_total, kv_heads, queries_per_group, head_dim)
    packed_value_gradient = elementwise_result(
        "stnx,nstz->xsz", probability_lower, output_gradient
    ).astype(jnp.bfloat16)
    probability_gradient = elementwise_result("yepz,jez->epyj", output_gradient, value_rows)
    row_delta = jnp.sum(attn_probs * probability_gradient, axis=-1, keepdims=True)
    score_gradient = (attn_probs * (probability_gradient - row_delta) * logit_scale).astype(
        jnp.bfloat16
    )
    normed_query_gradient = elementwise_result("qecz,zqo->cqeo", score_gradient, normalized_keys)
    normed_key_gradient = elementwise_result("stnx,nstz->xsz", score_gradient, normalized_queries)
    query_back = jax.vjp(lambda entries: rms_norm(entries, q_gain), query_f32)[1]
    key_back = jax.vjp(lambda entries: rms_norm(entries, k_gain), key_f32)[1]
    query_grad = query_back(normed_query_gradient)[0].astype(jnp.bfloat16)
    key_grad = key_back(normed_key_gradient)[0].astype(jnp.bfloat16)
    return (
        attention_lower.reshape(row_sum_total, -1),
        query_grad.reshape(row_sum_total, -1),
        key_grad.reshape(row_sum_total, -1),
        packed_value_gradient.reshape(row_sum_total, -1),
    )


def body(
    rollout_q,
    rollout_k,
    rollout_value_rows,
    q_gain,
    k_gain,
    out_weight,
    cotangent,
    seq_lengths,
    seq_source,
):
    shards = lax.axis_size("dp")
    my_shard = lax.axis_index("dp")
    seq_count = seq_lengths.shape[0]
    per_shard = seq_count // shards
    capacity = rollout_q.shape[0]
    tok_rows = cotangent.shape[0]
    seq_order = jnp.arange(seq_count, dtype=jnp.int32)
    earlier = (seq_source[None, :] == seq_source[:, None]) & (
        seq_order[None, :] < seq_order[:, None]
    )
    offsets = jnp.sum(jnp.where(earlier, seq_lengths[None, :], 0), axis=1)
    first_seq = my_shard * per_shard
    my_lengths = lax.dynamic_slice_in_dim(seq_lengths, first_seq, per_shard)
    my_sources = lax.dynamic_slice_in_dim(seq_source, first_seq, per_shard)
    my_offsets = lax.dynamic_slice_in_dim(offsets, first_seq, per_shard)
    starts = jnp.cumsum(my_lengths) - my_lengths
    row_ids = jnp.arange(tok_rows, dtype=jnp.int32)
    segment = jnp.sum((row_ids[:, None] >= starts[None, :]).astype(jnp.int32), axis=1) - 1
    onehot = segment[:, None] == jnp.arange(per_shard, dtype=jnp.int32)[None, :]

    def pick_from(table):
        return jnp.sum(jnp.where(onehot, table[None, :], 0), axis=1)

    position = row_ids - pick_from(starts)
    relative = pick_from(my_sources) - my_shard
    local_row = pick_from(my_offsets) + position
    payload = (rollout_q, rollout_k, rollout_value_rows)
    received = []
    for step_by in (1, -1):
        received.append(passed_along((rollout_q, rollout_k, rollout_value_rows), "dp", step_by))
    row_index = (relative + 1) * capacity + local_row
    packed = tuple(
        (
            jnp.take(
                jnp.concatenate(
                    [received[0][member], payload[member], received[1][member]], axis=0
                ),
                row_index,
                axis=0,
            )
            for member in range(3)
        )
    )
    full_cotan = lax.all_gather(cotangent, "tensor", axis=1, tiled=True)
    grad_attention = jnp.dot(
        full_cotan,
        lax.all_gather(out_weight, "dp", axis=0, tiled=True),
        preferred_element_type=jnp.float32,
    )
    attention, query_grad, key_grad, packed_value_gradient = attend(
        packed[0],
        packed[1],
        packed[2],
        grad_attention.astype(jnp.bfloat16),
        segment,
        position,
        q_gain,
        k_gain,
    )
    head_part = lax.dot_general(
        attention,
        lax.all_gather(out_weight, "dp", axis=0, tiled=True),
        (((1,), (1,)), ((), ())),
        preferred_element_type=jnp.float32,
    )
    layer_out = lax.psum_scatter(
        head_part.astype(jnp.bfloat16), "tensor", scatter_dimension=1, tiled=True
    )
    grad_scale = (tok_rows * shards) ** (-0.5)

    def grad_rows(first_row, row_count):
        term = lax.dot_general(
            full_cotan, attention, (((0,), (0,)), ((), ())), preferred_element_type=jnp.float32
        )
        return term * grad_scale

    weight_grad = lax.psum_scatter(
        grad_rows(jnp.int32(0), lax.axis_size("dp") * out_weight.shape[0]).astype(jnp.bfloat16),
        "dp",
        scatter_dimension=0,
        tiled=True,
    ).astype(jnp.float32)
    return (layer_out, query_grad, key_grad, packed_value_gradient, weight_grad)


def solution(mesh):
    in_specs = (
        P("dp", "tensor"),
        P("dp", "tensor"),
        P("dp", "tensor"),
        P(),
        P(),
        P("dp", "tensor"),
        P("dp", "tensor"),
        P(),
        P(),
    )
    out_specs = (
        P("dp", "tensor"),
        P("dp", "tensor"),
        P("dp", "tensor"),
        P("dp", "tensor"),
        P("dp", "tensor"),
    )
    return jax.shard_map(body, mesh=mesh, in_specs=in_specs, out_specs=out_specs, check_vma=False)
```

profile of v0, /device:TPU:1, one launch (start us, length us, event | category | flops | bytes accessed | tf_op | source)
XLA Modules:
  0.0 454.8 jit_solution(13147781436065219004)
XLA Ops:
  8.7 4.6 %collective-permute-start.2 = (bf16[1064,128]{1,0:T(8,128)(2,1)}, bf16[1064,128]{1,0:T(8,128)(2,1)S(1)}, u32[]{:S(2)}, u32[]{:S(2)}) collective-permute-start(bf16[1064,128]{1,0:T(8,128)(2,1)} %param.12), channel_id=1, source_target_pairs={{0,8},{8,16},{16,24},{24,32},{32,40},{40,48},{48,56},{56,64},{64,7... | collective-permute-start | bytes 817160 | tf_op jit(solution)/shard_map/ppermute | solution.py:14
  13.3 1.9 collective-permute-start.3
  15.2 3.6 collective-permute-start
  18.9 1.9 collective-permute-start.1
  20.8 3.6 collective-permute-start.4
  28.2 1.3 compare_and_fusion
  29.5 1.9 collective-permute-start.5
  32.4 2.0 gather_fusion.2
  35.5 2.5 gather_fusion.1
  38.3 22.4 %collective-permute-done.4 = bf16[1064,512]{1,0:T(8,128)(2,1)S(1)} collective-permute-done((bf16[1064,512]{1,0:T(8,128)(2,1)}, bf16[1064,512]{1,0:T(8,128)(2,1)S(1)}, u32[]{:S(2)}, u32[]{:S(2)}) %collective-permute-start.4) | collective-permute-done | bytes 1089568 | tf_op jit(solution)/shard_map/ppermute | solution.py:14
  61.8 2.0 pad_maximum_fusion
  63.8 3.3 gather_fusion
  67.1 1.7 gather.13
  69.5 3.2 fusion.7
  72.7 1.8 fusion.5
  74.6 3.0 fusion.23
  78.0 52.5 %all-gather.5.cloned.1.call-done = bf16[672,5120]{1,0:T(8,128)(2,1)} async-done(((bf16[672,640]{1,0:T(8,128)(2,1)}), bf16[672,5120]{1,0:T(8,128)(2,1)}) %all-gather.5.cloned.1.call-update) | async-done | bytes 6881296 | tf_op jit(solution)/shard_map/all_gather | solution.py:128
  130.5 9.1 %fusion.6 = bf16[5120,512]{0,1:T(8,128)(2,1)} fusion(bf16[672,5120]{1,0:T(8,128)(2,1)} %all-gather.5.cloned.1.call-done, bf16[84,8,4,128]{3,2,1,0:T(4,128)(2,1)S(1)} %bitcast.177), kind=kOutput, calls=%fused_computation.15 | convolution fusion | flops 3528458240 | bytes 12812288 | tf_op jit(solution)/shard_map/dot_general | solution.py:156
  139.6 7.8 %copy.51 = bf16[5120,512]{1,0:T(8,128)(2,1)} copy(bf16[5120,512]{0,1:T(8,128)(2,1)} %fusion.6) | data formatting | bytes 10485760
  147.4 51.9 %all-gather.3.cloned.1.call-done = bf16[5120,512]{1,0:T(8,128)(2,1)} async-done(((bf16[160,512]{1,0:T(8,128)(2,1)}), bf16[5120,512]{1,0:T(8,128)(2,1)}) %all-gather.3.cloned.1.call-update) | async-done | bytes 5242896 | tf_op jit(solution)/shard_map/all_gather | solution.py:146
  199.3 8.2 %convolution_convert_fusion = bf16[672,5120]{1,0:T(8,128)(2,1)} fusion(bf16[5120,512]{1,0:T(8,128)(2,1)} %all-gather.3.cloned.1.call-done, bf16[84,8,4,128]{3,2,1,0:T(4,128)(2,1)S(1)} %bitcast.178), kind=kOutput, calls=%fused_computation.12 | convolution fusion | flops 3526656000 | bytes 12812288 | tf_op jit(solution)/shard_map/dot_general | solution.py:144
  207.6 10.0 %copy.49 = bf16[672,5120]{0,1:T(8,128)(2,1)} copy(bf16[672,5120]{1,0:T(8,128)(2,1)} %convolution_convert_fusion) | data formatting | bytes 13762560
  217.6 8.4 %fusion.22 = bf16[84,4,8,128]{3,2,1,0:T(8,128)(2,1)S(1)} fusion(bf16[672,5120]{1,0:T(8,128)(2,1)} %all-gather.5.cloned.1.call-done, bf16[5120,512]{1,0:T(8,128)(2,1)} %all-gather.3.cloned.1.call-done), kind=kOutput, calls=%fused_computation.38 | convolution fusion | flops 3523559424 | bytes 12812288 | tf_op jit(solution)/shard_map/dot_general | solution.py:129
  226.0 5.9 %fusion = (f32[4,672]{1,0:T(4,128)S(1)}, f32[672,672,4]{1,0,2:T(8,128)S(1)}) fusion(f32[4,672]{1,0:T(4,128)S(1)} %fusion.5, f32[4,672]{1,0:T(4,128)S(1)} %get-tuple-element.32, f32[672,672,4]{1,0,2:T(8,128)} %copy-done, pred[672,672]{0,1:T(8,128)(4,1)S(1)} %copy-done.1, bf16[84,4,8,128]{3,2,1,0:T(8,128)(2,1)S(1)} %fusion.22, ...), kind=kOutput, calls=%fused_computation.7 | convolution fusion | flops 473343360 | bytes 15795360 | tf_op jit(solution)/shard_map/yepz,jez->epyj/dot_general | solution.py:23
  231.9 2.9 fusion.8
  234.8 2.6 fusion.17
  237.4 1.3 fusion.18
  240.1 1.6 fusion.51
  242.7 3.4 fusion.34
  246.1 76.9 %reduce-scatter.9.cloned.1.call-done = bf16[160,512]{1,0:T(8,128)(2,1)} async-done(((bf16[5120,512]{1,0:T(8,128)(2,1)}), bf16[160,512]{1,0:T(8,128)(2,1)}) %reduce-scatter.9.cloned.1.call-update) | async-done | bytes 163856
  324.9 121.2 %reduce-scatter.7.cloned.1.call-done = bf16[640,672]{1,0:T(8,128)(2,1)} async-done(((bf16[5120,672]{1,0:T(8,128)(2,1)}), bf16[640,672]{1,0:T(8,128)(2,1)}) %reduce-scatter.7.cloned.1.call-update) | async-done | bytes 860176
  446.1 2.2 copy.50
  (60 shorter events, 13.9 us)
Async XLA Ops:
  7.2 123.3 %all-gather.5.cloned.1.call-start = ((), (), s32[]{:S(2)}) async-start(), calls=%async_computation.3 | async-start | bytes 7741440 | tf_op jit(solution)/shard_map/all_gather | solution.py:128
  7.9 191.4 %all-gather.3.cloned.1.call-start = ((), (), s32[]{:S(2)}) async-start(), calls=%async_computation.2 | async-start | bytes 5406720 | tf_op jit(solution)/shard_map/all_gather | solution.py:146
  8.6 314.3 %reduce-scatter.9.cloned.1.call-start = ((), (), s32[]{:S(2)}) async-start(), calls=%async_computation.5 | async-start | bytes 5406720
  8.7 20.8 %collective-permute-start.2 = (bf16[1064,128]{1,0:T(8,128)(2,1)}, bf16[1064,128]{1,0:T(8,128)(2,1)S(1)}, u32[]{:S(2)}, u32[]{:S(2)}) collective-permute-start(bf16[1064,128]{1,0:T(8,128)(2,1)} %param.12), channel_id=1, source_target_pairs={{0,8},{8,16},{16,24},{24,32},{32,40},{40,48},{48,56},{56,64},{64,7... | collective-permute-start | bytes 817160 | tf_op jit(solution)/shard_map/ppermute | solution.py:14
  13.3 18.1 %collective-permute-start.3 = (bf16[1064,128]{1,0:T(8,128)(2,1)}, bf16[1064,128]{1,0:T(8,128)(2,1)S(1)}, u32[]{:S(2)}, u32[]{:S(2)}) collective-permute-start(bf16[1064,128]{1,0:T(8,128)(2,1)} %param.12), channel_id=1, source_target_pairs={{8,0},{16,8},{24,16},{32,24},{40,32},{48,40},{56,48},{64,56},{72,6... | collective-permute-start | bytes 817160 | tf_op jit(solution)/shard_map/ppermute | solution.py:14
  15.2 19.2 %collective-permute-start = (bf16[1064,128]{1,0:T(8,128)(2,1)}, bf16[1064,128]{1,0:T(8,128)(2,1)S(1)}, u32[]{:S(2)}, u32[]{:S(2)}) collective-permute-start(bf16[1064,128]{1,0:T(8,128)(2,1)} %param.13), channel_id=1, source_target_pairs={{0,8},{8,16},{16,24},{24,32},{32,40},{40,48},{48,56},{56,64},{64,7... | collective-permute-start | bytes 817160 | tf_op jit(solution)/shard_map/ppermute | solution.py:14
  18.9 15.6 %collective-permute-start.1 = (bf16[1064,128]{1,0:T(8,128)(2,1)}, bf16[1064,128]{1,0:T(8,128)(2,1)S(1)}, u32[]{:S(2)}, u32[]{:S(2)}) collective-permute-start(bf16[1064,128]{1,0:T(8,128)(2,1)} %param.13), channel_id=1, source_target_pairs={{8,0},{16,8},{24,16},{32,24},{40,32},{48,40},{56,48},{64,56},{72,6... | collective-permute-start | bytes 817160 | tf_op jit(solution)/shard_map/ppermute | solution.py:14
  20.8 39.9 %collective-permute-start.4 = (bf16[1064,512]{1,0:T(8,128)(2,1)}, bf16[1064,512]{1,0:T(8,128)(2,1)S(1)}, u32[]{:S(2)}, u32[]{:S(2)}) collective-permute-start(bf16[1064,512]{1,0:T(8,128)(2,1)} %param.11), channel_id=1, source_target_pairs={{0,8},{8,16},{16,24},{24,32},{32,40},{40,48},{48,56},{56,64},{64,7... | collective-permute-start | bytes 3268616 | tf_op jit(solution)/shard_map/ppermute | solution.py:14
  29.5 32.3 %collective-permute-start.5 = (bf16[1064,512]{1,0:T(8,128)(2,1)}, bf16[1064,512]{1,0:T(8,128)(2,1)}, u32[]{:S(2)}, u32[]{:S(2)}) collective-permute-start(bf16[1064,512]{1,0:T(8,128)(2,1)} %param.11), channel_id=1, source_target_pairs={{8,0},{16,8},{24,16},{32,24},{40,32},{48,40},{56,48},{64,56},{72,6... | collective-permute-start | bytes 3268616 | tf_op jit(solution)/shard_map/ppermute | solution.py:14
  38.3 31.1 %copy-start.5 = (f32[128]{0:T(128)S(1)}, f32[128]{0:T(128)}, u32[]{:S(2)}) copy-start(f32[128]{0:T(128)} %param.14) | copy-start | bytes 1540
  38.3 31.1 %copy-start.6 = (f32[128]{0:T(128)S(1)}, f32[128]{0:T(128)}, u32[]{:S(2)}) copy-start(f32[128]{0:T(128)} %param.15) | copy-start | bytes 1540
  60.7 1.0 copy-start.3
  67.1 5.6 %copy-start.1 = (pred[672,672]{0,1:T(8,128)(4,1)S(1)}, pred[672,672]{0,1:T(8,128)(4,1)}, u32[]{:S(2)}) copy-start(pred[672,672]{0,1:T(8,128)(4,1)} %compare_and_fusion) | copy-start | bytes 1354756
  72.7 4.9 %copy-start = (f32[672,672,4]{1,0,2:T(8,128)}, f32[672,672,4]{1,0,2:T(8,128)S(1)}, u32[]{:S(2)}) copy-start(f32[672,672,4]{1,0,2:T(8,128)S(1)} %get-tuple-element.33) | copy-start | bytes 21676036
  72.7 1.9 copy-start.4
  147.4 298.7 %reduce-scatter.7.cloned.1.call-start = ((), (), s32[]{:S(2)}) async-start(), calls=%async_computation.4 | async-start | bytes 8847360
  217.5 14.3 %slice-start = ((s8[8257536]{0:T(1024)(128)(4,1)}), s8[4194304]{0:T(1024)(128)(4,1)S(1)}, s32[]{:S(2)}) async-start(s8[8257536]{0:T(1024)(128)(4,1)} %bitcast.171), calls=%async_computation.6 | async-start | bytes 8388608
  226.0 5.9 %slice-start.1 = ((s8[8257536]{0:T(1024)(128)(4,1)}), s8[4063232]{0:T(1024)(128)(4,1)S(1)}, s32[]{:S(2)}) async-start(s8[8257536]{0:T(1024)(128)(4,1)} %bitcast.171), calls=%async_computation.7 | async-start | bytes 8126464
  234.8 5.3 %copy-start.2 = (bf16[672,512]{1,0:T(8,128)(2,1)S(1)}, bf16[672,512]{1,0:T(8,128)(2,1)}, u32[]{:S(2)}) copy-start(bf16[672,512]{1,0:T(8,128)(2,1)} %gather_fusion) | copy-start | bytes 2064388
Sparse Core Ops, SparseCore 0:
  10.6 119.7 all-gather.4
  132.3 66.9 all-gather.2
  201.9 121.0 reduce-scatter.8
  327.1 118.9 reduce-scatter.6
where the time goes:
time: 456 us; the launch traced here: 455 us
  waiting for transfers between devices  326 us (71%)
  matrix products  45.6 us (10%)
  local copies, waits for them, and re-layouts  35.6 us (8%)
  starting transfers between devices  17.8 us (4%)
  other arithmetic  15.4 us (3%)
  between operations  14.1 us (3%)
    unnamed x6, waiting for transfers between devices  199 us
    all_gather x1, waiting for transfers between devices, body(): full_cotan = lax.all_gather(cotangent, 'tensor', axis=1, tiled=True)  52.5 us
    all_gather x1, waiting for transfers between devices, body(): lax.all_gather(out_weight, 'dp', axis=0, tiled=True)  51.9 us
    unnamed x24, local copies, waits for them, and re-layouts  23.8 us
    ppermute x6, waiting for transfers between devices, passed_along(): lax.ppermute(value, axis, [(source, source + steps) for source in range(i...  22.4 us
    dot_general x6, matrix products, elementwise_result(): return jnp.einsum(form, left, right, preferred_element_type=jnp.float32)  19.8 us
    ppermute x6, starting transfers between devices, passed_along(): lax.ppermute(value, axis, [(source, source + steps) for source in range(i...  17.6 us
    gather x4, local copies, waits for them, and re-layouts, body(): jnp.take(jnp.concatenate([received[0][member], payload[member], received[...  9.54 us
  transfers between devices with their start and end apart: 10, of which 5 were waited for; matrix products, arithmetic and copies ran while one was open for 21% of the time, Pallas kernels for 0%

commit v1 on v0

v1 whole, which is shorter than its diff:
```python
import functools
import itertools
import math

import jax
import jax.numpy as jnp
from jax import lax
from jax.experimental import pallas as pl
from jax.experimental.pallas import tpu as pltpu
from jax.sharding import Mesh, PartitionSpec as P

EPS = 1e-06
BF = jnp.bfloat16
F32 = jnp.float32
ALL = ("z", "yl", "c", "yh", "x")
SIZES = (8, 2, 2, 2, 4)
TOK = 672
EDGE = 208
ROWS = 1064
BLK = 112
WIN = 384
NBLK = TOK // BLK
HEAD = 128
HEADS = 4
SCALE = 1.0 / math.sqrt(HEAD)
VMEM = 56 * 1024 * 1024


def params():
    return pltpu.CompilerParams(vmem_limit_bytes=VMEM)


def cost(flops, nbytes):
    return pl.CostEstimate(flops=int(flops), bytes_accessed=int(nbytes), transcendentals=0)


def window(i):
    return max(0, BLK * (i + 1) - WIN)


def dot(a, b, ca, cb):
    return lax.dot_general(a, b, (((ca,), (cb,)), ((), ())), preferred_element_type=F32)


def fwd_kernel(sc, rs, left, q, k, v, right, qg, kg, pk, p_out, o_out, com, qn, kn):
    com[0:EDGE, :] = left[...].astype(F32)
    com[EDGE : EDGE + ROWS, 0:512] = q[...].astype(F32)
    com[EDGE : EDGE + ROWS, 512:640] = k[...].astype(F32)
    com[EDGE : EDGE + ROWS, 640:768] = v[...].astype(F32)
    rest = lax.rem(sc[1], 8)
    at = pl.ds(pl.multiple_of(sc[1] - rest, 8), EDGE + 8)
    tail = jnp.concatenate([right[...].astype(F32), jnp.zeros((8, 768), F32)], axis=0)
    tail = pltpu.roll(tail, rest, 0)
    rows = lax.broadcasted_iota(jnp.int32, (EDGE + 8, 768), 0)
    com[at, :] = jnp.where(rows >= rest, tail, com[at, :])
    rest = lax.rem(sc[0], 8)
    base = pl.multiple_of(sc[0] - rest, 8)
    back = lax.rem(BLK + 8 - rest, BLK + 8)
    for i in range(NBLK):
        r = slice(BLK * i, BLK * (i + 1))
        x = com[pl.ds(base + BLK * i, BLK + 8), :]
        x = pltpu.roll(x, back, 0)[:BLK]
        pk[r, :] = x.astype(BF)
        for h in range(HEADS + 1):
            e = x[:, HEAD * h : HEAD * (h + 1)]
            ms = jnp.mean(e * e, axis=-1, keepdims=True)
            gain = qg[...] if h < HEADS else kg[...]
            n = (e * lax.rsqrt(ms + EPS) * gain).astype(BF)
            if h < HEADS:
                qn[r, HEAD * h : HEAD * (h + 1)] = n
            else:
                kn[r, :] = n
    for i in range(NBLK):
        r = slice(BLK * i, BLK * (i + 1))
        w = slice(window(i), window(i) + WIN)
        kw = kn[w, :]
        vw = pk[w, 640:768]
        qs = jnp.concatenate([qn[r, HEAD * h : HEAD * (h + 1)] for h in range(HEADS)], axis=0)
        s = dot(qs, kw, 1, 1)
        row = lax.broadcasted_iota(jnp.int32, (BLK, WIN), 0) + BLK * i
        col = lax.broadcasted_iota(jnp.int32, (BLK, WIN), 1) + window(i)
        ok = (col <= row) & (col >= rs[r, :])
        pbs = []
        for h in range(HEADS):
            sh = jnp.where(ok, s[BLK * h : BLK * (h + 1), :] * SCALE, -1e30)
            e = jnp.exp(sh - jnp.max(sh, axis=-1, keepdims=True))
            pr = e * (1.0 / jnp.sum(e, axis=-1, keepdims=True))
            p_out[i, BLK * h : BLK * (h + 1), :] = pr
            pbs.append(pr.astype(BF))
        o = dot(jnp.concatenate(pbs, axis=0), vw, 1, 0).astype(BF)
        for h in range(HEADS):
            o_out[r, HEAD * h : HEAD * (h + 1)] = o[BLK * h : BLK * (h + 1), :]


def forward(sc, rs, left, q, k, v, right, qg, kg):
    vm = pl.BlockSpec(memory_space=pltpu.VMEM)
    return pl.pallas_call(
        fwd_kernel,
        out_shape=(
            jax.ShapeDtypeStruct((TOK, 768), BF),
            jax.ShapeDtypeStruct((NBLK, HEADS * BLK, WIN), F32),
            jax.ShapeDtypeStruct((TOK, 512), BF),
        ),
        in_specs=[pl.BlockSpec(memory_space=pltpu.SMEM)] + [vm] * 8,
        out_specs=(vm, vm, vm),
        scratch_shapes=[
            pltpu.VMEM((EDGE + ROWS + EDGE + 8, 768), F32),
            pltpu.VMEM((TOK, 512), BF),
            pltpu.VMEM((TOK, HEAD), BF),
        ],
        compiler_params=params(),
        cost_estimate=cost(6e9, 9e6),
    )(sc, rs, left, q, k, v, right, qg, kg)


def norm_back(x, gain, dy):
    r = lax.rsqrt(jnp.mean(x * x, axis=-1, keepdims=True) + EPS)
    xh = x * r
    gd = gain * dy
    return r * (gd - xh * jnp.mean(xh * gd, axis=-1, keepdims=True))


def bwd_kernel(sel, gm, go, got, pk, p_in, qg, kg, dq, dk, dv, qn, kn, do, dk_acc, dv_acc):
    first = sel[0] == 1
    for i in range(NBLK):
        r = slice(BLK * i, BLK * (i + 1))
        for h in range(HEADS + 1):
            c = slice(HEAD * h, HEAD * (h + 1))
            e = pk[r, c].astype(F32)
            ms = jnp.mean(e * e, axis=-1, keepdims=True)
            gain = qg[...] if h < HEADS else kg[...]
            n = (e * lax.rsqrt(ms + EPS) * gain).astype(BF)
            if h < HEADS:
                qn[r, c] = n
                own = jnp.where(first, gm[r, c].astype(F32), go[r, c].astype(F32))
                do[r, c] = (own + got[r, c].astype(F32)).astype(BF)
            else:
                kn[r, :] = n
    dk_acc[...] = jnp.zeros_like(dk_acc)
    dv_acc[...] = jnp.zeros_like(dv_acc)
    for i in range(NBLK):
        r = slice(BLK * i, BLK * (i + 1))
        w = slice(window(i), window(i) + WIN)
        kw = kn[w, :]
        vw = pk[w, 640:768]
        qs = jnp.concatenate([qn[r, HEAD * h : HEAD * (h + 1)] for h in range(HEADS)], axis=0)
        ds_ = jnp.concatenate([do[r, HEAD * h : HEAD * (h + 1)] for h in range(HEADS)], axis=0)
        dp = dot(ds_, vw, 1, 1)
        dss, pbs = [], []
        for h in range(HEADS):
            rows = slice(BLK * h, BLK * (h + 1))
            pr = p_in[i, rows, :]
            dph = dp[rows, :]
            delta = jnp.sum(pr * dph, axis=-1, keepdims=True)
            dss.append((pr * (dph - delta) * SCALE).astype(BF))
            pbs.append(pr.astype(BF))
        dsc = jnp.concatenate(dss, axis=0)
        pb = jnp.concatenate(pbs, axis=0)
        dv_acc[w, :] += dot(pb, ds_, 0, 0)
        dk_acc[w, :] += dot(dsc, qs, 0, 0)
        dqn = dot(dsc, kw, 1, 0)
        for h in range(HEADS):
            c = slice(HEAD * h, HEAD * (h + 1))
            x = pk[r, c].astype(F32)
            dq[r, c] = norm_back(x, qg[...], dqn[BLK * h : BLK * (h + 1), :]).astype(BF)
    for i in range(NBLK):
        r = slice(BLK * i, BLK * (i + 1))
        dk[r, :] = norm_back(pk[r, 512:640].astype(F32), kg[...], dk_acc[r, :]).astype(BF)
        dv[r, :] = dv_acc[r, :].astype(BF)


def backward(sel, gm, go, got, pk, p, qg, kg):
    vm = pl.BlockSpec(memory_space=pltpu.VMEM)
    return pl.pallas_call(
        bwd_kernel,
        out_shape=(
            jax.ShapeDtypeStruct((TOK, 512), BF),
            jax.ShapeDtypeStruct((TOK, HEAD), BF),
            jax.ShapeDtypeStruct((TOK, HEAD), BF),
        ),
        in_specs=[pl.BlockSpec(memory_space=pltpu.SMEM)] + [vm] * 7,
        out_specs=(vm, vm, vm),
        scratch_shapes=[
            pltpu.VMEM((TOK, 512), BF),
            pltpu.VMEM((TOK, HEAD), BF),
            pltpu.VMEM((TOK, 512), BF),
            pltpu.VMEM((TOK, HEAD), F32),
            pltpu.VMEM((TOK, HEAD), F32),
        ],
        compiler_params=params(),
        cost_estimate=cost(6e9, 9e6),
    )(sel, gm, go, got, pk, p, qg, kg)


def halves_kernel(swap, rows, after, out0, out1):
    low, high = rows[0:160, :], rows[160:320, :]
    first = swap[0] == 0
    out0[...] = jnp.where(first, low, high)
    out1[...] = jnp.where(first, high, low)


def halves_of(swap, rows, after):
    vm = pl.BlockSpec(memory_space=pltpu.VMEM)
    out = jax.ShapeDtypeStruct((160, 512), BF)
    return pl.pallas_call(
        halves_kernel,
        out_shape=(out, out),
        in_specs=[
            pl.BlockSpec(memory_space=pltpu.SMEM),
            vm,
            pl.BlockSpec(memory_space=pl.ANY),
        ],
        out_specs=(vm, vm),
        compiler_params=params(),
        cost_estimate=cost(160 * 512, 1e6),
    )(swap, rows, after)


def product(a, b, ca, cb):
    return lax.dot_general(a, b, (((ca,), (cb,)), ((), ())), preferred_element_type=F32)


def shift(value, axis, k):
    n = lax.axis_size(axis)
    return lax.ppermute(value, axis, [(i, (i + k) % n) for i in range(n)])


def linear(z, yl, c, yh, x):
    return (((z * 2 + yl) * 2 + c) * 2 + yh) * 4 + x


def every(*sizes):
    return list(itertools.product(*(range(n) for n in sizes)))


def weight_moves(flip):
    return [
        (linear(4 * f + xh, r, s, h, x), linear(2 * (xh ^ (2 * h)) + r, s ^ flip, h, f, x))
        for f, xh, r, s, h, x in every(2, 4, 2, 2, 2, 4)
    ]


def final_moves(flip):
    return [
        (
            linear(4 * o + 2 * xl + r, s ^ flip, c, yh, x),
            linear(4 * yh + 2 * c + xl, r, s, yh ^ o, x),
        )
        for o, xl, r, s, c, yh, x in every(2, 2, 2, 2, 2, 2, 4)
    ]


def body(rollout_q, rollout_k, rollout_v, q_gain, k_gain, out_weight, cotangent, lengths, source):
    z, yl, c, yh, x = (lax.axis_index(name) for name in ALL)
    dp = (z * 2 + yl) * 2 + c
    shards = 32
    per = lengths.shape[0] // shards

    w_here, w_pair = (lax.ppermute(out_weight, ALL, weight_moves(flip)) for flip in (0, 1))
    w_both = jnp.where(
        yl == 0,
        jnp.concatenate([w_here, w_pair], axis=0),
        jnp.concatenate([w_pair, w_here], axis=0),
    )
    w_m = lax.all_gather(w_both, "z", axis=0, tiled=True)
    w_o = shift(w_m, "c", 1)

    total = jnp.sum(jnp.where(source == dp, lengths, 0))
    tail = total - EDGE
    to_right = jnp.concatenate(
        [lax.dynamic_slice_in_dim(a, tail, EDGE, 0) for a in (rollout_q, rollout_k, rollout_v)],
        axis=1,
    )
    to_left = jnp.concatenate([a[:EDGE] for a in (rollout_q, rollout_k, rollout_v)], axis=1)
    names = ("z", "yl", "c")
    left = lax.ppermute(to_right, names, [(i, i + 1) for i in range(shards - 1)])
    right = lax.ppermute(to_left, names, [(i, i - 1) for i in range(1, shards)])

    slots = [((x + k) % 4) ^ (2 * c) for k in range(4)]
    cots = jnp.zeros((TOK, 2560), BF)
    for k in (0, 1, 3, 2):
        part = shift(cotangent, "x", -k) if k else cotangent
        cots = lax.dynamic_update_slice(cots, part, (0, 640 * slots[k]))

    order = jnp.arange(lengths.shape[0], dtype=jnp.int32)
    first = dp * per
    mine_len = lax.dynamic_slice_in_dim(lengths, first, per)
    mine_src = lax.dynamic_slice_in_dim(source, first, per)
    ends = jnp.cumsum(mine_len)
    starts = ends - mine_len
    lead = jnp.sum(jnp.where(mine_src < dp, mine_len, 0))
    own_off = jnp.sum(jnp.where((source == dp) & (order < first), lengths, 0))
    row_ids = jnp.arange(TOK, dtype=jnp.int32)
    row_start = jnp.max(
        jnp.where(row_ids[:, None] >= starts[None, :], starts[None, :], 0), axis=1, keepdims=True
    )
    scalars = jnp.stack([EDGE + own_off - lead, EDGE + total]).astype(jnp.int32)
    qg = q_gain.reshape(1, HEAD)
    kg = k_gain.reshape(1, HEAD)
    packed, probs, att = forward(
        scalars, row_start, left, rollout_q, rollout_k, rollout_v, right, qg, kg
    )
    att_far = shift(att, "yh", 1)

    grad_scale = (TOK * shards) ** (-0.5)
    sums = []
    for rows in (att, att_far):
        send = (product(cots[:, 1280:], rows, 0, 0) * grad_scale).astype(BF)
        keep = (product(cots[:, :1280], rows, 0, 0) * grad_scale).astype(BF)
        got = shift(send, "c", 1)
        sums.append((keep.astype(F32) + got.astype(F32)).astype(BF))
    summed = lax.psum_scatter(
        jnp.concatenate(sums, axis=0), "z", scatter_dimension=0, tiled=True
    )

    same = yh == c
    part_m = product(cots, w_m, 1, 0).astype(BF)
    part_o = (
        product(cots[:, :1280], w_o[1280:], 1, 0) + product(cots[:, 1280:], w_o[:1280], 1, 0)
    ).astype(BF)
    got = shift(jnp.where(same, part_o, part_m), "yh", 1)
    query_grad, key_grad, value_grad = backward(
        same.astype(jnp.int32)[None], part_m, part_o, got, packed, probs, qg, kg
    )

    att_m = jnp.where(same, att, att_far)
    att_o = jnp.where(same, att_far, att)
    outs = {}
    for k in (2, 1, 3, 0):
        rows_m = lax.dynamic_slice_in_dim(w_m, 640 * slots[k], 640, 0)
        rows_o = lax.dynamic_slice_in_dim(w_o, 640 * (slots[k] ^ 2), 640, 0)
        outs[k] = (product(att_m, rows_m, 1, 1) + product(att_o, rows_o, 1, 1)).astype(BF)
    got = [shift(outs[k], "x", k).astype(F32) for k in (1, 2, 3)]
    layer_out = (outs[0].astype(F32) + got[0] + got[1] + got[2]).astype(BF)

    ready = halves_of(yl.astype(jnp.int32)[None], summed, key_grad)
    landed = [lax.ppermute(ready[flip], ALL, final_moves(flip)) for flip in (0, 1)]
    weight_grad = landed[0].astype(F32) + landed[1].astype(F32)
    return layer_out, query_grad, key_grad, value_grad, weight_grad


def solution(mesh):
    grid = Mesh(mesh.devices.reshape(SIZES), ALL)
    dp, tensor = ("z", "yl", "c"), ("yh", "x")
    two = P(dp, tensor)
    return jax.shard_map(
        body,
        mesh=grid,
        in_specs=(two, two, two, P(), P(), two, two, P(), P()),
        out_specs=(two,) * 5,
        check_vma=False,
    )
```

time: 456 us -> 174 us (0.38)
  waiting for transfers between devices: 326 us -> 32.9 us
  starting transfers between devices: 17.8 us -> 48 us
  local copies, waits for them, and re-layouts: 35.6 us -> 9.84 us
  Pallas kernels: 0 us -> 19.7 us
  matrix products: 45.6 us -> 32.6 us
    unnamed x6 -> x2, waiting for transfers between devices: 199 us -> 0.03 us
    all_gather x2 -> x1, waiting for transfers between devices: 104 us -> 0.01 us  [body(): w_m = lax.all_gather(w_both, 'z', axis=0, tiled=True)]
    ppermute x6 -> x17, starting transfers between devices: 17.6 us -> 47.9 us  [the longest x11 29.4 us: shift(): return lax.ppermute(value, axis, [(i, (i + k) % n) for i in range(n)])]
    unnamed x24 -> x20, local copies, waits for them, and re-layouts: 23.8 us -> 1.44 us
    pallas_call x0 -> x3, Pallas kernels: none -> 19.7 us  [the longest x1 9.77 us: backward(): pl.pallas_call(bwd_kernel, out_shape=(jax.ShapeDtypeStruct((TOK, 512), BF...]
    dot_general x9 -> x15, matrix products: 45.6 us -> 32.6 us  [product(): lax.dot_general(a, b, (((ca,), (cb,)), ((), ())), preferred_element_type=...]
    ppermute x6 -> x17, waiting for transfers between devices: 22.4 us -> 32.9 us  [the longest x11 22.7 us: shift(): return lax.ppermute(value, axis, [(i, (i + k) % n) for i in range(n)])]
    gather x4 -> x0, local copies, waits for them, and re-layouts: 9.54 us -> none  [body(): jnp.take(jnp.concatenate([received[0][member], payload[member], received[...]
  transfers between devices with their start and end apart: 10 -> 19, of which waited for: 5 -> 7; matrix products, arithmetic and copies ran while one was open for 21% -> 29% of each run, Pallas kernels for 0% -> 11%
where the time goes in v1:
time: 174 us; the launch traced here: 173 us
  starting transfers between devices  48 us (28%)
  waiting for transfers between devices  32.9 us (19%)
  matrix products  32.6 us (19%)
  Pallas kernels  19.7 us (11%)
  between operations  17.6 us (10%)
  other arithmetic  12.2 us (7%)
  local copies, waits for them, and re-layouts  9.84 us (6%)
    dot_general x15, matrix products, product(): lax.dot_general(a, b, (((ca,), (cb,)), ((), ())), preferred_element_type=...  32.6 us
    ppermute x11, starting transfers between devices, shift(): return lax.ppermute(value, axis, [(i, (i + k) % n) for i in range(n)])  29.4 us
    ppermute x11, waiting for transfers between devices, shift(): return lax.ppermute(value, axis, [(i, (i + k) % n) for i in range(n)])  22.7 us
    pallas_call x1, Pallas kernels, backward(): pl.pallas_call(bwd_kernel, out_shape=(jax.ShapeDtypeStruct((TOK, 512), BF...  9.77 us
    ppermute x2, waiting for transfers between devices, body(): lax.ppermute(out_weight, ALL, weight_moves(flip))  8.61 us
    ppermute x2, starting transfers between devices, body(): lax.ppermute(out_weight, ALL, weight_moves(flip))  8.42 us
    pallas_call x1, Pallas kernels, forward(): pl.pallas_call(fwd_kernel, out_shape=(jax.ShapeDtypeStruct((TOK, 768), BF...  8.21 us
    dynamic_update_slice x4, local copies, waits for them, and re-layouts, body(): cots = lax.dynamic_update_slice(cots, part, (0, 640 * slots[k]))  5.18 us
  transfers between devices with their start and end apart: 19, of which 7 were waited for; matrix products, arithmetic and copies ran while one was open for 29% of the time, Pallas kernels for 11%

profile of v1, /device:TPU:1, one launch (start us, length us, event | category | flops | bytes accessed | tf_op | source)
XLA Modules:
  0.0 173.0 jit_solution(14658175629637665490)
XLA Ops:
  7.2 5.1 %collective-permute-start.4 = (bf16[160,512]{1,0:T(8,128)(2,1)}, bf16[160,512]{1,0:T(8,128)(2,1)S(1)}, u32[]{:S(2)}, u32[]{:S(2)}) collective-permute-start(bf16[160,512]{1,0:T(8,128)(2,1)} %param.14), channel_id=1, source_target_pairs={{0,16},{1,17},{2,18},{3,19},{4,152},{5,153},{6,154},{7,155},{8,0},... | collective-permute-start | bytes 491528 | tf_op jit(solution)/shard_map/ppermute | solution.py:259
  12.4 3.3 %collective-permute-start.3 = (bf16[160,512]{1,0:T(8,128)(2,1)}, bf16[160,512]{1,0:T(8,128)(2,1)S(1)}, u32[]{:S(2)}, u32[]{:S(2)}) collective-permute-start(bf16[160,512]{1,0:T(8,128)(2,1)} %param.14), channel_id=1, source_target_pairs={{0,0},{1,1},{2,2},{3,3},{4,136},{5,137},{6,138},{7,139},{8,16},{9,... | collective-permute-start | bytes 491528 | tf_op jit(solution)/shard_map/ppermute | solution.py:259
  15.7 3.7 %collective-permute-done.4 = bf16[160,512]{1,0:T(8,128)(2,1)S(1)} collective-permute-done((bf16[160,512]{1,0:T(8,128)(2,1)}, bf16[160,512]{1,0:T(8,128)(2,1)S(1)}, u32[]{:S(2)}, u32[]{:S(2)}) %collective-permute-start.4) | collective-permute-done | bytes 163872 | tf_op jit(solution)/shard_map/ppermute | solution.py:259
  19.4 4.9 %collective-permute-done.3 = bf16[160,512]{1,0:T(8,128)(2,1)S(1)} collective-permute-done((bf16[160,512]{1,0:T(8,128)(2,1)}, bf16[160,512]{1,0:T(8,128)(2,1)S(1)}, u32[]{:S(2)}, u32[]{:S(2)}) %collective-permute-start.3) | collective-permute-done | bytes 163872 | tf_op jit(solution)/shard_map/ppermute | solution.py:259
  25.2 2.4 %collective-permute-start.9 = (bf16[672,640]{1,0:T(8,128)(2,1)}, bf16[672,640]{1,0:T(8,128)(2,1)}, u32[]{:S(2)}, u32[]{:S(2)}) collective-permute-start(bf16[672,640]{1,0:T(8,128)(2,1)} %param.15), channel_id=1, source_target_pairs={{0,3},{1,0},{2,1},{3,2},{4,7},{5,4},{6,5},{7,6},{8,11},{9,8},{10,9... | collective-permute-start | bytes 2580488 | tf_op jit(solution)/shard_map/ppermute | solution.py:225
  34.1 1.9 %collective-permute-start = (bf16[208,768]{1,0:T(8,128)(2,1)}, bf16[208,768]{1,0:T(8,128)(2,1)}, u32[]{:S(2)}, u32[]{:S(2)}) collective-permute-start(bf16[208,768]{1,0:T(8,128)(2,1)} %pad_maximum_fusion.1), channel_id=1, source_target_pairs={{0,8},{8,16},{16,24},{24,32},{32,40},{40,48},{48,56},{56,64},{64,7... | collective-permute-start | bytes 958472 | tf_op jit(solution)/shard_map/ppermute | solution.py:276
  36.8 3.1 %collective-permute-start.1 = (bf16[208,768]{1,0:T(8,128)(2,1)}, bf16[208,768]{1,0:T(8,128)(2,1)}, u32[]{:S(2)}, u32[]{:S(2)}) collective-permute-start(bf16[208,768]{1,0:T(8,128)(2,1)} %pad_maximum_fusion.2), channel_id=1, source_target_pairs={{8,0},{16,8},{24,16},{32,24},{40,32},{48,40},{56,48},{64,56},{72,6... | collective-permute-start | bytes 958472 | tf_op jit(solution)/shard_map/ppermute | solution.py:277
  46.0 8.2 %shard_map.128 = (bf16[672,768]{1,0:T(8,128)(2,1)}, f32[6,448,384]{2,1,0:T(8,128)}, bf16[672,512]{1,0:T(8,128)(2,1)}) custom-call(s32[2]{0:T(128)} %pad_add_fusion.sc, s32[672,1]{1,0:T(8,128)} %broadcast_in_dim.45.rs, bf16[208,768]{1,0:T(8,128)(2,1)} %collective-permute-done.left, bf16[1064,512]{1,0:T(8,128)(2,1)} %q.1, bf16[1064,128]{1,0:T(8,128)(2,1)} %k.1, ...), custom_call_target="tpu_custom_call" | custom-call | flops 6000000000 | bytes 9000000 | tf_op jit(solution)/shard_map/pallas_call | solution.py:97
  54.2 18.8 %collective-permute-start.2 = (bf16[672,512]{1,0:T(8,128)(2,1)}, bf16[672,512]{1,0:T(8,128)(2,1)S(1)}, u32[]{:S(2)}, u32[]{:S(2)}) collective-permute-start(bf16[672,512]{1,0:T(8,128)(2,1)} %get-tuple-element.13), channel_id=1, source_target_pairs={{0,4},{4,0},{1,5},{5,1},{2,6},{6,2},{3,7},{7,3},{8,12},{12,8},{9,1... | collective-permute-start | bytes 2064392 | tf_op jit(solution)/shard_map/ppermute | solution.py:225
  78.3 9.1 %collective-permute-done.2 = bf16[672,512]{1,0:T(8,128)(2,1)S(1)} collective-permute-done((bf16[672,512]{1,0:T(8,128)(2,1)}, bf16[672,512]{1,0:T(8,128)(2,1)S(1)}, u32[]{:S(2)}, u32[]{:S(2)}) %collective-permute-start.2) | collective-permute-done | bytes 688160 | tf_op jit(solution)/shard_map/ppermute | solution.py:225
  87.4 2.3 %fusion.9 = bf16[1280,512]{1,0:T(8,128)(2,1)} fusion(bf16[672,512]{1,0:T(8,128)(2,1)S(1)} %collective-permute-done.2, bf16[672,2560]{1,0:T(8,128)(2,1)S(1)} %constant_dynamic-update-slice_fusion), kind=kOutput, calls=%fused_computation.13 | convolution fusion | flops 882114560 | bytes 3719168 | tf_op jit(solution)/shard_map/dot_general | solution.py:220
  89.7 2.3 %fusion.3 = bf16[1280,512]{1,0:T(8,128)(2,1)} fusion(bf16[672,512]{1,0:T(8,128)(2,1)S(1)} %copy-done.4, bf16[1280,512]{1,0:T(8,128)(2,1)S(1)} %collective-permute-done.13, bf16[672,2560]{1,0:T(8,128)(2,1)S(1)} %constant_dynamic-update-slice_fusion), kind=kOutput, calls=%fused_computation.7 | convolution fusion | flops 884736000 | bytes 5029888 | tf_op jit(solution)/shard_map/dot_general | solution.py:220
  93.0 2.8 %fusion.8 = bf16[1280,512]{1,0:T(8,128)(2,1)S(1)} fusion(bf16[672,512]{1,0:T(8,128)(2,1)} %copy-done.5, bf16[1280,512]{1,0:T(8,128)(2,1)} %collective-permute-done.14, bf16[672,2560]{1,0:T(8,128)(2,1)S(1)} %constant_dynamic-update-slice_fusion), kind=kOutput, calls=%fused_computation.12 | convolution fusion | flops 884736000 | bytes 5029888 | tf_op jit(solution)/shard_map/dot_general | solution.py:220
  95.8 1.7 pad_maximum_fusion
  99.7 4.1 %convolution_convert_fusion.gm = bf16[672,512]{1,0:T(8,128)(2,1)S(1)} fusion(bf16[672,2560]{1,0:T(8,128)(2,1)} %copy-done, bf16[2560,512]{1,0:T(8,128)(2,1)S(1)} %copy-done.2), kind=kOutput, calls=%fused_computation.21 | convolution fusion | flops 1761951744 | bytes 6750208 | tf_op jit(solution)/shard_map/dot_general | solution.py:220
  103.8 2.6 %fusion.12 = f32[672,512]{1,0:T(8,128)S(1)} fusion(bf16[672,2560]{1,0:T(8,128)(2,1)S(1)} %copy-done.1, bf16[2560,512]{1,0:T(8,128)(2,1)} %collective-permute-done.5), kind=kOutput, calls=%fused_computation.24 | convolution fusion | flops 880803840 | bytes 4407296 | tf_op jit(solution)/shard_map/dot_general | solution.py:220
  106.4 3.2 %broadcast_select_fusion = (bf16[672,512]{1,0:T(8,128)(2,1)S(1)}, bf16[672,512]{1,0:T(8,128)(2,1)}) fusion(bf16[672,512]{1,0:T(8,128)(2,1)S(1)} %convolution_convert_fusion.gm, pred[]{:T(512)S(6)} %eq.19, f32[672,512]{1,0:T(8,128)S(1)} %fusion.12, bf16[2560,512]{1,0:T(8,128)(2,1)} %collective-permute-done.5, bf16[672,2560]{1,0:T(8,128)(2,1)S(1)} %copy-done.1), kind=kOutput, calls=%fused_computation.31 | convolution fusion | flops 881836032 | bytes 6471681 | tf_op jit(solution)/shard_map/dot_general | solution.py:220
  109.6 3.2 %collective-permute-start.12 = (bf16[672,512]{1,0:T(8,128)(2,1)S(1)}, bf16[672,512]{1,0:T(8,128)(2,1)S(1)}, u32[]{:S(2)}, u32[]{:S(2)}) collective-permute-start(bf16[672,512]{1,0:T(8,128)(2,1)S(1)} %get-tuple-element.33), channel_id=1, source_target_pairs={{0,4},{4,0},{1,5},{5,1},{2,6},{6,2},{3,7},{7,3},{8,12},{12,8},{9,1... | collective-permute-start | bytes 2064392 | tf_op jit(solution)/shard_map/ppermute | solution.py:225
  112.8 1.8 %fusion.19 = f32[672,640]{1,0:T(8,128)S(1)} fusion(bf16[672,512]{1,0:T(8,128)(2,1)S(1)} %get-tuple-element.24, bf16[2560,512]{1,0:T(8,128)(2,1)} %collective-permute-done.5, s32[]{:T(128)S(6)} %select_n.117), kind=kOutput, calls=%fused_computation.34 | convolution fusion | flops 440401920 | bytes 3063812 | tf_op jit(solution)/shard_map/dot_general | solution.py:220
  114.6 1.7 add_convert_fusion.1
  116.3 2.0 %collective-permute-start.8 = (bf16[672,640]{1,0:T(8,128)(2,1)}, bf16[672,640]{1,0:T(8,128)(2,1)}, u32[]{:S(2)}, u32[]{:S(2)}) collective-permute-start(bf16[672,640]{1,0:T(8,128)(2,1)} %add_convert_fusion.1), channel_id=1, source_target_pairs={{0,3},{1,0},{2,1},{3,2},{4,7},{5,4},{6,5},{7,6},{8,11},{9,8},{10,9... | collective-permute-start | bytes 2580488 | tf_op jit(solution)/shard_map/ppermute | solution.py:225
  118.3 1.8 %fusion.22 = f32[672,640]{1,0:T(8,128)S(1)} fusion(bf16[672,512]{1,0:T(8,128)(2,1)S(1)} %get-tuple-element.24, bf16[2560,512]{1,0:T(8,128)(2,1)} %collective-permute-done.5, s32[]{:T(128)S(6)} %select_n.114), kind=kOutput, calls=%fused_computation.37 | convolution fusion | flops 440401920 | bytes 3063812 | tf_op jit(solution)/shard_map/dot_general | solution.py:220
  120.2 1.7 add_convert_fusion.2
  123.0 1.8 %fusion.25 = f32[672,640]{1,0:T(8,128)S(1)} fusion(bf16[672,512]{1,0:T(8,128)(2,1)S(1)} %get-tuple-element.24, bf16[2560,512]{1,0:T(8,128)(2,1)} %collective-permute-done.5, s32[]{:T(128)S(6)} %select_n.111), kind=kOutput, calls=%fused_computation.40 | convolution fusion | flops 440401920 | bytes 3063812 | tf_op jit(solution)/shard_map/dot_general | solution.py:220
  124.9 1.7 add_convert_fusion.3
  126.6 1.8 %fusion.28 = f32[672,640]{1,0:T(8,128)S(1)} fusion(bf16[672,512]{1,0:T(8,128)(2,1)S(1)} %get-tuple-element.24, bf16[2560,512]{1,0:T(8,128)(2,1)} %collective-permute-done.5, s32[]{:T(128)S(6)} %select_n.108), kind=kOutput, calls=%fused_computation.43 | convolution fusion | flops 440401920 | bytes 3063812 | tf_op jit(solution)/shard_map/dot_general | solution.py:220
  129.4 9.8 %shard_map.129 = (bf16[672,512]{1,0:T(8,128)(2,1)}, bf16[672,128]{1,0:T(8,128)(2,1)}, bf16[672,128]{1,0:T(8,128)(2,1)}) custom-call(s32[1]{0:T(128)} %bitcast.6.sel, bf16[672,512]{1,0:T(8,128)(2,1)} %copy-done.9, bf16[672,512]{1,0:T(8,128)(2,1)} %get-tuple-element.34.go, bf16[672,512]{1,0:T(8,128)(2,1)} %copy-done.8, bf16[672,768]{1,0:T(8,128)(2,1)} %get-tuple-element.14.pk, ...), custom_call_target="tpu_custom_call" | custom-call | flops 6000000000 | bytes 9000000 | tf_op jit(solution)/shard_map/pallas_call | solution.py:174
  139.2 1.7 shard_map.130
  140.9 3.7 %collective-permute-start.15 = (bf16[160,512]{1,0:T(8,128)(2,1)}, bf16[160,512]{1,0:T(8,128)(2,1)S(1)}, u32[]{:S(2)}, u32[]{:S(2)}) collective-permute-start(bf16[160,512]{1,0:T(8,128)(2,1)} %get-tuple-element.19), channel_id=1, source_target_pairs={{0,0},{1,1},{2,2},{3,3},{4,132},{5,133},{6,134},{7,135},{8,64},{9,... | collective-permute-start | bytes 491528 | tf_op jit(solution)/shard_map/ppermute | solution.py:337
  146.0 1.8 %add_convert_fusion.4 = bf16[672,640]{1,0:T(8,128)(2,1)S(1)} fusion(f32[672,640]{1,0:T(8,128)S(1)} %fusion.28, bf16[672,512]{1,0:T(8,128)(2,1)S(1)} %get-tuple-element.23, bf16[2560,512]{1,0:T(8,128)(2,1)} %all-gather.2.cloned.1.call-done, s32[]{:T(128)S(6)} %select_n.106), kind=kOutput, calls=%fused_computation.19 | convolution fusion | flops 441262080 | bytes 3923972 | tf_op jit(solution)/shard_map/dot_general | solution.py:220
  150.1 13.0 %collective-permute-done.6 = bf16[672,640]{1,0:T(8,128)(2,1)} collective-permute-done((bf16[672,640]{1,0:T(8,128)(2,1)}, bf16[672,640]{1,0:T(8,128)(2,1)}, u32[]{:S(2)}, u32[]{:S(2)}) %collective-permute-start.6) | collective-permute-done | bytes 860192 | tf_op jit(solution)/shard_map/ppermute | solution.py:225
  163.1 3.0 %add_convert_fusion = bf16[672,640]{1,0:T(8,128)(2,1)} fusion(bf16[672,640]{1,0:T(8,128)(2,1)} %collective-permute-done.8, bf16[672,640]{1,0:T(8,128)(2,1)} %collective-permute-done.7, bf16[672,640]{1,0:T(8,128)(2,1)} %collective-permute-done.6, bf16[672,640]{1,0:T(8,128)(2,1)S(1)} %add_convert_fusion.4), kind=kLoop, calls=%fused_computation.15 | loop fusion | flops 3440640 | bytes 4300800 | tf_op jit(solution)/shard_map/convert_element_type | solution.py:334
  (67 shorter events, 25.3 us)
Async XLA Ops:
  7.2 32.8 %copy-start.6 = (s32[192]{0:T(256)S(1)}, s32[192]{0:T(256)}, u32[]{:S(2)}) copy-start(s32[192]{0:T(256)} %param.16) | copy-start | bytes 2308
  7.2 33.1 %copy-start.7 = (s32[192]{0:T(256)S(1)}, s32[192]{0:T(256)}, u32[]{:S(2)}) copy-start(s32[192]{0:T(256)} %param.17) | copy-start | bytes 2308
  7.2 84.8 %all-gather.2.cloned.1.call-start = ((), (), s32[]{:S(2)}) async-start(), calls=%async_computation.1 | async-start | bytes 2949120 | tf_op jit(solution)/shard_map/all_gather | solution.py:265
  7.2 12.2 %collective-permute-start.4 = (bf16[160,512]{1,0:T(8,128)(2,1)}, bf16[160,512]{1,0:T(8,128)(2,1)S(1)}, u32[]{:S(2)}, u32[]{:S(2)}) collective-permute-start(bf16[160,512]{1,0:T(8,128)(2,1)} %param.14), channel_id=1, source_target_pairs={{0,16},{1,17},{2,18},{3,19},{4,152},{5,153},{6,154},{7,155},{8,0},... | collective-permute-start | bytes 491528 | tf_op jit(solution)/shard_map/ppermute | solution.py:259
  12.4 11.9 %collective-permute-start.3 = (bf16[160,512]{1,0:T(8,128)(2,1)}, bf16[160,512]{1,0:T(8,128)(2,1)S(1)}, u32[]{:S(2)}, u32[]{:S(2)}) collective-permute-start(bf16[160,512]{1,0:T(8,128)(2,1)} %param.14), channel_id=1, source_target_pairs={{0,0},{1,1},{2,2},{3,3},{4,136},{5,137},{6,138},{7,139},{8,16},{9,... | collective-permute-start | bytes 491528 | tf_op jit(solution)/shard_map/ppermute | solution.py:259
  25.1 114.0 %reduce-scatter.2.cloned.1.call-start = ((), (), s32[]{:S(2)}) async-start(), calls=%async_computation.2 | async-start | bytes 2949120 | tf_op jit(solution)/shard_map/reduce_scatter | solution.py:312
  25.2 47.8 %collective-permute-start.9 = (bf16[672,640]{1,0:T(8,128)(2,1)}, bf16[672,640]{1,0:T(8,128)(2,1)}, u32[]{:S(2)}, u32[]{:S(2)}) collective-permute-start(bf16[672,640]{1,0:T(8,128)(2,1)} %param.15), channel_id=1, source_target_pairs={{0,3},{1,0},{2,1},{3,2},{4,7},{5,4},{6,5},{7,6},{8,11},{9,8},{10,9... | collective-permute-start | bytes 2580488 | tf_op jit(solution)/shard_map/ppermute | solution.py:225
  27.6 48.0 %collective-permute-start.11 = (bf16[672,640]{1,0:T(8,128)(2,1)}, bf16[672,640]{1,0:T(8,128)(2,1)}, u32[]{:S(2)}, u32[]{:S(2)}) collective-permute-start(bf16[672,640]{1,0:T(8,128)(2,1)} %param.15), channel_id=1, source_target_pairs={{0,2},{1,3},{2,0},{3,1},{4,6},{5,7},{6,4},{7,5},{8,10},{9,11},{10,... | collective-permute-start | bytes 2580488 | tf_op jit(solution)/shard_map/ppermute | solution.py:225
  28.1 46.2 %collective-permute-start.10 = (bf16[672,640]{1,0:T(8,128)(2,1)}, bf16[672,640]{1,0:T(8,128)(2,1)}, u32[]{:S(2)}, u32[]{:S(2)}) collective-permute-start(bf16[672,640]{1,0:T(8,128)(2,1)} %param.15), channel_id=1, source_target_pairs={{0,1},{1,2},{2,3},{3,0},{4,5},{5,6},{6,7},{7,4},{8,9},{9,10},{10,1... | collective-permute-start | bytes 2580488 | tf_op jit(solution)/shard_map/ppermute | solution.py:225
  34.1 11.8 %collective-permute-start = (bf16[208,768]{1,0:T(8,128)(2,1)}, bf16[208,768]{1,0:T(8,128)(2,1)}, u32[]{:S(2)}, u32[]{:S(2)}) collective-permute-start(bf16[208,768]{1,0:T(8,128)(2,1)} %pad_maximum_fusion.1), channel_id=1, source_target_pairs={{0,8},{8,16},{16,24},{24,32},{32,40},{40,48},{48,56},{56,64},{64,7... | collective-permute-start | bytes 958472 | tf_op jit(solution)/shard_map/ppermute | solution.py:276
  36.8 9.2 %collective-permute-start.1 = (bf16[208,768]{1,0:T(8,128)(2,1)}, bf16[208,768]{1,0:T(8,128)(2,1)}, u32[]{:S(2)}, u32[]{:S(2)}) collective-permute-start(bf16[208,768]{1,0:T(8,128)(2,1)} %pad_maximum_fusion.2), channel_id=1, source_target_pairs={{8,0},{16,8},{24,16},{32,24},{40,32},{48,40},{56,48},{64,56},{72,6... | collective-permute-start | bytes 958472 | tf_op jit(solution)/shard_map/ppermute | solution.py:277
  54.2 22.7 %copy-start.4 = (bf16[672,512]{1,0:T(8,128)(2,1)S(1)}, bf16[672,512]{1,0:T(8,128)(2,1)}, u32[]{:S(2)}) copy-start(bf16[672,512]{1,0:T(8,128)(2,1)} %get-tuple-element.13) | copy-start | bytes 2064388
  54.2 33.2 %collective-permute-start.2 = (bf16[672,512]{1,0:T(8,128)(2,1)}, bf16[672,512]{1,0:T(8,128)(2,1)S(1)}, u32[]{:S(2)}, u32[]{:S(2)}) collective-permute-start(bf16[672,512]{1,0:T(8,128)(2,1)} %get-tuple-element.13), channel_id=1, source_target_pairs={{0,4},{4,0},{1,5},{5,1},{2,6},{6,2},{3,7},{7,3},{8,12},{12,8},{9,1... | collective-permute-start | bytes 2064392 | tf_op jit(solution)/shard_map/ppermute | solution.py:225
  76.9 16.1 %copy-start = (bf16[672,2560]{1,0:T(8,128)(2,1)}, bf16[672,2560]{1,0:T(8,128)(2,1)S(1)}, u32[]{:S(2)}) copy-start(bf16[672,2560]{1,0:T(8,128)(2,1)S(1)} %constant_dynamic-update-slice_fusion) | copy-start | bytes 10321924
  78.2 11.5 %collective-permute-start.13 = (bf16[1280,512]{1,0:T(8,128)(2,1)S(1)}, bf16[1280,512]{1,0:T(8,128)(2,1)S(1)}, u32[]{:S(2)}, u32[]{:S(2)}) collective-permute-start(bf16[1280,512]{1,0:T(8,128)(2,1)S(1)} %fusion.4), channel_id=1, source_target_pairs={{0,8},{8,0},{1,9},{9,1},{2,10},{10,2},{3,11},{11,3},{4,12},{12,4},... | collective-permute-start | bytes 3932168 | tf_op jit(solution)/shard_map/ppermute | solution.py:225
  87.4 2.3 %copy-start.5 = (bf16[672,512]{1,0:T(8,128)(2,1)}, bf16[672,512]{1,0:T(8,128)(2,1)S(1)}, u32[]{:S(2)}) copy-start(bf16[672,512]{1,0:T(8,128)(2,1)S(1)} %collective-permute-done.2) | copy-start | bytes 2064388
  89.7 3.4 %collective-permute-start.14 = (bf16[1280,512]{1,0:T(8,128)(2,1)}, bf16[1280,512]{1,0:T(8,128)(2,1)}, u32[]{:S(2)}, u32[]{:S(2)}) collective-permute-start(bf16[1280,512]{1,0:T(8,128)(2,1)} %fusion.9), channel_id=1, source_target_pairs={{0,8},{8,0},{1,9},{9,1},{2,10},{10,2},{3,11},{11,3},{4,12},{12,4},... | collective-permute-start | bytes 3932168 | tf_op jit(solution)/shard_map/ppermute | solution.py:225
  92.0 3.8 %copy-start.3 = (bf16[1280,512]{1,0:T(8,128)(2,1)S(1)}, bf16[1280,512]{1,0:T(8,128)(2,1)}, u32[]{:S(2)}) copy-start(bf16[1280,512]{1,0:T(8,128)(2,1)} %fusion.3) | copy-start | bytes 3932164
  92.0 11.8 %collective-permute-start.5 = (bf16[2560,512]{1,0:T(8,128)(2,1)}, bf16[2560,512]{1,0:T(8,128)(2,1)}, u32[]{:S(2)}, u32[]{:S(2)}) collective-permute-start(bf16[2560,512]{1,0:T(8,128)(2,1)} %all-gather.2.cloned.1.call-done), channel_id=1, source_target_pairs={{0,8},{8,0},{1,9},{9,1},{2,10},{10,2},{3,11},{11,3},{4,12},{12,4},... | collective-permute-start | bytes 7864328 | tf_op jit(solution)/shard_map/ppermute | solution.py:225
  97.5 2.2 %copy-start.2 = (bf16[2560,512]{1,0:T(8,128)(2,1)S(1)}, bf16[2560,512]{1,0:T(8,128)(2,1)}, u32[]{:S(2)}) copy-start(bf16[2560,512]{1,0:T(8,128)(2,1)} %all-gather.2.cloned.1.call-done) | copy-start | bytes 7864324
  99.7 4.1 %copy-start.1 = (bf16[672,2560]{1,0:T(8,128)(2,1)S(1)}, bf16[672,2560]{1,0:T(8,128)(2,1)}, u32[]{:S(2)}) copy-start(bf16[672,2560]{1,0:T(8,128)(2,1)} %copy-done) | copy-start | bytes 10321924
  103.7 2.6 %copy-start.9 = (bf16[672,512]{1,0:T(8,128)(2,1)}, bf16[672,512]{1,0:T(8,128)(2,1)S(1)}, u32[]{:S(2)}) copy-start(bf16[672,512]{1,0:T(8,128)(2,1)S(1)} %convolution_convert_fusion.gm) | copy-start | bytes 2064388
  109.6 18.9 %collective-permute-start.12 = (bf16[672,512]{1,0:T(8,128)(2,1)S(1)}, bf16[672,512]{1,0:T(8,128)(2,1)S(1)}, u32[]{:S(2)}, u32[]{:S(2)}) collective-permute-start(bf16[672,512]{1,0:T(8,128)(2,1)S(1)} %get-tuple-element.33), channel_id=1, source_target_pairs={{0,4},{4,0},{1,5},{5,1},{2,6},{6,2},{3,7},{7,3},{8,12},{12,8},{9,1... | collective-permute-start | bytes 2064392 | tf_op jit(solution)/shard_map/ppermute | solution.py:225
  116.3 33.8 %collective-permute-start.8 = (bf16[672,640]{1,0:T(8,128)(2,1)}, bf16[672,640]{1,0:T(8,128)(2,1)}, u32[]{:S(2)}, u32[]{:S(2)}) collective-permute-start(bf16[672,640]{1,0:T(8,128)(2,1)} %add_convert_fusion.1), channel_id=1, source_target_pairs={{0,3},{1,0},{2,1},{3,2},{4,7},{5,4},{6,5},{7,6},{8,11},{9,8},{10,9... | collective-permute-start | bytes 2580488 | tf_op jit(solution)/shard_map/ppermute | solution.py:225
  121.8 28.3 %collective-permute-start.7 = (bf16[672,640]{1,0:T(8,128)(2,1)}, bf16[672,640]{1,0:T(8,128)(2,1)}, u32[]{:S(2)}, u32[]{:S(2)}) collective-permute-start(bf16[672,640]{1,0:T(8,128)(2,1)} %add_convert_fusion.2), channel_id=1, source_target_pairs={{0,2},{1,3},{2,0},{3,1},{4,6},{5,7},{6,4},{7,5},{8,10},{9,11},{10,... | collective-permute-start | bytes 2580488 | tf_op jit(solution)/shard_map/ppermute | solution.py:225
  126.6 36.6 %collective-permute-start.6 = (bf16[672,640]{1,0:T(8,128)(2,1)}, bf16[672,640]{1,0:T(8,128)(2,1)}, u32[]{:S(2)}, u32[]{:S(2)}) collective-permute-start(bf16[672,640]{1,0:T(8,128)(2,1)} %add_convert_fusion.3), channel_id=1, source_target_pairs={{0,1},{1,2},{2,3},{3,0},{4,5},{5,6},{6,7},{7,4},{8,9},{9,10},{10,1... | collective-permute-start | bytes 2580488 | tf_op jit(solution)/shard_map/ppermute | solution.py:225
  128.5 0.9 copy-start.8
  140.9 8.5 %collective-permute-start.15 = (bf16[160,512]{1,0:T(8,128)(2,1)}, bf16[160,512]{1,0:T(8,128)(2,1)S(1)}, u32[]{:S(2)}, u32[]{:S(2)}) collective-permute-start(bf16[160,512]{1,0:T(8,128)(2,1)} %get-tuple-element.19), channel_id=1, source_target_pairs={{0,0},{1,1},{2,2},{3,3},{4,132},{5,133},{6,134},{7,135},{8,64},{9,... | collective-permute-start | bytes 491528 | tf_op jit(solution)/shard_map/ppermute | solution.py:337
  144.6 4.8 %collective-permute-start.16 = (bf16[160,512]{1,0:T(8,128)(2,1)}, bf16[160,512]{1,0:T(8,128)(2,1)S(1)}, u32[]{:S(2)}, u32[]{:S(2)}) collective-permute-start(bf16[160,512]{1,0:T(8,128)(2,1)} %get-tuple-element.20), channel_id=1, source_target_pairs={{16,0},{17,1},{18,2},{19,3},{20,132},{21,133},{22,134},{23,135},{2... | collective-permute-start | bytes 491528 | tf_op jit(solution)/shard_map/ppermute | solution.py:337
Sparse Core Ops, SparseCore 0:
  25.3 53.4 all-gather.1
  97.7 37.5 reduce-scatter.1

commit v2 on v1

--- a/solution.py
+++ b/solution.py
@@ -109,7 +109,7 @@
             pltpu.VMEM((TOK, HEAD), BF),
         ],
         compiler_params=params(),
-        cost_estimate=cost(6e9, 9e6),
+        cost_estimate=cost(3e10, 9e6),
     )(sc, rs, left, q, k, v, right, qg, kg)
 
 
@@ -216,6 +216,39 @@
     )(swap, rows, after)
 
 
+def pair_kernel(swap, here, pair, out):
+    first = swap[0] == 0
+    out[0:160, :] = jnp.where(first, here[...], pair[...])
+    out[160:320, :] = jnp.where(first, pair[...], here[...])
+
+
+def pair_of(swap, here, pair):
+    vm = pl.BlockSpec(memory_space=pltpu.VMEM)
+    return pl.pallas_call(
+        pair_kernel,
+        out_shape=jax.ShapeDtypeStruct((320, 512), BF),
+        in_specs=[pl.BlockSpec(memory_space=pltpu.SMEM), vm, vm],
+        out_specs=vm,
+        compiler_params=params(),
+        cost_estimate=cost(1, 1),
+    )(swap, here, pair)
+
+
+def hold_kernel(*refs):
+    pass
+
+
+def hold(value, *after):
+    return pl.pallas_call(
+        hold_kernel,
+        out_shape=jax.ShapeDtypeStruct(value.shape, value.dtype),
+        in_specs=[pl.BlockSpec(memory_space=pl.ANY)] * (1 + len(after)),
+        out_specs=pl.BlockSpec(memory_space=pl.ANY),
+        input_output_aliases={0: 0},
+        cost_estimate=cost(1, 1),
+    )(value, *after)
+
+
 def product(a, b, ca, cb):
     return lax.dot_general(a, b, (((ca,), (cb,)), ((), ())), preferred_element_type=F32)
 
@@ -233,21 +266,29 @@
     return list(itertools.product(*(range(n) for n in sizes)))
 
 
-def weight_moves(flip):
+def place(xh, f):
+    high = xh // 2
+    return (2 * ((xh + high + f + 1) % 2)) + 1 - high
+
+
+def weight_moves():
     return [
-        (linear(4 * f + xh, r, s, h, x), linear(2 * (xh ^ (2 * h)) + r, s ^ flip, h, f, x))
-        for f, xh, r, s, h, x in every(2, 4, 2, 2, 2, 4)
+        (linear(4 * f + xh, r, c, h, x), linear(2 * place(xh, f) + r, c, h, f, x))
+        for f, xh, r, c, h, x in every(2, 4, 2, 2, 2, 4)
     ]
 
 
 def final_moves(flip):
-    return [
-        (
-            linear(4 * o + 2 * xl + r, s ^ flip, c, yh, x),
-            linear(4 * yh + 2 * c + xl, r, s, yh ^ o, x),
+    moves = []
+    for o, r, s, yh, x, xh in every(2, 2, 2, 2, 4, 4):
+        c, low = divmod(place(xh, yh), 2)
+        moves.append(
+            (
+                linear(4 * o + 2 * low + r, s ^ flip, c, yh, x),
+                linear(4 * yh + xh, r, s, yh ^ o, x),
+            )
         )
-        for o, xl, r, s, c, yh, x in every(2, 2, 2, 2, 2, 2, 4)
-    ]
+    return moves
 
 
 def body(rollout_q, rollout_k, rollout_v, q_gain, k_gain, out_weight, cotangent, lengths, source):
@@ -256,14 +297,10 @@
     shards = 32
     per = lengths.shape[0] // shards
 
-    w_here, w_pair = (lax.ppermute(out_weight, ALL, weight_moves(flip)) for flip in (0, 1))
-    w_both = jnp.where(
-        yl == 0,
-        jnp.concatenate([w_here, w_pair], axis=0),
-        jnp.concatenate([w_pair, w_here], axis=0),
-    )
-    w_m = lax.all_gather(w_both, "z", axis=0, tiled=True)
-    w_o = shift(w_m, "c", 1)
+    core = c.astype(jnp.int32)[None]
+    w_chip = pair_of(core, out_weight, shift(out_weight, "c", 1))
+
+    lengths, source = hold(lengths, w_chip), hold(source, w_chip)
 
     total = jnp.sum(jnp.where(source == dp, lengths, 0))
     tail = total - EDGE
@@ -272,11 +309,15 @@
         axis=1,
     )
     to_left = jnp.concatenate([a[:EDGE] for a in (rollout_q, rollout_k, rollout_v)], axis=1)
+
+    w_moved = lax.ppermute(w_chip, ALL, weight_moves())
+
     names = ("z", "yl", "c")
+    to_left = hold(to_left, w_chip)
     left = lax.ppermute(to_right, names, [(i, i + 1) for i in range(shards - 1)])
     right = lax.ppermute(to_left, names, [(i, i - 1) for i in range(1, shards)])
 
-    slots = [((x + k) % 4) ^ (2 * c) for k in range(4)]
+    slots = [place((x + k) % 4, yh) for k in range(4)]
     cots = jnp.zeros((TOK, 2560), BF)
     for k in (0, 1, 3, 2):
         part = shift(cotangent, "x", -k) if k else cotangent
@@ -302,22 +343,26 @@
     )
     att_far = shift(att, "yh", 1)
 
+    w_m = lax.all_gather(w_moved, "z", axis=0, tiled=True)
+    w_o = shift(w_m, "c", 1)
+
     grad_scale = (TOK * shards) ** (-0.5)
-    sums = []
-    for rows in (att, att_far):
-        send = (product(cots[:, 1280:], rows, 0, 0) * grad_scale).astype(BF)
-        keep = (product(cots[:, :1280], rows, 0, 0) * grad_scale).astype(BF)
-        got = shift(send, "c", 1)
-        sums.append((keep.astype(F32) + got.astype(F32)).astype(BF))
-    summed = lax.psum_scatter(
-        jnp.concatenate(sums, axis=0), "z", scatter_dimension=0, tiled=True
-    )
+    cots_send = lax.dynamic_slice_in_dim(cots, 1280 * (1 - c), 1280, 1)
+    cots_keep = lax.dynamic_slice_in_dim(cots, 1280 * c, 1280, 1)
+
+    def half(columns, rows):
+        return (product(columns, rows, 0, 0) * grad_scale).astype(BF)
+
+    both = jnp.concatenate([att, att_far], axis=1)
+    got = shift(half(cots_send, both), "c", 1)
+    keep = half(cots_keep, hold(both, w_m))
+    sums = (keep.astype(F32) + got.astype(F32)).astype(BF)
+    sums = jnp.concatenate([sums[:, :512], sums[:, 512:]], axis=0)
+    summed = lax.psum_scatter(sums, "z", scatter_dimension=0, tiled=True)
 
     same = yh == c
     part_m = product(cots, w_m, 1, 0).astype(BF)
-    part_o = (
-        product(cots[:, :1280], w_o[1280:], 1, 0) + product(cots[:, 1280:], w_o[:1280], 1, 0)
-    ).astype(BF)
+    part_o = product(cots, w_o, 1, 0).astype(BF)
     got = shift(jnp.where(same, part_o, part_m), "yh", 1)
     query_grad, key_grad, value_grad = backward(
         same.astype(jnp.int32)[None], part_m, part_o, got, packed, probs, qg, kg
@@ -328,7 +373,7 @@
     outs = {}
     for k in (2, 1, 3, 0):
         rows_m = lax.dynamic_slice_in_dim(w_m, 640 * slots[k], 640, 0)
-        rows_o = lax.dynamic_slice_in_dim(w_o, 640 * (slots[k] ^ 2), 640, 0)
+        rows_o = lax.dynamic_slice_in_dim(w_o, 640 * slots[k], 640, 0)
         outs[k] = (product(att_m, rows_m, 1, 1) + product(att_o, rows_o, 1, 1)).astype(BF)
     got = [shift(outs[k], "x", k).astype(F32) for k in (1, 2, 3)]
     layer_out = (outs[0].astype(F32) + got[0] + got[1] + got[2]).astype(BF)

time: 174 us -> 165 us (0.948)
  starting transfers between devices: 48 us -> 36.2 us
  local copies, waits for them, and re-layouts: 9.84 us -> 13.8 us
  matrix products: 32.6 us -> 30.7 us
  Pallas kernels: 19.7 us -> 21.5 us
    ppermute x11, starting transfers between devices: 29.4 us -> 17 us  [shift(): return lax.ppermute(value, axis, [(i, (i + k) % n) for i in range(n)])]
    ppermute x2 -> x1, waiting for transfers between devices: 8.61 us -> 0.01 us  [body(): w_moved = lax.ppermute(w_chip, ALL, weight_moves())]
    all_gather x1, waiting for transfers between devices: 0.01 us -> 5.11 us  [body(): w_m = lax.all_gather(w_moved, 'z', axis=0, tiled=True)]
    unnamed x20 -> x31, local copies, waits for them, and re-layouts: 1.44 us -> 5.66 us
    convert_element_type x0 -> x1, other arithmetic: none -> 2.98 us  [body(): sums = (keep.astype(F32) + got.astype(F32)).astype(BF)]
    ppermute x11, waiting for transfers between devices: 22.7 us -> 25.4 us  [shift(): return lax.ppermute(value, axis, [(i, (i + k) % n) for i in range(n)])]
    ppermute x2, starting transfers between devices: 5.09 us -> 7.22 us  [body(): lax.ppermute(ready[flip], ALL, final_moves(flip))]
    dot_general x15 -> x12, matrix products: 32.6 us -> 30.7 us  [product(): lax.dot_general(a, b, (((ca,), (cb,)), ((), ())), preferred_element_type=...]
  transfers between devices with their start and end apart: 19 -> 18, of which waited for: 7 -> 6; matrix products, arithmetic and copies ran while one was open for 29% -> 31% of each run, Pallas kernels for 11% -> 13%
where the time goes in v2:
time: 165 us; the launch traced here: 164 us
  starting transfers between devices  36.2 us (22%)
  waiting for transfers between devices  31.6 us (19%)
  matrix products  30.7 us (19%)
  Pallas kernels  21.5 us (13%)
  between operations  17.5 us (11%)
  local copies, waits for them, and re-layouts  13.8 us (8%)
  other arithmetic  13.2 us (8%)
    dot_general x12, matrix products, product(): lax.dot_general(a, b, (((ca,), (cb,)), ((), ())), preferred_element_type=...  30.7 us
    ppermute x11, waiting for transfers between devices, shift(): return lax.ppermute(value, axis, [(i, (i + k) % n) for i in range(n)])  25.4 us
    ppermute x11, starting transfers between devices, shift(): return lax.ppermute(value, axis, [(i, (i + k) % n) for i in range(n)])  17 us
    pallas_call x1, Pallas kernels, backward(): pl.pallas_call(bwd_kernel, out_shape=(jax.ShapeDtypeStruct((TOK, 512), BF...  9.79 us
    pallas_call x1, Pallas kernels, forward(): pl.pallas_call(fwd_kernel, out_shape=(jax.ShapeDtypeStruct((TOK, 768), BF...  8.13 us
    ppermute x1, starting transfers between devices, body(): w_moved = lax.ppermute(w_chip, ALL, weight_moves())  7.48 us
    ppermute x2, starting transfers between devices, body(): lax.ppermute(ready[flip], ALL, final_moves(flip))  7.22 us
    unnamed x31, local copies, waits for them, and re-layouts  5.66 us
  transfers between devices with their start and end apart: 18, of which 6 were waited for; matrix products, arithmetic and copies ran while one was open for 31% of the time, Pallas kernels for 13%

profile of v2, /device:TPU:1, one launch (start us, length us, event | category | flops | bytes accessed | tf_op | source)
XLA Modules:
  0.0 164.4 jit_solution(14913092508517700893)
XLA Ops:
  9.7 3.2 %collective-permute-start = (bf16[160,512]{1,0:T(8,128)(2,1)}, bf16[160,512]{1,0:T(8,128)(2,1)S(1)}, u32[]{:S(2)}, u32[]{:S(2)}) collective-permute-start(bf16[160,512]{1,0:T(8,128)(2,1)} %here.1), channel_id=1, source_target_pairs={{0,8},{8,0},{1,9},{9,1},{2,10},{10,2},{3,11},{11,3},{4,12},{12,4},... | collective-permute-start | bytes 491528 | tf_op jit(solution)/shard_map/ppermute | solution.py:258
  14.9 1.8 %shard_map.128.refs_1_ = bf16[320,512]{1,0:T(8,128)(2,1)} custom-call(s32[1]{0:T(128)} %bitcast.swap, bf16[160,512]{1,0:T(8,128)(2,1)} %here.1, bf16[160,512]{1,0:T(8,128)(2,1)} %copy-done.7), custom_call_target="tpu_custom_call" | custom-call | flops 1 | bytes 1 | tf_op jit(solution)/shard_map/pallas_call | solution.py:227
  16.7 7.5 %collective-permute-start.4 = (bf16[320,512]{1,0:T(8,128)(2,1)}, bf16[320,512]{1,0:T(8,128)(2,1)S(1)}, u32[]{:S(2)}, u32[]{:S(2)}) collective-permute-start(bf16[320,512]{1,0:T(8,128)(2,1)} %shard_map.128.refs_1_), channel_id=1, source_target_pairs={{0,192},{1,193},{2,194},{3,195},{4,200},{5,201},{6,202},{7,203},{8... | collective-permute-start | bytes 983048 | tf_op jit(solution)/shard_map/ppermute | solution.py:313
  30.6 1.9 %collective-permute-start.1 = (bf16[208,768]{1,0:T(8,128)(2,1)S(1)}, bf16[208,768]{1,0:T(8,128)(2,1)S(1)}, u32[]{:S(2)}, u32[]{:S(2)}) collective-permute-start(bf16[208,768]{1,0:T(8,128)(2,1)S(1)} %pad_maximum_fusion.1), channel_id=1, source_target_pairs={{0,8},{8,16},{16,24},{24,32},{32,40},{40,48},{48,56},{56,64},{64,7... | collective-permute-start | bytes 958472 | tf_op jit(solution)/shard_map/ppermute | solution.py:317
  32.6 2.4 %collective-permute-start.2 = (bf16[208,768]{1,0:T(8,128)(2,1)}, bf16[208,768]{1,0:T(8,128)(2,1)S(1)}, u32[]{:S(2)}, u32[]{:S(2)}) collective-permute-start(bf16[208,768]{1,0:T(8,128)(2,1)} %shard_map.131), channel_id=1, source_target_pairs={{8,0},{16,8},{24,16},{32,24},{40,32},{48,40},{56,48},{64,56},{72,6... | collective-permute-start | bytes 958472 | tf_op jit(solution)/shard_map/ppermute | solution.py:318
  41.8 8.1 %shard_map.132 = (bf16[672,768]{1,0:T(8,128)(2,1)}, f32[6,448,384]{2,1,0:T(8,128)}, bf16[672,512]{1,0:T(8,128)(2,1)}) custom-call(s32[2]{0:T(128)} %pad_add_fusion.sc, s32[672,1]{1,0:T(8,128)} %broadcast_in_dim.49.rs, bf16[208,768]{1,0:T(8,128)(2,1)} %copy-done.11, bf16[1064,512]{1,0:T(8,128)(2,1)} %q.1, bf16[1064,128]{1,0:T(8,128)(2,1)} %k.1, ...), custom_call_target="tpu_custom_call" | custom-call | flops 30000001024 | bytes 9000000 | tf_op jit(solution)/shard_map/pallas_call | solution.py:97
  49.9 1.9 %collective-permute-start.3 = (bf16[672,512]{1,0:T(8,128)(2,1)}, bf16[672,512]{1,0:T(8,128)(2,1)}, u32[]{:S(2)}, u32[]{:S(2)}) collective-permute-start(bf16[672,512]{1,0:T(8,128)(2,1)} %get-tuple-element.13), channel_id=1, source_target_pairs={{0,4},{4,0},{1,5},{5,1},{2,6},{6,2},{3,7},{7,3},{8,12},{12,8},{9,1... | collective-permute-start | bytes 2064392 | tf_op jit(solution)/shard_map/ppermute | solution.py:258
  54.4 7.3 %collective-permute-done.10 = bf16[672,640]{1,0:T(8,128)(2,1)} collective-permute-done((bf16[672,640]{1,0:T(8,128)(2,1)S(1)}, bf16[672,640]{1,0:T(8,128)(2,1)}, u32[]{:S(2)}, u32[]{:S(2)}) %collective-permute-start.10) | collective-permute-done | bytes 860192 | tf_op jit(solution)/shard_map/ppermute | solution.py:258
  64.3 3.8 %collective-permute-done.3 = bf16[672,512]{1,0:T(8,128)(2,1)} collective-permute-done((bf16[672,512]{1,0:T(8,128)(2,1)}, bf16[672,512]{1,0:T(8,128)(2,1)}, u32[]{:S(2)}, u32[]{:S(2)}) %collective-permute-start.3) | collective-permute-done | bytes 688160 | tf_op jit(solution)/shard_map/ppermute | solution.py:258
  69.5 3.8 %multiply_convert_fusion = bf16[1280,1024]{1,0:T(8,128)(2,1)} fusion(bf16[672,1024]{1,0:T(8,128)(2,1)S(1)} %get-tuple-element.29.refs_0_, bf16[672,2560]{1,0:T(8,128)(2,1)S(1)} %constant_dynamic-update-slice_fusion.2, s32[]{:T(128)S(6)} %select_n.141), kind=kOutput, calls=%fused_computation.1 | convolution fusion | flops 1764229120 | bytes 5718020 | tf_op jit(solution)/shard_map/dot_general | solution.py:253
  73.4 5.1 %all-gather.2.cloned.1.call-done.refs_1_ = bf16[2560,512]{1,0:T(8,128)(2,1)} async-done(((bf16[320,512]{1,0:T(8,128)(2,1)}), bf16[2560,512]{1,0:T(8,128)(2,1)}) %all-gather.2.cloned.1.call-update) | async-done | bytes 2621456 | tf_op jit(solution)/shard_map/all_gather | solution.py:346
  78.5 3.7 %collective-permute-start.5 = (bf16[2560,512]{1,0:T(8,128)(2,1)}, bf16[2560,512]{1,0:T(8,128)(2,1)}, u32[]{:S(2)}, u32[]{:S(2)}) collective-permute-start(bf16[2560,512]{1,0:T(8,128)(2,1)} %all-gather.2.cloned.1.call-done.refs_1_), channel_id=1, source_target_pairs={{0,8},{8,0},{1,9},{9,1},{2,10},{10,2},{3,11},{11,3},{4,12},{12,4},... | collective-permute-start | bytes 7864328 | tf_op jit(solution)/shard_map/ppermute | solution.py:258
  82.1 4.1 %multiply_convert_fusion.1 = bf16[1280,1024]{1,0:T(8,128)(2,1)S(1)} fusion(bf16[672,1024]{1,0:T(8,128)(2,1)} %shard_map.134, bf16[672,2560]{1,0:T(8,128)(2,1)} %copy-done.1, s32[]{:T(128)S(6)} %select_n.140), kind=kOutput, calls=%fused_computation.2 | convolution fusion | flops 1764229120 | bytes 5718020 | tf_op jit(solution)/shard_map/dot_general | solution.py:253
  86.2 3.0 %add_convert_fusion = bf16[1280,1024]{1,0:T(8,128)(2,1)S(1)} fusion(bf16[1280,1024]{1,0:T(8,128)(2,1)} %collective-permute-done.13, bf16[1280,1024]{1,0:T(8,128)(2,1)S(1)} %multiply_convert_fusion.1), kind=kLoop, calls=%fused_computation | loop fusion | flops 5242880 | bytes 7864320 | tf_op jit(solution)/shard_map/convert_element_type | solution.py:359
  89.4 1.7 %pad_maximum_fusion = bf16[2560,512]{1,0:T(8,128)(2,1)} fusion(bf16[1280,512]{1,0:T(8,128)(2,1)S(1)} %get-tuple-element.24, bf16[1280,512]{1,0:T(8,128)(2,1)S(1)} %get-tuple-element.23), kind=kLoop, calls=%fused_computation.3 | loop fusion | flops 5242880 | bytes 5242880 | tf_op jit(solution)/shard_map/concatenate | solution.py:360
  91.2 4.9 %convolution_convert_fusion.1.gm = bf16[672,512]{1,0:T(8,128)(2,1)S(1)} fusion(bf16[672,2560]{1,0:T(8,128)(2,1)} %copy-done.1, bf16[2560,512]{1,0:T(8,128)(2,1)} %all-gather.2.cloned.1.call-done.refs_1_), kind=kOutput, calls=%fused_computation.12 | convolution fusion | flops 1761951744 | bytes 6750208 | tf_op jit(solution)/shard_map/dot_general | solution.py:253
  96.1 4.8 %broadcast_select_fusion = (bf16[672,512]{1,0:T(8,128)(2,1)S(1)}, bf16[672,512]{1,0:T(8,128)(2,1)}) fusion(bf16[672,512]{1,0:T(8,128)(2,1)S(1)} %convolution_convert_fusion.1.gm, pred[]{:T(512)S(6)} %eq.20, bf16[672,2560]{1,0:T(8,128)(2,1)S(1)} %copy-done.2, bf16[2560,512]{1,0:T(8,128)(2,1)} %collective-permute-done.5), kind=kOutput, calls=%fused_computation.13 | convolution fusion | flops 1762295808 | bytes 8126465 | tf_op jit(solution)/shard_map/dot_general | solution.py:253
  100.9 2.7 %collective-permute-start.12 = (bf16[672,512]{1,0:T(8,128)(2,1)S(1)}, bf16[672,512]{1,0:T(8,128)(2,1)S(1)}, u32[]{:S(2)}, u32[]{:S(2)}) collective-permute-start(bf16[672,512]{1,0:T(8,128)(2,1)S(1)} %get-tuple-element.36), channel_id=1, source_target_pairs={{0,4},{4,0},{1,5},{5,1},{2,6},{6,2},{3,7},{7,3},{8,12},{12,8},{9,1... | collective-permute-start | bytes 2064392 | tf_op jit(solution)/shard_map/ppermute | solution.py:258
  103.5 1.8 %fusion.2 = f32[672,640]{1,0:T(8,128)S(1)} fusion(bf16[672,512]{1,0:T(8,128)(2,1)S(1)} %get-tuple-element.26, bf16[2560,512]{1,0:T(8,128)(2,1)} %collective-permute-done.5, s32[]{:T(128)S(6)} %select_n.138), kind=kOutput, calls=%fused_computation.16 | convolution fusion | flops 440401920 | bytes 3063812 | tf_op jit(solution)/shard_map/dot_general | solution.py:253
  105.3 1.7 %add_convert_fusion.2 = bf16[672,640]{1,0:T(8,128)(2,1)} fusion(f32[672,640]{1,0:T(8,128)S(1)} %fusion.2, bf16[672,512]{1,0:T(8,128)(2,1)S(1)} %get-tuple-element.25, bf16[2560,512]{1,0:T(8,128)(2,1)S(1)} %copy-done, s32[]{:T(128)S(6)} %select_n.138), kind=kOutput, calls=%fused_computation.7 | convolution fusion | flops 441262080 | bytes 3923972 | tf_op jit(solution)/shard_map/dot_general | solution.py:253
  107.0 2.4 %collective-permute-start.8 = (bf16[672,640]{1,0:T(8,128)(2,1)}, bf16[672,640]{1,0:T(8,128)(2,1)S(1)}, u32[]{:S(2)}, u32[]{:S(2)}) collective-permute-start(bf16[672,640]{1,0:T(8,128)(2,1)} %add_convert_fusion.2), channel_id=1, source_target_pairs={{0,3},{1,0},{2,1},{3,2},{4,7},{5,4},{6,5},{7,6},{8,11},{9,8},{10,9... | collective-permute-start | bytes 2580488 | tf_op jit(solution)/shard_map/ppermute | solution.py:258
  109.4 1.8 %fusion.5 = f32[672,640]{1,0:T(8,128)S(1)} fusion(bf16[672,512]{1,0:T(8,128)(2,1)S(1)} %get-tuple-element.26, bf16[2560,512]{1,0:T(8,128)(2,1)} %collective-permute-done.5, s32[]{:T(128)S(6)} %select_n.134), kind=kOutput, calls=%fused_computation.19 | convolution fusion | flops 440401920 | bytes 3063812 | tf_op jit(solution)/shard_map/dot_general | solution.py:253
  111.3 1.7 %add_convert_fusion.3 = bf16[672,640]{1,0:T(8,128)(2,1)} fusion(f32[672,640]{1,0:T(8,128)S(1)} %fusion.5, bf16[672,512]{1,0:T(8,128)(2,1)S(1)} %get-tuple-element.25, bf16[2560,512]{1,0:T(8,128)(2,1)S(1)} %copy-done, s32[]{:T(128)S(6)} %select_n.134), kind=kOutput, calls=%fused_computation.8 | convolution fusion | flops 441262080 | bytes 3923972 | tf_op jit(solution)/shard_map/dot_general | solution.py:253
  113.5 1.8 %fusion.8 = f32[672,640]{1,0:T(8,128)S(1)} fusion(bf16[672,512]{1,0:T(8,128)(2,1)S(1)} %get-tuple-element.26, bf16[2560,512]{1,0:T(8,128)(2,1)} %collective-permute-done.5, s32[]{:T(128)S(6)} %select_n.130), kind=kOutput, calls=%fused_computation.22 | convolution fusion | flops 440401920 | bytes 3063812 | tf_op jit(solution)/shard_map/dot_general | solution.py:253
  115.4 1.7 %add_convert_fusion.4 = bf16[672,640]{1,0:T(8,128)(2,1)} fusion(f32[672,640]{1,0:T(8,128)S(1)} %fusion.8, bf16[672,512]{1,0:T(8,128)(2,1)S(1)} %get-tuple-element.25, bf16[2560,512]{1,0:T(8,128)(2,1)S(1)} %copy-done, s32[]{:T(128)S(6)} %select_n.130), kind=kOutput, calls=%fused_computation.9 | convolution fusion | flops 441262080 | bytes 3923972 | tf_op jit(solution)/shard_map/dot_general | solution.py:253
  117.6 1.8 %fusion.11 = f32[672,640]{1,0:T(8,128)S(1)} fusion(bf16[672,512]{1,0:T(8,128)(2,1)S(1)} %get-tuple-element.26, bf16[2560,512]{1,0:T(8,128)(2,1)} %collective-permute-done.5, s32[]{:T(128)S(6)} %select_n.125), kind=kOutput, calls=%fused_computation.25 | convolution fusion | flops 440401920 | bytes 3063812 | tf_op jit(solution)/shard_map/dot_general | solution.py:253
  121.1 9.8 %shard_map.133 = (bf16[672,512]{1,0:T(8,128)(2,1)}, bf16[672,128]{1,0:T(8,128)(2,1)}, bf16[672,128]{1,0:T(8,128)(2,1)}) custom-call(s32[1]{0:T(128)} %bitcast.7.sel, bf16[672,512]{1,0:T(8,128)(2,1)} %copy-done.13, bf16[672,512]{1,0:T(8,128)(2,1)} %get-tuple-element.37.go, bf16[672,512]{1,0:T(8,128)(2,1)} %copy-done.10, ...), custom_call_target="tpu_custom_call" | custom-call | flops 6000000000 | bytes 9000000 | tf_op jit(solution)/shard_map/pallas_call | solution.py:174
  130.9 1.7 %shard_map.135 = (bf16[160,512]{1,0:T(8,128)(2,1)}, bf16[160,512]{1,0:T(8,128)(2,1)}) custom-call(s32[1]{0:T(128)} %bitcast.8.swap, bf16[320,512]{1,0:T(8,128)(2,1)} %reduce-scatter.2.cloned.1.call-done.rows, bf16[672,128]{1,0:T(8,128)(2,1)} %get-tuple-element.10.after), custom_call_target="tpu_custom_call" | custom-call | flops 81920 | bytes 1000000 | tf_op jit(solution)/shard_map/pallas_call | solution.py:205
  132.6 5.6 %collective-permute-start.14 = (bf16[160,512]{1,0:T(8,128)(2,1)}, bf16[160,512]{1,0:T(8,128)(2,1)S(1)}, u32[]{:S(2)}, u32[]{:S(2)}) collective-permute-start(bf16[160,512]{1,0:T(8,128)(2,1)} %get-tuple-element.19), channel_id=1, source_target_pairs={{72,0},{64,32},{0,64},{8,96},{73,1},{65,33},{1,65},{9,97},{74,2},{... | collective-permute-start | bytes 491528 | tf_op jit(solution)/shard_map/ppermute | solution.py:382
  139.9 6.4 %collective-permute-done.8 = bf16[672,640]{1,0:T(8,128)(2,1)S(1)} collective-permute-done((bf16[672,640]{1,0:T(8,128)(2,1)}, bf16[672,640]{1,0:T(8,128)(2,1)S(1)}, u32[]{:S(2)}, u32[]{:S(2)}) %collective-permute-start.8) | collective-permute-done | bytes 860192 | tf_op jit(solution)/shard_map/ppermute | solution.py:258
  146.3 8.0 %collective-permute-done.6 = bf16[672,640]{1,0:T(8,128)(2,1)} collective-permute-done((bf16[672,640]{1,0:T(8,128)(2,1)}, bf16[672,640]{1,0:T(8,128)(2,1)}, u32[]{:S(2)}, u32[]{:S(2)}) %collective-permute-start.6) | collective-permute-done | bytes 860192 | tf_op jit(solution)/shard_map/ppermute | solution.py:258
  154.3 2.5 %add_convert_fusion.1 = bf16[672,640]{1,0:T(8,128)(2,1)} fusion(bf16[672,640]{1,0:T(8,128)(2,1)S(1)} %collective-permute-done.8, bf16[672,640]{1,0:T(8,128)(2,1)S(1)} %collective-permute-done.7, bf16[672,640]{1,0:T(8,128)(2,1)} %collective-permute-done.6, bf16[672,640]{1,0:T(8,128)(2,1)S(1)} %add_convert_fusion.5), kind=kLoop, calls=%fused_computation.6 | loop fusion | flops 3440640 | bytes 4300800 | tf_op jit(solution)/shard_map/convert_element_type | solution.py:379
  (79 shorter events, 26.4 us)
Async XLA Ops:
  7.2 71.3 %all-gather.2.cloned.1.call-start = ((), (), s32[]{:S(2)}) async-start(), calls=%async_computation.1 | async-start | bytes 2949120 | tf_op jit(solution)/shard_map/all_gather | solution.py:346
  9.7 4.5 %collective-permute-start = (bf16[160,512]{1,0:T(8,128)(2,1)}, bf16[160,512]{1,0:T(8,128)(2,1)S(1)}, u32[]{:S(2)}, u32[]{:S(2)}) collective-permute-start(bf16[160,512]{1,0:T(8,128)(2,1)} %here.1), channel_id=1, source_target_pairs={{0,8},{8,0},{1,9},{9,1},{2,10},{10,2},{3,11},{11,3},{4,12},{12,4},... | collective-permute-start | bytes 491528 | tf_op jit(solution)/shard_map/ppermute | solution.py:258
  12.9 40.2 %collective-permute-start.9 = (bf16[672,640]{1,0:T(8,128)(2,1)}, bf16[672,640]{1,0:T(8,128)(2,1)}, u32[]{:S(2)}, u32[]{:S(2)}) collective-permute-start(bf16[672,640]{1,0:T(8,128)(2,1)} %param.15), channel_id=1, source_target_pairs={{0,3},{1,0},{2,1},{3,2},{4,7},{5,4},{6,5},{7,6},{8,11},{9,8},{10,9... | collective-permute-start | bytes 2580488 | tf_op jit(solution)/shard_map/ppermute | solution.py:258
  13.7 49.3 %collective-permute-start.11 = (bf16[672,640]{1,0:T(8,128)(2,1)}, bf16[672,640]{1,0:T(8,128)(2,1)}, u32[]{:S(2)}, u32[]{:S(2)}) collective-permute-start(bf16[672,640]{1,0:T(8,128)(2,1)} %param.15), channel_id=1, source_target_pairs={{0,2},{1,3},{2,0},{3,1},{4,6},{5,7},{6,4},{7,5},{8,10},{9,11},{10,... | collective-permute-start | bytes 2580488 | tf_op jit(solution)/shard_map/ppermute | solution.py:258
  14.2 0.7 copy-start.7
  14.9 24.4 %copy-start.5 = (bf16[672,640]{1,0:T(8,128)(2,1)S(1)}, bf16[672,640]{1,0:T(8,128)(2,1)}, u32[]{:S(2)}) copy-start(bf16[672,640]{1,0:T(8,128)(2,1)} %param.15) | copy-start | bytes 2580484
  16.7 22.6 %collective-permute-start.4 = (bf16[320,512]{1,0:T(8,128)(2,1)}, bf16[320,512]{1,0:T(8,128)(2,1)S(1)}, u32[]{:S(2)}, u32[]{:S(2)}) collective-permute-start(bf16[320,512]{1,0:T(8,128)(2,1)} %shard_map.128.refs_1_), channel_id=1, source_target_pairs={{0,192},{1,193},{2,194},{3,195},{4,200},{5,201},{6,202},{7,203},{8... | collective-permute-start | bytes 983048 | tf_op jit(solution)/shard_map/ppermute | solution.py:313
  24.2 10.8 %copy-start.9 = (s32[192]{0:T(256)S(1)}, s32[192]{0:T(256)}, u32[]{:S(2)}) copy-start(s32[192]{0:T(256)} %shard_map.130) | copy-start | bytes 2308
  24.2 10.8 %copy-start.8 = (s32[192]{0:T(256)S(1)}, s32[192]{0:T(256)}, u32[]{:S(2)}) copy-start(s32[192]{0:T(256)} %shard_map.129) | copy-start | bytes 2308
  30.6 9.4 %collective-permute-start.1 = (bf16[208,768]{1,0:T(8,128)(2,1)S(1)}, bf16[208,768]{1,0:T(8,128)(2,1)S(1)}, u32[]{:S(2)}, u32[]{:S(2)}) collective-permute-start(bf16[208,768]{1,0:T(8,128)(2,1)S(1)} %pad_maximum_fusion.1), channel_id=1, source_target_pairs={{0,8},{8,16},{16,24},{24,32},{32,40},{40,48},{48,56},{56,64},{64,7... | collective-permute-start | bytes 958472 | tf_op jit(solution)/shard_map/ppermute | solution.py:317
  32.6 8.5 %collective-permute-start.2 = (bf16[208,768]{1,0:T(8,128)(2,1)}, bf16[208,768]{1,0:T(8,128)(2,1)S(1)}, u32[]{:S(2)}, u32[]{:S(2)}) collective-permute-start(bf16[208,768]{1,0:T(8,128)(2,1)} %shard_map.131), channel_id=1, source_target_pairs={{8,0},{16,8},{24,16},{32,24},{40,32},{48,40},{56,48},{64,56},{72,6... | collective-permute-start | bytes 958472 | tf_op jit(solution)/shard_map/ppermute | solution.py:318
  39.3 0.7 copy-start.6
  39.3 22.4 %collective-permute-start.10 = (bf16[672,640]{1,0:T(8,128)(2,1)S(1)}, bf16[672,640]{1,0:T(8,128)(2,1)}, u32[]{:S(2)}, u32[]{:S(2)}) collective-permute-start(bf16[672,640]{1,0:T(8,128)(2,1)S(1)} %copy-done.5), channel_id=1, source_target_pairs={{0,1},{1,2},{2,3},{3,0},{4,5},{5,6},{6,7},{7,4},{8,9},{9,10},{10,1... | collective-permute-start | bytes 2580488 | tf_op jit(solution)/shard_map/ppermute | solution.py:258
  40.0 90.9 %reduce-scatter.2.cloned.1.call-start = ((), (), s32[]{:S(2)}) async-start(), calls=%async_computation.2 | async-start | bytes 2949120 | tf_op jit(solution)/shard_map/reduce_scatter | solution.py:361
  40.1 1.0 copy-start.11
  41.1 0.7 copy-start.12
  49.9 18.1 %collective-permute-start.3 = (bf16[672,512]{1,0:T(8,128)(2,1)}, bf16[672,512]{1,0:T(8,128)(2,1)}, u32[]{:S(2)}, u32[]{:S(2)}) collective-permute-start(bf16[672,512]{1,0:T(8,128)(2,1)} %get-tuple-element.13), channel_id=1, source_target_pairs={{0,4},{4,0},{1,5},{5,1},{2,6},{6,2},{3,7},{7,3},{8,12},{12,8},{9,1... | collective-permute-start | bytes 2064392 | tf_op jit(solution)/shard_map/ppermute | solution.py:258
  51.9 1.1 copy-start.4
  64.3 9.1 %copy-start.1 = (bf16[672,2560]{1,0:T(8,128)(2,1)}, bf16[672,2560]{1,0:T(8,128)(2,1)S(1)}, u32[]{:S(2)}) copy-start(bf16[672,2560]{1,0:T(8,128)(2,1)S(1)} %constant_dynamic-update-slice_fusion.2) | copy-start | bytes 10321924
  69.5 3.9 %copy-start.3 = (bf16[672,1024]{1,0:T(8,128)(2,1)}, bf16[672,1024]{1,0:T(8,128)(2,1)S(1)}, u32[]{:S(2)}) copy-start(bf16[672,1024]{1,0:T(8,128)(2,1)S(1)} %get-tuple-element.29.refs_0_) | copy-start | bytes 4128772
  73.4 12.9 %collective-permute-start.13 = (bf16[1280,1024]{1,0:T(8,128)(2,1)}, bf16[1280,1024]{1,0:T(8,128)(2,1)}, u32[]{:S(2)}, u32[]{:S(2)}) collective-permute-start(bf16[1280,1024]{1,0:T(8,128)(2,1)} %multiply_convert_fusion), channel_id=1, source_target_pairs={{0,8},{8,0},{1,9},{9,1},{2,10},{10,2},{3,11},{11,3},{4,12},{12,4},... | collective-permute-start | bytes 7864328 | tf_op jit(solution)/shard_map/ppermute | solution.py:258
  78.5 17.6 %collective-permute-start.5 = (bf16[2560,512]{1,0:T(8,128)(2,1)}, bf16[2560,512]{1,0:T(8,128)(2,1)}, u32[]{:S(2)}, u32[]{:S(2)}) collective-permute-start(bf16[2560,512]{1,0:T(8,128)(2,1)} %all-gather.2.cloned.1.call-done.refs_1_), channel_id=1, source_target_pairs={{0,8},{8,0},{1,9},{9,1},{2,10},{10,2},{3,11},{11,3},{4,12},{12,4},... | collective-permute-start | bytes 7864328 | tf_op jit(solution)/shard_map/ppermute | solution.py:258
  91.2 4.9 %copy-start.2 = (bf16[672,2560]{1,0:T(8,128)(2,1)S(1)}, bf16[672,2560]{1,0:T(8,128)(2,1)}, u32[]{:S(2)}) copy-start(bf16[672,2560]{1,0:T(8,128)(2,1)} %copy-done.1) | copy-start | bytes 10321924
  96.0 4.8 %copy-start.13 = (bf16[672,512]{1,0:T(8,128)(2,1)}, bf16[672,512]{1,0:T(8,128)(2,1)S(1)}, u32[]{:S(2)}) copy-start(bf16[672,512]{1,0:T(8,128)(2,1)S(1)} %convolution_convert_fusion.1.gm) | copy-start | bytes 2064388
  100.8 4.5 %copy-start = (bf16[2560,512]{1,0:T(8,128)(2,1)S(1)}, bf16[2560,512]{1,0:T(8,128)(2,1)}, u32[]{:S(2)}) copy-start(bf16[2560,512]{1,0:T(8,128)(2,1)} %all-gather.2.cloned.1.call-done.refs_1_) | copy-start | bytes 7864324
  100.9 19.4 %collective-permute-start.12 = (bf16[672,512]{1,0:T(8,128)(2,1)S(1)}, bf16[672,512]{1,0:T(8,128)(2,1)S(1)}, u32[]{:S(2)}, u32[]{:S(2)}) collective-permute-start(bf16[672,512]{1,0:T(8,128)(2,1)S(1)} %get-tuple-element.36), channel_id=1, source_target_pairs={{0,4},{4,0},{1,5},{5,1},{2,6},{6,2},{3,7},{7,3},{8,12},{12,8},{9,1... | collective-permute-start | bytes 2064392 | tf_op jit(solution)/shard_map/ppermute | solution.py:258
  107.0 39.3 %collective-permute-start.8 = (bf16[672,640]{1,0:T(8,128)(2,1)}, bf16[672,640]{1,0:T(8,128)(2,1)S(1)}, u32[]{:S(2)}, u32[]{:S(2)}) collective-permute-start(bf16[672,640]{1,0:T(8,128)(2,1)} %add_convert_fusion.2), channel_id=1, source_target_pairs={{0,3},{1,0},{2,1},{3,2},{4,7},{5,4},{6,5},{7,6},{8,11},{9,8},{10,9... | collective-permute-start | bytes 2580488 | tf_op jit(solution)/shard_map/ppermute | solution.py:258
  113.0 33.3 %collective-permute-start.7 = (bf16[672,640]{1,0:T(8,128)(2,1)}, bf16[672,640]{1,0:T(8,128)(2,1)S(1)}, u32[]{:S(2)}, u32[]{:S(2)}) collective-permute-start(bf16[672,640]{1,0:T(8,128)(2,1)} %add_convert_fusion.3), channel_id=1, source_target_pairs={{0,2},{1,3},{2,0},{3,1},{4,6},{5,7},{6,4},{7,5},{8,10},{9,11},{10,... | collective-permute-start | bytes 2580488 | tf_op jit(solution)/shard_map/ppermute | solution.py:258
  117.1 37.2 %collective-permute-start.6 = (bf16[672,640]{1,0:T(8,128)(2,1)}, bf16[672,640]{1,0:T(8,128)(2,1)}, u32[]{:S(2)}, u32[]{:S(2)}) collective-permute-start(bf16[672,640]{1,0:T(8,128)(2,1)} %add_convert_fusion.4), channel_id=1, source_target_pairs={{0,1},{1,2},{2,3},{3,0},{4,5},{5,6},{6,7},{7,4},{8,9},{9,10},{10,1... | collective-permute-start | bytes 2580488 | tf_op jit(solution)/shard_map/ppermute | solution.py:258
  120.2 0.9 copy-start.10
  132.6 24.1 %collective-permute-start.14 = (bf16[160,512]{1,0:T(8,128)(2,1)}, bf16[160,512]{1,0:T(8,128)(2,1)S(1)}, u32[]{:S(2)}, u32[]{:S(2)}) collective-permute-start(bf16[160,512]{1,0:T(8,128)(2,1)} %get-tuple-element.19), channel_id=1, source_target_pairs={{72,0},{64,32},{0,64},{8,96},{73,1},{65,33},{1,65},{9,97},{74,2},{... | collective-permute-start | bytes 491528 | tf_op jit(solution)/shard_map/ppermute | solution.py:382
  138.2 18.6 %collective-permute-start.15 = (bf16[160,512]{1,0:T(8,128)(2,1)}, bf16[160,512]{1,0:T(8,128)(2,1)S(1)}, u32[]{:S(2)}, u32[]{:S(2)}) collective-permute-start(bf16[160,512]{1,0:T(8,128)(2,1)} %get-tuple-element.20), channel_id=1, source_target_pairs={{88,0},{80,32},{16,64},{24,96},{89,1},{81,33},{17,65},{25,97},{90,... | collective-permute-start | bytes 491528 | tf_op jit(solution)/shard_map/ppermute | solution.py:382
Sparse Core Ops, SparseCore 0:
  40.2 38.2 all-gather.1
  91.3 38.4 reduce-scatter.1

commit v3 on v2

--- a/solution.py
+++ b/solution.py
@@ -20,6 +20,7 @@
 BLK = 112
 WIN = 384
 NBLK = TOK // BLK
+SEQS = 6
 HEAD = 128
 HEADS = 4
 SCALE = 1.0 / math.sqrt(HEAD)
@@ -42,7 +43,56 @@
     return lax.dot_general(a, b, (((ca,), (cb,)), ((), ())), preferred_element_type=F32)
 
 
-def fwd_kernel(sc, rs, left, q, k, v, right, qg, kg, pk, p_out, o_out, com, qn, kn):
+def edge_kernel(place, lengths, source, q, k, v, after, to_right, to_left, sc, wide):
+    me = place[0]
+    first = SEQS * me
+    count = lengths.shape[0]
+
+    def held(i):
+        j = jnp.clip(i, 0, count - 1)
+        return jnp.where((i == j) & (source[j] == me), lengths[j], 0)
+
+    before = held(first - 1)
+    total = before
+    for t in range(SEQS + 1):
+        total = total + held(first + t)
+    lead = jnp.where(source[first] < me, lengths[first], 0)
+    sc[0] = EDGE + before - lead
+    sc[1] = EDGE + total
+    begin = jnp.int32(0)
+    for t in range(SEQS):
+        sc[2 + t] = begin
+        begin = begin + lengths[first + t]
+
+    wide[0:ROWS, 0:512] = q[...].astype(F32)
+    wide[0:ROWS, 512:640] = k[...].astype(F32)
+    wide[0:ROWS, 640:768] = v[...].astype(F32)
+    tail = jnp.clip(total - EDGE, 0, ROWS - EDGE)
+    rest = lax.rem(tail, 8)
+    rows = wide[pl.ds(pl.multiple_of(tail - rest, 8), EDGE + 8), :]
+    rows = pltpu.roll(rows, lax.rem(EDGE + 8 - rest, EDGE + 8), 0)
+    to_right[...] = rows[:EDGE].astype(BF)
+    to_left[:, 0:512] = q[0:EDGE, :]
+    to_left[:, 512:640] = k[0:EDGE, :]
+    to_left[:, 640:768] = v[0:EDGE, :]
+
+
+def edges(place, lengths, source, q, k, v, after):
+    vm = pl.BlockSpec(memory_space=pltpu.VMEM)
+    sm = pl.BlockSpec(memory_space=pltpu.SMEM)
+    out = jax.ShapeDtypeStruct((EDGE, 768), BF)
+    return pl.pallas_call(
+        edge_kernel,
+        out_shape=(out, out, jax.ShapeDtypeStruct((2 + SEQS,), jnp.int32)),
+        in_specs=[sm, sm, sm, vm, vm, vm, pl.BlockSpec(memory_space=pl.ANY)],
+        out_specs=(vm, vm, sm),
+        scratch_shapes=[pltpu.VMEM((ROWS + 8, 768), F32)],
+        compiler_params=params(),
+        cost_estimate=cost(1, 1),
+    )(place, lengths, source, q, k, v, after)
+
+
+def fwd_kernel(sc, left, q, k, v, right, qg, kg, pk, p_out, o_out, com, qn, kn, p_buf, sems):
     com[0:EDGE, :] = left[...].astype(F32)
     com[EDGE : EDGE + ROWS, 0:512] = q[...].astype(F32)
     com[EDGE : EDGE + ROWS, 512:640] = k[...].astype(F32)
@@ -79,20 +129,27 @@
         s = dot(qs, kw, 1, 1)
         row = lax.broadcasted_iota(jnp.int32, (BLK, WIN), 0) + BLK * i
         col = lax.broadcasted_iota(jnp.int32, (BLK, WIN), 1) + window(i)
-        ok = (col <= row) & (col >= rs[r, :])
+        line = lax.broadcasted_iota(jnp.int32, (BLK, 1), 0) + BLK * i
+        begin = jnp.zeros((BLK, 1), jnp.int32)
+        for j in range(1, SEQS):
+            begin = jnp.where(line >= sc[2 + j], sc[2 + j], begin)
+        ok = (col <= row) & (col >= begin)
         pbs = []
         for h in range(HEADS):
             sh = jnp.where(ok, s[BLK * h : BLK * (h + 1), :] * SCALE, -1e30)
             e = jnp.exp(sh - jnp.max(sh, axis=-1, keepdims=True))
             pr = e * (1.0 / jnp.sum(e, axis=-1, keepdims=True))
-            p_out[i, BLK * h : BLK * (h + 1), :] = pr
+            p_buf[i, BLK * h : BLK * (h + 1), :] = pr
             pbs.append(pr.astype(BF))
+        pltpu.make_async_copy(p_buf.at[i], p_out.at[i], sems.at[i]).start()
         o = dot(jnp.concatenate(pbs, axis=0), vw, 1, 0).astype(BF)
         for h in range(HEADS):
             o_out[r, HEAD * h : HEAD * (h + 1)] = o[BLK * h : BLK * (h + 1), :]
-
-
-def forward(sc, rs, left, q, k, v, right, qg, kg):
+    for i in range(NBLK):
+        pltpu.make_async_copy(p_buf.at[i], p_out.at[i], sems.at[i]).wait()
+
+
+def forward(sc, left, q, k, v, right, qg, kg):
     vm = pl.BlockSpec(memory_space=pltpu.VMEM)
     return pl.pallas_call(
         fwd_kernel,
@@ -101,16 +158,18 @@
             jax.ShapeDtypeStruct((NBLK, HEADS * BLK, WIN), F32),
             jax.ShapeDtypeStruct((TOK, 512), BF),
         ),
-        in_specs=[pl.BlockSpec(memory_space=pltpu.SMEM)] + [vm] * 8,
-        out_specs=(vm, vm, vm),
+        in_specs=[pl.BlockSpec(memory_space=pltpu.SMEM)] + [vm] * 7,
+        out_specs=(vm, pl.BlockSpec(memory_space=pl.ANY), vm),
         scratch_shapes=[
             pltpu.VMEM((EDGE + ROWS + EDGE + 8, 768), F32),
             pltpu.VMEM((TOK, 512), BF),
             pltpu.VMEM((TOK, HEAD), BF),
+            pltpu.VMEM((NBLK, HEADS * BLK, WIN), F32),
+            pltpu.SemaphoreType.DMA((NBLK,)),
         ],
         compiler_params=params(),
         cost_estimate=cost(3e10, 9e6),
-    )(sc, rs, left, q, k, v, right, qg, kg)
+    )(sc, left, q, k, v, right, qg, kg)
 
 
 def norm_back(x, gain, dy):
@@ -120,7 +179,11 @@
     return r * (gd - xh * jnp.mean(xh * gd, axis=-1, keepdims=True))
 
 
-def bwd_kernel(sel, gm, go, got, pk, p_in, qg, kg, dq, dk, dv, qn, kn, do, dk_acc, dv_acc):
+def bwd_kernel(
+    sel, gm, go, got, pk, p_in, qg, kg, dq, dk, dv, qn, kn, do, dk_acc, dv_acc, p_buf, sems
+):
+    for i in range(NBLK):
+        pltpu.make_async_copy(p_in.at[i], p_buf.at[i], sems.at[i]).start()
     first = sel[0] == 1
     for i in range(NBLK):
         r = slice(BLK * i, BLK * (i + 1))
@@ -146,10 +209,11 @@
         qs = jnp.concatenate([qn[r, HEAD * h : HEAD * (h + 1)] for h in range(HEADS)], axis=0)
         ds_ = jnp.concatenate([do[r, HEAD * h : HEAD * (h + 1)] for h in range(HEADS)], axis=0)
         dp = dot(ds_, vw, 1, 1)
+        pltpu.make_async_copy(p_in.at[i], p_buf.at[i], sems.at[i]).wait()
         dss, pbs = [], []
         for h in range(HEADS):
             rows = slice(BLK * h, BLK * (h + 1))
-            pr = p_in[i, rows, :]
+            pr = p_buf[i, rows, :]
             dph = dp[rows, :]
             delta = jnp.sum(pr * dph, axis=-1, keepdims=True)
             dss.append((pr * (dph - delta) * SCALE).astype(BF))
@@ -178,7 +242,9 @@
             jax.ShapeDtypeStruct((TOK, HEAD), BF),
             jax.ShapeDtypeStruct((TOK, HEAD), BF),
         ),
-        in_specs=[pl.BlockSpec(memory_space=pltpu.SMEM)] + [vm] * 7,
+        in_specs=[pl.BlockSpec(memory_space=pltpu.SMEM)]
+        + [vm] * 4
+        + [pl.BlockSpec(memory_space=pl.ANY), vm, vm],
         out_specs=(vm, vm, vm),
         scratch_shapes=[
             pltpu.VMEM((TOK, 512), BF),
@@ -186,6 +252,8 @@
             pltpu.VMEM((TOK, 512), BF),
             pltpu.VMEM((TOK, HEAD), F32),
             pltpu.VMEM((TOK, HEAD), F32),
+            pltpu.VMEM((NBLK, HEADS * BLK, WIN), F32),
+            pltpu.SemaphoreType.DMA((NBLK,)),
         ],
         compiler_params=params(),
         cost_estimate=cost(6e9, 9e6),
@@ -295,51 +363,33 @@
     z, yl, c, yh, x = (lax.axis_index(name) for name in ALL)
     dp = (z * 2 + yl) * 2 + c
     shards = 32
-    per = lengths.shape[0] // shards
 
     core = c.astype(jnp.int32)[None]
     w_chip = pair_of(core, out_weight, shift(out_weight, "c", 1))
 
-    lengths, source = hold(lengths, w_chip), hold(source, w_chip)
-
-    total = jnp.sum(jnp.where(source == dp, lengths, 0))
-    tail = total - EDGE
-    to_right = jnp.concatenate(
-        [lax.dynamic_slice_in_dim(a, tail, EDGE, 0) for a in (rollout_q, rollout_k, rollout_v)],
-        axis=1,
+    w_moved = lax.ppermute(w_chip, ALL, weight_moves())
+
+    names = ("z", "yl", "c")
+    to_right, to_left, scalars = edges(
+        dp.astype(jnp.int32)[None], lengths, source, rollout_q, rollout_k, rollout_v, w_chip
     )
-    to_left = jnp.concatenate([a[:EDGE] for a in (rollout_q, rollout_k, rollout_v)], axis=1)
-
-    w_moved = lax.ppermute(w_chip, ALL, weight_moves())
-
-    names = ("z", "yl", "c")
-    to_left = hold(to_left, w_chip)
     left = lax.ppermute(to_right, names, [(i, i + 1) for i in range(shards - 1)])
     right = lax.ppermute(to_left, names, [(i, i - 1) for i in range(1, shards)])
 
     slots = [place((x + k) % 4, yh) for k in range(4)]
+    mid = TOK // 2
+    after, before = shift(cotangent, "x", -1), shift(cotangent, "x", 1)
+    across = (shift(after[:mid], "x", -1), shift(before[mid:], "x", 1))
     cots = jnp.zeros((TOK, 2560), BF)
-    for k in (0, 1, 3, 2):
-        part = shift(cotangent, "x", -k) if k else cotangent
+    for k, part in ((0, cotangent), (1, after), (3, before)):
         cots = lax.dynamic_update_slice(cots, part, (0, 640 * slots[k]))
-
-    order = jnp.arange(lengths.shape[0], dtype=jnp.int32)
-    first = dp * per
-    mine_len = lax.dynamic_slice_in_dim(lengths, first, per)
-    mine_src = lax.dynamic_slice_in_dim(source, first, per)
-    ends = jnp.cumsum(mine_len)
-    starts = ends - mine_len
-    lead = jnp.sum(jnp.where(mine_src < dp, mine_len, 0))
-    own_off = jnp.sum(jnp.where((source == dp) & (order < first), lengths, 0))
-    row_ids = jnp.arange(TOK, dtype=jnp.int32)
-    row_start = jnp.max(
-        jnp.where(row_ids[:, None] >= starts[None, :], starts[None, :], 0), axis=1, keepdims=True
-    )
-    scalars = jnp.stack([EDGE + own_off - lead, EDGE + total]).astype(jnp.int32)
+    for row, part in zip((0, mid), across):
+        cots = lax.dynamic_update_slice(cots, part, (row, 640 * slots[2]))
+
     qg = q_gain.reshape(1, HEAD)
     kg = k_gain.reshape(1, HEAD)
     packed, probs, att = forward(
-        scalars, row_start, left, rollout_q, rollout_k, rollout_v, right, qg, kg
+        scalars, left, rollout_q, rollout_k, rollout_v, right, qg, kg
     )
     att_far = shift(att, "yh", 1)
 
@@ -355,30 +405,36 @@
 
     both = jnp.concatenate([att, att_far], axis=1)
     got = shift(half(cots_send, both), "c", 1)
-    keep = half(cots_keep, hold(both, w_m))
-    sums = (keep.astype(F32) + got.astype(F32)).astype(BF)
+    keep = half(cots_keep, both)
+    sums = (keep.astype(F32) + hold(got, w_m).astype(F32)).astype(BF)
     sums = jnp.concatenate([sums[:, :512], sums[:, 512:]], axis=0)
     summed = lax.psum_scatter(sums, "z", scatter_dimension=0, tiled=True)
 
     same = yh == c
     part_m = product(cots, w_m, 1, 0).astype(BF)
     part_o = product(cots, w_o, 1, 0).astype(BF)
-    got = shift(jnp.where(same, part_o, part_m), "yh", 1)
-    query_grad, key_grad, value_grad = backward(
-        same.astype(jnp.int32)[None], part_m, part_o, got, packed, probs, qg, kg
-    )
-
+    got_yh = shift(jnp.where(same, part_o, part_m), "yh", 1)
     att_m = jnp.where(same, att, att_far)
     att_o = jnp.where(same, att_far, att)
-    outs = {}
-    for k in (2, 1, 3, 0):
+
+    def layer(k):
         rows_m = lax.dynamic_slice_in_dim(w_m, 640 * slots[k], 640, 0)
         rows_o = lax.dynamic_slice_in_dim(w_o, 640 * slots[k], 640, 0)
-        outs[k] = (product(att_m, rows_m, 1, 1) + product(att_o, rows_o, 1, 1)).astype(BF)
-    got = [shift(outs[k], "x", k).astype(F32) for k in (1, 2, 3)]
-    layer_out = (outs[0].astype(F32) + got[0] + got[1] + got[2]).astype(BF)
-
-    ready = halves_of(yl.astype(jnp.int32)[None], summed, key_grad)
+        return product(att_m, rows_m, 1, 1) + product(att_o, rows_o, 1, 1)
+
+    opposite = layer(2).astype(BF)
+    up = shift(opposite[:mid], "x", 1).astype(F32)
+    down = shift(opposite[mid:], "x", -1).astype(F32)
+    up = (layer(1) + jnp.pad(up, ((0, mid), (0, 0)))).astype(BF)
+    down = (layer(3) + jnp.pad(down, ((mid, 0), (0, 0)))).astype(BF)
+    last = down
+    got = [shift(up, "x", 1).astype(F32), shift(down, "x", -1).astype(F32)]
+    layer_out = (layer(0) + got[0] + got[1]).astype(BF)
+
+    ready = halves_of(yl.astype(jnp.int32)[None], summed, last)
+    query_grad, key_grad, value_grad = backward(
+        same.astype(jnp.int32)[None], part_m, part_o, got_yh, packed, probs, qg, kg
+    )
     landed = [lax.ppermute(ready[flip], ALL, final_moves(flip)) for flip in (0, 1)]
     weight_grad = landed[0].astype(F32) + landed[1].astype(F32)
     return layer_out, query_grad, key_grad, value_grad, weight_grad

time: 165 us -> 157 us (0.952)
  local copies, waits for them, and re-layouts: 13.8 us -> 6.28 us
  waiting for transfers between devices: 31.6 us -> 36.6 us
  between operations: 17.5 us -> 14.3 us
  starting transfers between devices: 36.2 us -> 33.3 us
  other arithmetic: 13.2 us -> 10.8 us
    ppermute x2, waiting for transfers between devices: 0.01 us -> 10.6 us  [body(): lax.ppermute(ready[flip], ALL, final_moves(flip))]
    all_gather x1, waiting for transfers between devices: 5.11 us -> 0.01 us  [body(): w_m = lax.all_gather(w_moved, 'z', axis=0, tiled=True)]
    pallas_call x0 -> x1, Pallas kernels: none -> 2.64 us  [edges(): pl.pallas_call(edge_kernel, out_shape=(out, out, jax.ShapeDtypeStruct((2...]
    dynamic_update_slice x4 -> x3, local copies, waits for them, and re-layouts: 4.04 us -> 1.56 us  [body(): cots = lax.dynamic_update_slice(cots, part, (0, 640 * slots[k]))]
    ppermute x11 -> x13, waiting for transfers between devices: 25.4 us -> 23 us  [shift(): return lax.ppermute(value, axis, [(i, (i + k) % n) for i in range(n)])]
    ppermute x1, waiting for transfers between devices: 0.01 us -> 2.37 us  [body(): lax.ppermute(to_right, names, [(i, i + 1) for i in range(shards - 1)])]
    ppermute x2, starting transfers between devices: 7.22 us -> 5.15 us  [body(): lax.ppermute(ready[flip], ALL, final_moves(flip))]
    ppermute x1, starting transfers between devices: 7.48 us -> 5.55 us  [body(): w_moved = lax.ppermute(w_chip, ALL, weight_moves())]
  transfers between devices with their start and end apart: 18 -> 20, of which waited for: 6 -> 10; matrix products, arithmetic and copies ran while one was open for 31% -> 29% of each run, Pallas kernels for 13% -> 13%
where the time goes in v3:
time: 157 us; the launch traced here: 156 us
  waiting for transfers between devices  36.6 us (23%)
  starting transfers between devices  33.3 us (21%)
  matrix products  32.2 us (21%)
  Pallas kernels  22.4 us (14%)
  between operations  14.3 us (9%)
  other arithmetic  10.8 us (7%)
  local copies, waits for them, and re-layouts  6.28 us (4%)
    dot_general x12, matrix products, product(): lax.dot_general(a, b, (((ca,), (cb,)), ((), ())), preferred_element_type=...  32.2 us
    ppermute x13, waiting for transfers between devices, shift(): return lax.ppermute(value, axis, [(i, (i + k) % n) for i in range(n)])  23 us
    ppermute x13, starting transfers between devices, shift(): return lax.ppermute(value, axis, [(i, (i + k) % n) for i in range(n)])  18.2 us
    ppermute x2, waiting for transfers between devices, body(): lax.ppermute(ready[flip], ALL, final_moves(flip))  10.6 us
    pallas_call x1, Pallas kernels, backward(): pl.pallas_call(bwd_kernel, out_shape=(jax.ShapeDtypeStruct((TOK, 512), BF...  8.43 us
    pallas_call x1, Pallas kernels, forward(): pl.pallas_call(fwd_kernel, out_shape=(jax.ShapeDtypeStruct((TOK, 768), BF...  7.89 us
    ppermute x1, starting transfers between devices, body(): w_moved = lax.ppermute(w_chip, ALL, weight_moves())  5.55 us
    ppermute x2, starting transfers between devices, body(): lax.ppermute(ready[flip], ALL, final_moves(flip))  5.15 us
  transfers between devices with their start and end apart: 20, of which 10 were waited for; matrix products, arithmetic and copies ran while one was open for 29% of the time, Pallas kernels for 13%

profile of v3, /device:TPU:1, one launch (start us, length us, event | category | flops | bytes accessed | tf_op | source)
XLA Modules:
  0.0 155.9 jit_solution(4889519970040368481)
XLA Ops:
  7.2 3.3 %collective-permute-start = (bf16[160,512]{1,0:T(8,128)(2,1)}, bf16[160,512]{1,0:T(8,128)(2,1)S(1)}, u32[]{:S(2)}, u32[]{:S(2)}) collective-permute-start(bf16[160,512]{1,0:T(8,128)(2,1)} %here.1), channel_id=1, source_target_pairs={{0,8},{8,0},{1,9},{9,1},{2,10},{10,2},{3,11},{11,3},{4,12},{12,4},... | collective-permute-start | bytes 491528 | tf_op jit(solution)/shard_map/ppermute | solution.py:326
  12.4 1.7 %shard_map.128.after = bf16[320,512]{1,0:T(8,128)(2,1)} custom-call(s32[1]{0:T(128)} %bitcast.1.swap, bf16[160,512]{1,0:T(8,128)(2,1)} %here.1, bf16[160,512]{1,0:T(8,128)(2,1)} %copy-done.6), custom_call_target="tpu_custom_call" | custom-call | flops 1 | bytes 1 | tf_op jit(solution)/shard_map/pallas_call | solution.py:295
  14.2 5.5 %collective-permute-start.4 = (bf16[320,512]{1,0:T(8,128)(2,1)}, bf16[320,512]{1,0:T(8,128)(2,1)S(1)}, u32[]{:S(2)}, u32[]{:S(2)}) collective-permute-start(bf16[320,512]{1,0:T(8,128)(2,1)} %shard_map.128.after), channel_id=1, source_target_pairs={{0,192},{1,193},{2,194},{3,195},{4,200},{5,201},{6,202},{7,203},{8... | collective-permute-start | bytes 983048 | tf_op jit(solution)/shard_map/ppermute | solution.py:370
  19.7 2.6 %shard_map.129 = (bf16[208,768]{1,0:T(8,128)(2,1)}, bf16[208,768]{1,0:T(8,128)(2,1)}, s32[8]{0:T(128)}) custom-call(s32[1]{0:T(128)} %bitcast.place, s32[192]{0:T(256)} %lengths.1, s32[192]{0:T(256)} %source.1, bf16[1064,512]{1,0:T(8,128)(2,1)} %q.3, bf16[1064,128]{1,0:T(8,128)(2,1)} %k.3, bf16[1064,128]{1,0:T(8,128)(2,1)} %v.3, ...), custom_call_target="tpu_custom_call" | custom-call | flops 1 | bytes 1 | tf_op jit(solution)/shard_map/pallas_call | solution.py:84
  22.4 1.9 %collective-permute-start.1 = (bf16[208,768]{1,0:T(8,128)(2,1)}, bf16[208,768]{1,0:T(8,128)(2,1)S(1)}, u32[]{:S(2)}, u32[]{:S(2)}) collective-permute-start(bf16[208,768]{1,0:T(8,128)(2,1)} %get-tuple-element.17), channel_id=1, source_target_pairs={{0,8},{8,16},{16,24},{24,32},{32,40},{40,48},{48,56},{56,64},{64,7... | collective-permute-start | bytes 958472 | tf_op jit(solution)/shard_map/ppermute | solution.py:376
  24.3 2.4 %collective-permute-start.2 = (bf16[208,768]{1,0:T(8,128)(2,1)}, bf16[208,768]{1,0:T(8,128)(2,1)S(1)}, u32[]{:S(2)}, u32[]{:S(2)}) collective-permute-start(bf16[208,768]{1,0:T(8,128)(2,1)} %get-tuple-element.18), channel_id=1, source_target_pairs={{8,0},{16,8},{24,16},{32,24},{40,32},{48,40},{56,48},{64,56},{72,6... | collective-permute-start | bytes 958472 | tf_op jit(solution)/shard_map/ppermute | solution.py:377
  26.7 2.6 %collective-permute-start.10 = (bf16[672,640]{1,0:T(8,128)(2,1)}, bf16[672,640]{1,0:T(8,128)(2,1)S(1)}, u32[]{:S(2)}, u32[]{:S(2)}) collective-permute-start(bf16[672,640]{1,0:T(8,128)(2,1)} %param.15), channel_id=1, source_target_pairs={{0,3},{1,0},{2,1},{3,2},{4,7},{5,4},{6,5},{7,6},{8,11},{9,8},{10,9... | collective-permute-start | bytes 2580488 | tf_op jit(solution)/shard_map/ppermute | solution.py:326
  30.1 2.4 %collective-permute-done.1.left = bf16[208,768]{1,0:T(8,128)(2,1)S(1)} collective-permute-done((bf16[208,768]{1,0:T(8,128)(2,1)}, bf16[208,768]{1,0:T(8,128)(2,1)S(1)}, u32[]{:S(2)}, u32[]{:S(2)}) %collective-permute-start.1) | collective-permute-done | bytes 319520 | tf_op jit(solution)/shard_map/ppermute | solution.py:376
  33.8 7.9 %shard_map.130 = (bf16[672,768]{1,0:T(8,128)(2,1)}, f32[6,448,384]{2,1,0:T(8,128)}, bf16[672,512]{1,0:T(8,128)(2,1)}) custom-call(s32[8]{0:T(128)} %get-tuple-element.16.sc, bf16[208,768]{1,0:T(8,128)(2,1)} %copy-done.8, bf16[1064,512]{1,0:T(8,128)(2,1)} %q.3, bf16[1064,128]{1,0:T(8,128)(2,1)} %k.3, bf16[1064,128]{1,0:T(8,128)(2,1)} %v.3, ...), custom_call_target="tpu_custom_call" | custom-call | flops 30000001024 | bytes 9000000 | tf_op jit(solution)/shard_map/pallas_call | solution.py:154
  41.7 2.2 %collective-permute-start.3 = (bf16[672,512]{1,0:T(8,128)(2,1)}, bf16[672,512]{1,0:T(8,128)(2,1)}, u32[]{:S(2)}, u32[]{:S(2)}) collective-permute-start(bf16[672,512]{1,0:T(8,128)(2,1)} %get-tuple-element.19), channel_id=1, source_target_pairs={{0,4},{4,0},{1,5},{5,1},{2,6},{6,2},{3,7},{7,3},{8,12},{12,8},{9,1... | collective-permute-start | bytes 2064392 | tf_op jit(solution)/shard_map/ppermute | solution.py:326
  45.6 2.8 %collective-permute-done.10 = bf16[672,640]{1,0:T(8,128)(2,1)S(1)} collective-permute-done((bf16[672,640]{1,0:T(8,128)(2,1)}, bf16[672,640]{1,0:T(8,128)(2,1)S(1)}, u32[]{:S(2)}, u32[]{:S(2)}) %collective-permute-start.10) | collective-permute-done | bytes 860192 | tf_op jit(solution)/shard_map/ppermute | solution.py:326
  48.4 3.5 %collective-permute-start.12 = (bf16[336,640]{1,0:T(8,128)(2,1)S(1)}, bf16[336,640]{1,0:T(8,128)(2,1)S(1)}, u32[]{:S(2)}, u32[]{:S(2)}) collective-permute-start(bf16[336,640]{1,0:T(8,128)(2,1)S(1)} %slice.26), channel_id=1, source_target_pairs={{0,3},{1,0},{2,1},{3,2},{4,7},{5,4},{6,5},{7,6},{8,11},{9,8},{10,9... | collective-permute-start | bytes 1290248 | tf_op jit(solution)/shard_map/ppermute | solution.py:326
  52.5 5.5 %collective-permute-done.3 = bf16[672,512]{1,0:T(8,128)(2,1)} collective-permute-done((bf16[672,512]{1,0:T(8,128)(2,1)}, bf16[672,512]{1,0:T(8,128)(2,1)}, u32[]{:S(2)}, u32[]{:S(2)}) %collective-permute-start.3) | collective-permute-done | bytes 688160 | tf_op jit(solution)/shard_map/ppermute | solution.py:326
  61.2 3.4 %collective-permute-done.13 = bf16[336,640]{1,0:T(8,128)(2,1)S(1)} collective-permute-done((bf16[336,640]{1,0:T(8,128)(2,1)S(1)}, bf16[336,640]{1,0:T(8,128)(2,1)S(1)}, u32[]{:S(2)}, u32[]{:S(2)}) %collective-permute-start.13) | collective-permute-done | bytes 430112 | tf_op jit(solution)/shard_map/ppermute | solution.py:326
  64.7 3.7 %multiply_convert_fusion = bf16[1280,1024]{1,0:T(8,128)(2,1)} fusion(bf16[672,1024]{1,0:T(8,128)(2,1)S(1)} %get-tuple-element.33, bf16[672,2560]{1,0:T(8,128)(2,1)S(1)} %constant_dynamic-update-slice_fusion.6, s32[]{:T(128)S(6)} %select_n.112), kind=kOutput, calls=%fused_computation.1 | convolution fusion | flops 1764229120 | bytes 5718020 | tf_op jit(solution)/shard_map/dot_general | solution.py:321
  69.6 5.6 %multiply_convert_fusion.1 = bf16[1280,1024]{1,0:T(8,128)(2,1)} fusion(bf16[672,1024]{1,0:T(8,128)(2,1)} %copy-done.4, bf16[672,2560]{1,0:T(8,128)(2,1)} %copy-done.1, s32[]{:T(128)S(6)} %select_n.111), kind=kOutput, calls=%fused_computation.2 | convolution fusion | flops 1764229120 | bytes 5718020 | tf_op jit(solution)/shard_map/dot_general | solution.py:321
  75.2 3.8 %add_convert_fusion = bf16[1280,1024]{1,0:T(8,128)(2,1)S(1)} fusion(bf16[1280,1024]{1,0:T(8,128)(2,1)} %shard_map.132, bf16[1280,1024]{1,0:T(8,128)(2,1)} %multiply_convert_fusion.1), kind=kLoop, calls=%fused_computation | loop fusion | flops 5242880 | bytes 7864320 | tf_op jit(solution)/shard_map/convert_element_type | solution.py:409
  79.2 1.8 %pad_maximum_fusion = bf16[2560,512]{1,0:T(8,128)(2,1)} fusion(bf16[1280,512]{1,0:T(8,128)(2,1)S(1)} %get-tuple-element.28, bf16[1280,512]{1,0:T(8,128)(2,1)S(1)} %get-tuple-element.27), kind=kLoop, calls=%fused_computation.3 | loop fusion | flops 5242880 | bytes 5242880 | tf_op jit(solution)/shard_map/concatenate | solution.py:410
  80.9 4.7 %convolution_convert_fusion.1.gm = bf16[672,512]{1,0:T(8,128)(2,1)S(1)} fusion(bf16[672,2560]{1,0:T(8,128)(2,1)} %copy-done.1, bf16[2560,512]{1,0:T(8,128)(2,1)} %all-gather.2.cloned.1.call-done.refs_1_), kind=kOutput, calls=%fused_computation.11 | convolution fusion | flops 1761951744 | bytes 6750208 | tf_op jit(solution)/shard_map/dot_general | solution.py:321
  85.7 2.1 %fusion.8 = f32[672,640]{1,0:T(8,128)S(1)} fusion(bf16[672,512]{1,0:T(8,128)(2,1)S(1)} %get-tuple-element.30, bf16[2560,512]{1,0:T(8,128)(2,1)} %collective-permute-done.5, s32[]{:T(128)S(6)} %select_n.105), kind=kOutput, calls=%fused_computation.19 | convolution fusion | flops 440401920 | bytes 3063812 | tf_op jit(solution)/shard_map/dot_general | solution.py:321
  90.1 4.5 %broadcast_select_fusion = (bf16[672,512]{1,0:T(8,128)(2,1)S(1)}, bf16[672,512]{1,0:T(8,128)(2,1)}) fusion(bf16[672,512]{1,0:T(8,128)(2,1)S(1)} %convolution_convert_fusion.1.gm, pred[]{:T(512)S(6)} %eq.12, bf16[672,2560]{1,0:T(8,128)(2,1)S(1)} %copy-done.2, bf16[2560,512]{1,0:T(8,128)(2,1)} %collective-permute-done.5), kind=kOutput, calls=%fused_computation.12 | convolution fusion | flops 1762295808 | bytes 8126465 | tf_op jit(solution)/shard_map/dot_general | solution.py:321
  94.6 1.7 %collective-permute-start.14 = (bf16[672,512]{1,0:T(8,128)(2,1)S(1)}, bf16[672,512]{1,0:T(8,128)(2,1)S(1)}, u32[]{:S(2)}, u32[]{:S(2)}) collective-permute-start(bf16[672,512]{1,0:T(8,128)(2,1)S(1)} %get-tuple-element.34), channel_id=1, source_target_pairs={{0,4},{4,0},{1,5},{5,1},{2,6},{6,2},{3,7},{7,3},{8,12},{12,8},{9,1... | collective-permute-start | bytes 2064392 | tf_op jit(solution)/shard_map/ppermute | solution.py:326
  96.6 1.8 %fusion.2 = f32[672,640]{1,0:T(8,128)S(1)} fusion(bf16[672,512]{1,0:T(8,128)(2,1)S(1)} %get-tuple-element.30, bf16[2560,512]{1,0:T(8,128)(2,1)} %collective-permute-done.5, s32[]{:T(128)S(6)} %select_n.109), kind=kOutput, calls=%fused_computation.15 | convolution fusion | flops 440401920 | bytes 3063812 | tf_op jit(solution)/shard_map/dot_general | solution.py:321
  98.5 1.8 %fusion.11 = f32[672,640]{1,0:T(8,128)S(1)} fusion(bf16[672,512]{1,0:T(8,128)(2,1)S(1)} %get-tuple-element.30, bf16[2560,512]{1,0:T(8,128)(2,1)} %collective-permute-done.5, s32[]{:T(128)S(6)} %select_n.101), kind=kOutput, calls=%fused_computation.22 | convolution fusion | flops 440401920 | bytes 3063812 | tf_op jit(solution)/shard_map/dot_general | solution.py:321
  100.3 8.3 %collective-permute-done.6 = bf16[336,640]{1,0:T(8,128)(2,1)S(1)} collective-permute-done((bf16[336,640]{1,0:T(8,128)(2,1)S(1)}, bf16[336,640]{1,0:T(8,128)(2,1)S(1)}, u32[]{:S(2)}, u32[]{:S(2)}) %collective-permute-start.6) | collective-permute-done | bytes 430112 | tf_op jit(solution)/shard_map/ppermute | solution.py:326
  111.9 2.7 %collective-permute-start.9 = (bf16[672,640]{1,0:T(8,128)(2,1)}, bf16[672,640]{1,0:T(8,128)(2,1)}, u32[]{:S(2)}, u32[]{:S(2)}) collective-permute-start(bf16[672,640]{1,0:T(8,128)(2,1)} %add_convert_fusion.2.after), channel_id=1, source_target_pairs={{0,3},{1,0},{2,1},{3,2},{4,7},{5,4},{6,5},{7,6},{8,11},{9,8},{10,9... | collective-permute-start | bytes 2580488 | tf_op jit(solution)/shard_map/ppermute | solution.py:326
  115.3 3.1 %fusion.17 = f32[672,640]{1,0:T(8,128)} fusion(bf16[672,512]{1,0:T(8,128)(2,1)S(1)} %get-tuple-element.30, bf16[2560,512]{1,0:T(8,128)(2,1)} %collective-permute-done.5, s32[]{:T(128)S(6)} %select_n.96), kind=kOutput, calls=%fused_computation.26 | convolution fusion | flops 440401920 | bytes 3063812 | tf_op jit(solution)/shard_map/dot_general | solution.py:321
  119.2 8.4 %shard_map.131 = (bf16[672,512]{1,0:T(8,128)(2,1)}, bf16[672,128]{1,0:T(8,128)(2,1)}, bf16[672,128]{1,0:T(8,128)(2,1)}) custom-call(s32[1]{0:T(128)} %bitcast.4.sel, bf16[672,512]{1,0:T(8,128)(2,1)} %copy-done.10, bf16[672,512]{1,0:T(8,128)(2,1)} %get-tuple-element.35.go, bf16[672,512]{1,0:T(8,128)(2,1)} %copy-done.7, ...), custom_call_target="tpu_custom_call" | custom-call | flops 6000000000 | bytes 9000000 | tf_op jit(solution)/shard_map/pallas_call | solution.py:238
  129.4 4.4 %collective-permute-start.16 = (bf16[160,512]{1,0:T(8,128)(2,1)}, bf16[160,512]{1,0:T(8,128)(2,1)S(1)}, u32[]{:S(2)}, u32[]{:S(2)}) collective-permute-start(bf16[160,512]{1,0:T(8,128)(2,1)} %get-tuple-element.25), channel_id=1, source_target_pairs={{72,0},{64,32},{0,64},{8,96},{73,1},{65,33},{1,65},{9,97},{74,2},{... | collective-permute-start | bytes 491528 | tf_op jit(solution)/shard_map/ppermute | solution.py:438
  134.5 3.2 %add_convert_fusion.1 = bf16[672,640]{1,0:T(8,128)(2,1)} fusion(bf16[672,640]{1,0:T(8,128)(2,1)} %collective-permute-done.9, bf16[672,640]{1,0:T(8,128)(2,1)} %collective-permute-done.7, f32[672,640]{1,0:T(8,128)S(1)} %fusion.19, f32[672,640]{1,0:T(8,128)} %fusion.17), kind=kLoop, calls=%fused_computation.6 | loop fusion | flops 2580480 | bytes 6021120 | tf_op jit(solution)/shard_map/convert_element_type | solution.py:432
  137.7 4.4 %collective-permute-done.16 = bf16[160,512]{1,0:T(8,128)(2,1)S(1)} collective-permute-done((bf16[160,512]{1,0:T(8,128)(2,1)}, bf16[160,512]{1,0:T(8,128)(2,1)S(1)}, u32[]{:S(2)}, u32[]{:S(2)}) %collective-permute-start.16) | collective-permute-done | bytes 163872 | tf_op jit(solution)/shard_map/ppermute | solution.py:438
  142.1 6.2 %collective-permute-done.17 = bf16[160,512]{1,0:T(8,128)(2,1)S(1)} collective-permute-done((bf16[160,512]{1,0:T(8,128)(2,1)}, bf16[160,512]{1,0:T(8,128)(2,1)S(1)}, u32[]{:S(2)}, u32[]{:S(2)}) %collective-permute-start.17) | collective-permute-done | bytes 163872 | tf_op jit(solution)/shard_map/ppermute | solution.py:438
  (66 shorter events, 21.5 us)
Async XLA Ops:
  7.2 68.0 %all-gather.2.cloned.1.call-start = ((), (), s32[]{:S(2)}) async-start(), calls=%async_computation.1 | async-start | bytes 2949120 | tf_op jit(solution)/shard_map/all_gather | solution.py:396
  7.2 4.6 %collective-permute-start = (bf16[160,512]{1,0:T(8,128)(2,1)}, bf16[160,512]{1,0:T(8,128)(2,1)S(1)}, u32[]{:S(2)}, u32[]{:S(2)}) collective-permute-start(bf16[160,512]{1,0:T(8,128)(2,1)} %here.1), channel_id=1, source_target_pairs={{0,8},{8,0},{1,9},{9,1},{2,10},{10,2},{3,11},{11,3},{4,12},{12,4},... | collective-permute-start | bytes 491528 | tf_op jit(solution)/shard_map/ppermute | solution.py:326
  11.8 0.7 copy-start.6
  14.2 15.1 %collective-permute-start.4 = (bf16[320,512]{1,0:T(8,128)(2,1)}, bf16[320,512]{1,0:T(8,128)(2,1)S(1)}, u32[]{:S(2)}, u32[]{:S(2)}) collective-permute-start(bf16[320,512]{1,0:T(8,128)(2,1)} %shard_map.128.after), channel_id=1, source_target_pairs={{0,192},{1,193},{2,194},{3,195},{4,200},{5,201},{6,202},{7,203},{8... | collective-permute-start | bytes 983048 | tf_op jit(solution)/shard_map/ppermute | solution.py:370
  22.4 10.1 %collective-permute-start.1 = (bf16[208,768]{1,0:T(8,128)(2,1)}, bf16[208,768]{1,0:T(8,128)(2,1)S(1)}, u32[]{:S(2)}, u32[]{:S(2)}) collective-permute-start(bf16[208,768]{1,0:T(8,128)(2,1)} %get-tuple-element.17), channel_id=1, source_target_pairs={{0,8},{8,16},{16,24},{24,32},{32,40},{40,48},{48,56},{56,64},{64,7... | collective-permute-start | bytes 958472 | tf_op jit(solution)/shard_map/ppermute | solution.py:376
  24.3 8.8 %collective-permute-start.2 = (bf16[208,768]{1,0:T(8,128)(2,1)}, bf16[208,768]{1,0:T(8,128)(2,1)S(1)}, u32[]{:S(2)}, u32[]{:S(2)}) collective-permute-start(bf16[208,768]{1,0:T(8,128)(2,1)} %get-tuple-element.18), channel_id=1, source_target_pairs={{8,0},{16,8},{24,16},{32,24},{40,32},{48,40},{56,48},{64,56},{72,6... | collective-permute-start | bytes 958472 | tf_op jit(solution)/shard_map/ppermute | solution.py:377
  26.7 21.7 %collective-permute-start.10 = (bf16[672,640]{1,0:T(8,128)(2,1)}, bf16[672,640]{1,0:T(8,128)(2,1)S(1)}, u32[]{:S(2)}, u32[]{:S(2)}) collective-permute-start(bf16[672,640]{1,0:T(8,128)(2,1)} %param.15), channel_id=1, source_target_pairs={{0,3},{1,0},{2,1},{3,2},{4,7},{5,4},{6,5},{7,6},{8,11},{9,8},{10,9... | collective-permute-start | bytes 2580488 | tf_op jit(solution)/shard_map/ppermute | solution.py:326
  29.3 22.6 %collective-permute-start.11 = (bf16[672,640]{1,0:T(8,128)(2,1)}, bf16[672,640]{1,0:T(8,128)(2,1)S(1)}, u32[]{:S(2)}, u32[]{:S(2)}) collective-permute-start(bf16[672,640]{1,0:T(8,128)(2,1)} %param.15), channel_id=1, source_target_pairs={{0,1},{1,2},{2,3},{3,0},{4,5},{5,6},{6,7},{7,4},{8,9},{9,10},{10,1... | collective-permute-start | bytes 2580488 | tf_op jit(solution)/shard_map/ppermute | solution.py:326
  29.3 0.7 copy-start.5
  30.1 97.6 %reduce-scatter.2.cloned.1.call-start = ((), (), s32[]{:S(2)}) async-start(), calls=%async_computation.2 | async-start | bytes 2949120 | tf_op jit(solution)/shard_map/reduce_scatter | solution.py:411
  32.5 0.7 copy-start.8
  33.1 0.7 copy-start.9
  41.7 16.3 %collective-permute-start.3 = (bf16[672,512]{1,0:T(8,128)(2,1)}, bf16[672,512]{1,0:T(8,128)(2,1)}, u32[]{:S(2)}, u32[]{:S(2)}) collective-permute-start(bf16[672,512]{1,0:T(8,128)(2,1)} %get-tuple-element.19), channel_id=1, source_target_pairs={{0,4},{4,0},{1,5},{5,1},{2,6},{6,2},{3,7},{7,3},{8,12},{12,8},{9,1... | collective-permute-start | bytes 2064392 | tf_op jit(solution)/shard_map/ppermute | solution.py:326
  44.0 1.5 copy-start.3
  48.4 12.7 %collective-permute-start.12 = (bf16[336,640]{1,0:T(8,128)(2,1)S(1)}, bf16[336,640]{1,0:T(8,128)(2,1)S(1)}, u32[]{:S(2)}, u32[]{:S(2)}) collective-permute-start(bf16[336,640]{1,0:T(8,128)(2,1)S(1)} %slice.26), channel_id=1, source_target_pairs={{0,3},{1,0},{2,1},{3,2},{4,7},{5,4},{6,5},{7,6},{8,11},{9,8},{10,9... | collective-permute-start | bytes 1290248 | tf_op jit(solution)/shard_map/ppermute | solution.py:326
  52.0 12.6 %collective-permute-start.13 = (bf16[336,640]{1,0:T(8,128)(2,1)S(1)}, bf16[336,640]{1,0:T(8,128)(2,1)S(1)}, u32[]{:S(2)}, u32[]{:S(2)}) collective-permute-start(bf16[336,640]{1,0:T(8,128)(2,1)S(1)} %slice.27), channel_id=1, source_target_pairs={{0,1},{1,2},{2,3},{3,0},{4,5},{5,6},{6,7},{7,4},{8,9},{9,10},{10,1... | collective-permute-start | bytes 1290248 | tf_op jit(solution)/shard_map/ppermute | solution.py:326
  59.4 9.0 %copy-start.4 = (bf16[672,1024]{1,0:T(8,128)(2,1)}, bf16[672,1024]{1,0:T(8,128)(2,1)S(1)}, u32[]{:S(2)}) copy-start(bf16[672,1024]{1,0:T(8,128)(2,1)S(1)} %get-tuple-element.33) | copy-start | bytes 4128772
  64.7 3.7 %copy-start.1 = (bf16[672,2560]{1,0:T(8,128)(2,1)}, bf16[672,2560]{1,0:T(8,128)(2,1)S(1)}, u32[]{:S(2)}) copy-start(bf16[672,2560]{1,0:T(8,128)(2,1)S(1)} %constant_dynamic-update-slice_fusion.6) | copy-start | bytes 10321924
  68.4 6.8 %collective-permute-start.15 = (bf16[1280,1024]{1,0:T(8,128)(2,1)}, bf16[1280,1024]{1,0:T(8,128)(2,1)}, u32[]{:S(2)}, u32[]{:S(2)}) collective-permute-start(bf16[1280,1024]{1,0:T(8,128)(2,1)} %multiply_convert_fusion), channel_id=1, source_target_pairs={{0,8},{8,0},{1,9},{9,1},{2,10},{10,2},{3,11},{11,3},{4,12},{12,4},... | collective-permute-start | bytes 7864328 | tf_op jit(solution)/shard_map/ppermute | solution.py:326
  75.2 10.5 %collective-permute-start.5 = (bf16[2560,512]{1,0:T(8,128)(2,1)}, bf16[2560,512]{1,0:T(8,128)(2,1)}, u32[]{:S(2)}, u32[]{:S(2)}) collective-permute-start(bf16[2560,512]{1,0:T(8,128)(2,1)} %all-gather.2.cloned.1.call-done.refs_1_), channel_id=1, source_target_pairs={{0,8},{8,0},{1,9},{9,1},{2,10},{10,2},{3,11},{11,3},{4,12},{12,4},... | collective-permute-start | bytes 7864328 | tf_op jit(solution)/shard_map/ppermute | solution.py:326
  85.7 3.5 %copy-start.10 = (bf16[672,512]{1,0:T(8,128)(2,1)}, bf16[672,512]{1,0:T(8,128)(2,1)S(1)}, u32[]{:S(2)}) copy-start(bf16[672,512]{1,0:T(8,128)(2,1)S(1)} %convolution_convert_fusion.1.gm) | copy-start | bytes 2064388
  85.7 2.2 %copy-start = (bf16[2560,512]{1,0:T(8,128)(2,1)S(1)}, bf16[2560,512]{1,0:T(8,128)(2,1)}, u32[]{:S(2)}) copy-start(bf16[2560,512]{1,0:T(8,128)(2,1)} %all-gather.2.cloned.1.call-done.refs_1_) | copy-start | bytes 7864324
  87.9 2.2 %copy-start.2 = (bf16[672,2560]{1,0:T(8,128)(2,1)S(1)}, bf16[672,2560]{1,0:T(8,128)(2,1)}, u32[]{:S(2)}) copy-start(bf16[672,2560]{1,0:T(8,128)(2,1)} %copy-done.1) | copy-start | bytes 10321924
  88.7 21.6 %collective-permute-start.8 = (bf16[336,640]{1,0:T(8,128)(2,1)S(1)}, bf16[336,640]{1,0:T(8,128)(2,1)S(1)}, u32[]{:S(2)}, u32[]{:S(2)}) collective-permute-start(bf16[336,640]{1,0:T(8,128)(2,1)S(1)} %get-tuple-element.32), channel_id=1, source_target_pairs={{0,3},{1,0},{2,1},{3,2},{4,7},{5,4},{6,5},{7,6},{8,11},{9,8},{10,9... | collective-permute-start | bytes 1290248 | tf_op jit(solution)/shard_map/ppermute | solution.py:326
  94.6 23.7 %collective-permute-start.14 = (bf16[672,512]{1,0:T(8,128)(2,1)S(1)}, bf16[672,512]{1,0:T(8,128)(2,1)S(1)}, u32[]{:S(2)}, u32[]{:S(2)}) collective-permute-start(bf16[672,512]{1,0:T(8,128)(2,1)S(1)} %get-tuple-element.34), channel_id=1, source_target_pairs={{0,4},{4,0},{1,5},{5,1},{2,6},{6,2},{3,7},{7,3},{8,12},{12,8},{9,1... | collective-permute-start | bytes 2064392 | tf_op jit(solution)/shard_map/ppermute | solution.py:326
  96.4 12.2 %collective-permute-start.6 = (bf16[336,640]{1,0:T(8,128)(2,1)S(1)}, bf16[336,640]{1,0:T(8,128)(2,1)S(1)}, u32[]{:S(2)}, u32[]{:S(2)}) collective-permute-start(bf16[336,640]{1,0:T(8,128)(2,1)S(1)} %get-tuple-element.31), channel_id=1, source_target_pairs={{0,1},{1,2},{2,3},{3,0},{4,5},{5,6},{6,7},{7,4},{8,9},{9,10},{10,1... | collective-permute-start | bytes 1290248 | tf_op jit(solution)/shard_map/ppermute | solution.py:326
  110.2 24.3 %collective-permute-start.7 = (bf16[672,640]{1,0:T(8,128)(2,1)}, bf16[672,640]{1,0:T(8,128)(2,1)}, u32[]{:S(2)}, u32[]{:S(2)}) collective-permute-start(bf16[672,640]{1,0:T(8,128)(2,1)} %add_convert_fusion.3), channel_id=1, source_target_pairs={{0,1},{1,2},{2,3},{3,0},{4,5},{5,6},{6,7},{7,4},{8,9},{9,10},{10,1... | collective-permute-start | bytes 2580488 | tf_op jit(solution)/shard_map/ppermute | solution.py:326
  111.9 22.7 %collective-permute-start.9 = (bf16[672,640]{1,0:T(8,128)(2,1)}, bf16[672,640]{1,0:T(8,128)(2,1)}, u32[]{:S(2)}, u32[]{:S(2)}) collective-permute-start(bf16[672,640]{1,0:T(8,128)(2,1)} %add_convert_fusion.2.after), channel_id=1, source_target_pairs={{0,3},{1,0},{2,1},{3,2},{4,7},{5,4},{6,5},{7,6},{8,11},{9,8},{10,9... | collective-permute-start | bytes 2580488 | tf_op jit(solution)/shard_map/ppermute | solution.py:326
  118.3 0.8 copy-start.7
  129.4 12.8 %collective-permute-start.16 = (bf16[160,512]{1,0:T(8,128)(2,1)}, bf16[160,512]{1,0:T(8,128)(2,1)S(1)}, u32[]{:S(2)}, u32[]{:S(2)}) collective-permute-start(bf16[160,512]{1,0:T(8,128)(2,1)} %get-tuple-element.25), channel_id=1, source_target_pairs={{72,0},{64,32},{0,64},{8,96},{73,1},{65,33},{1,65},{9,97},{74,2},{... | collective-permute-start | bytes 491528 | tf_op jit(solution)/shard_map/ppermute | solution.py:438
  133.8 14.5 %collective-permute-start.17 = (bf16[160,512]{1,0:T(8,128)(2,1)}, bf16[160,512]{1,0:T(8,128)(2,1)S(1)}, u32[]{:S(2)}, u32[]{:S(2)}) collective-permute-start(bf16[160,512]{1,0:T(8,128)(2,1)} %get-tuple-element.26), channel_id=1, source_target_pairs={{88,0},{80,32},{16,64},{24,96},{89,1},{81,33},{17,65},{25,97},{90,... | collective-permute-start | bytes 491528 | tf_op jit(solution)/shard_map/ppermute | solution.py:438
Sparse Core Ops, SparseCore 0:
  30.2 39.3 all-gather.1
  81.1 36.6 reduce-scatter.1

commit v4 on v3

--- a/solution.py
+++ b/solution.py
@@ -64,14 +64,11 @@
         sc[2 + t] = begin
         begin = begin + lengths[first + t]
 
-    wide[0:ROWS, 0:512] = q[...].astype(F32)
-    wide[0:ROWS, 512:640] = k[...].astype(F32)
-    wide[0:ROWS, 640:768] = v[...].astype(F32)
     tail = jnp.clip(total - EDGE, 0, ROWS - EDGE)
-    rest = lax.rem(tail, 8)
-    rows = wide[pl.ds(pl.multiple_of(tail - rest, 8), EDGE + 8), :]
-    rows = pltpu.roll(rows, lax.rem(EDGE + 8 - rest, EDGE + 8), 0)
-    to_right[...] = rows[:EDGE].astype(BF)
+    for t in range(6):
+        ref, at = (q, t) if t < 4 else ((k, 0) if t == 4 else (v, 0))
+        wide[t, :, :] = ref[:, HEAD * at : HEAD * (at + 1)].astype(F32)
+        to_right[:, HEAD * t : HEAD * (t + 1)] = wide[t, pl.ds(tail, EDGE), :].astype(BF)
     to_left[:, 0:512] = q[0:EDGE, :]
     to_left[:, 512:640] = k[0:EDGE, :]
     to_left[:, 640:768] = v[0:EDGE, :]
@@ -86,33 +83,29 @@
         out_shape=(out, out, jax.ShapeDtypeStruct((2 + SEQS,), jnp.int32)),
         in_specs=[sm, sm, sm, vm, vm, vm, pl.BlockSpec(memory_space=pl.ANY)],
         out_specs=(vm, vm, sm),
-        scratch_shapes=[pltpu.VMEM((ROWS + 8, 768), F32)],
+        scratch_shapes=[pltpu.VMEM((6, ROWS, HEAD), F32)],
         compiler_params=params(),
         cost_estimate=cost(1, 1),
     )(place, lengths, source, q, k, v, after)
 
 
 def fwd_kernel(sc, left, q, k, v, right, qg, kg, pk, p_out, o_out, com, qn, kn, p_buf, sems):
-    com[0:EDGE, :] = left[...].astype(F32)
-    com[EDGE : EDGE + ROWS, 0:512] = q[...].astype(F32)
-    com[EDGE : EDGE + ROWS, 512:640] = k[...].astype(F32)
-    com[EDGE : EDGE + ROWS, 640:768] = v[...].astype(F32)
-    rest = lax.rem(sc[1], 8)
-    at = pl.ds(pl.multiple_of(sc[1] - rest, 8), EDGE + 8)
-    tail = jnp.concatenate([right[...].astype(F32), jnp.zeros((8, 768), F32)], axis=0)
-    tail = pltpu.roll(tail, rest, 0)
-    rows = lax.broadcasted_iota(jnp.int32, (EDGE + 8, 768), 0)
-    com[at, :] = jnp.where(rows >= rest, tail, com[at, :])
-    rest = lax.rem(sc[0], 8)
-    base = pl.multiple_of(sc[0] - rest, 8)
-    back = lax.rem(BLK + 8 - rest, BLK + 8)
+    parts = ((q, 0, 4), (k, 4, 1), (v, 5, 1))
+    for ref, at, count in parts:
+        for t in range(count):
+            lanes = slice(HEAD * t, HEAD * (t + 1))
+            com[at + t, EDGE : EDGE + ROWS, :] = ref[:, lanes].astype(F32)
+    for t in range(6):
+        lanes = slice(HEAD * t, HEAD * (t + 1))
+        com[t, 0:EDGE, :] = left[:, lanes].astype(F32)
+        com[t, pl.ds(sc[1], EDGE), :] = right[:, lanes].astype(F32)
     for i in range(NBLK):
         r = slice(BLK * i, BLK * (i + 1))
-        x = com[pl.ds(base + BLK * i, BLK + 8), :]
-        x = pltpu.roll(x, back, 0)[:BLK]
-        pk[r, :] = x.astype(BF)
+        xs = [com[t, pl.ds(sc[0] + BLK * i, BLK), :] for t in range(6)]
+        for t in range(6):
+            pk[r, HEAD * t : HEAD * (t + 1)] = xs[t].astype(BF)
         for h in range(HEADS + 1):
-            e = x[:, HEAD * h : HEAD * (h + 1)]
+            e = xs[h]
             ms = jnp.mean(e * e, axis=-1, keepdims=True)
             gain = qg[...] if h < HEADS else kg[...]
             n = (e * lax.rsqrt(ms + EPS) * gain).astype(BF)
@@ -161,7 +154,7 @@
         in_specs=[pl.BlockSpec(memory_space=pltpu.SMEM)] + [vm] * 7,
         out_specs=(vm, pl.BlockSpec(memory_space=pl.ANY), vm),
         scratch_shapes=[
-            pltpu.VMEM((EDGE + ROWS + EDGE + 8, 768), F32),
+            pltpu.VMEM((6, EDGE + ROWS + EDGE + 8, HEAD), F32),
             pltpu.VMEM((TOK, 512), BF),
             pltpu.VMEM((TOK, HEAD), BF),
             pltpu.VMEM((NBLK, HEADS * BLK, WIN), F32),
@@ -423,13 +416,14 @@
         return product(att_m, rows_m, 1, 1) + product(att_o, rows_o, 1, 1)
 
     opposite = layer(2).astype(BF)
-    up = shift(opposite[:mid], "x", 1).astype(F32)
+    own = layer(0)
+    up = hold(shift(opposite[:mid], "x", 1), own).astype(F32)
     down = shift(opposite[mid:], "x", -1).astype(F32)
     up = (layer(1) + jnp.pad(up, ((0, mid), (0, 0)))).astype(BF)
     down = (layer(3) + jnp.pad(down, ((mid, 0), (0, 0)))).astype(BF)
     last = down
     got = [shift(up, "x", 1).astype(F32), shift(down, "x", -1).astype(F32)]
-    layer_out = (layer(0) + got[0] + got[1]).astype(BF)
+    layer_out = (own + got[0] + got[1]).astype(BF)
 
     ready = halves_of(yl.astype(jnp.int32)[None], summed, last)
     query_grad, key_grad, value_grad = backward(

time: 157 us -> 151 us (0.962)
  waiting for transfers between devices: 36.6 us -> 30.8 us
  local copies, waits for them, and re-layouts: 6.28 us -> 3.4 us
  starting transfers between devices: 33.3 us -> 35.4 us
    ppermute x2, waiting for transfers between devices: 10.6 us -> 6.05 us  [body(): lax.ppermute(ready[flip], ALL, final_moves(flip))]
    ppermute x13, starting transfers between devices: 18.2 us -> 20.7 us  [shift(): return lax.ppermute(value, axis, [(i, (i + k) % n) for i in range(n)])]
    unnamed x23, local copies, waits for them, and re-layouts: 4.06 us -> 2.34 us
    dot_general x12, matrix products: 32.2 us -> 33.7 us  [product(): lax.dot_general(a, b, (((ca,), (cb,)), ((), ())), preferred_element_type=...]
where the time goes in v4:
time: 151 us; the launch traced here: 150 us
  starting transfers between devices  35.4 us (23%)
  matrix products  33.7 us (22%)
  waiting for transfers between devices  30.8 us (20%)
  Pallas kernels  21.8 us (14%)
  between operations  14.3 us (9%)
  other arithmetic  9.97 us (7%)
  local copies, waits for them, and re-layouts  3.4 us (2%)
    dot_general x12, matrix products, product(): lax.dot_general(a, b, (((ca,), (cb,)), ((), ())), preferred_element_type=...  33.7 us
    ppermute x13, waiting for transfers between devices, shift(): return lax.ppermute(value, axis, [(i, (i + k) % n) for i in range(n)])  21.9 us
    ppermute x13, starting transfers between devices, shift(): return lax.ppermute(value, axis, [(i, (i + k) % n) for i in range(n)])  20.7 us
    pallas_call x1, Pallas kernels, backward(): pl.pallas_call(bwd_kernel, out_shape=(jax.ShapeDtypeStruct((TOK, 512), BF...  8.6 us
    pallas_call x1, Pallas kernels, forward(): pl.pallas_call(fwd_kernel, out_shape=(jax.ShapeDtypeStruct((TOK, 768), BF...  7.25 us
    ppermute x2, waiting for transfers between devices, body(): lax.ppermute(ready[flip], ALL, final_moves(flip))  6.05 us
    ppermute x1, starting transfers between devices, body(): w_moved = lax.ppermute(w_chip, ALL, weight_moves())  5.55 us
    ppermute x2, starting transfers between devices, body(): lax.ppermute(ready[flip], ALL, final_moves(flip))  4.81 us
  transfers between devices with their start and end apart: 20, of which 10 were waited for; matrix products, arithmetic and copies ran while one was open for 29% of the time, Pallas kernels for 13%

profile of v4, /device:TPU:1, one launch (start us, length us, event | category | flops | bytes accessed | tf_op | source)
XLA Modules:
  0.0 149.5 jit_solution(14930589724087023399)
XLA Ops:
  7.2 3.3 %collective-permute-start = (bf16[160,512]{1,0:T(8,128)(2,1)}, bf16[160,512]{1,0:T(8,128)(2,1)S(1)}, u32[]{:S(2)}, u32[]{:S(2)}) collective-permute-start(bf16[160,512]{1,0:T(8,128)(2,1)} %here.1), channel_id=1, source_target_pairs={{0,8},{8,0},{1,9},{9,1},{2,10},{10,2},{3,11},{11,3},{4,12},{12,4},... | collective-permute-start | bytes 491528 | tf_op jit(solution)/shard_map/ppermute | solution.py:319
  14.2 5.5 %collective-permute-start.4 = (bf16[320,512]{1,0:T(8,128)(2,1)}, bf16[320,512]{1,0:T(8,128)(2,1)S(1)}, u32[]{:S(2)}, u32[]{:S(2)}) collective-permute-start(bf16[320,512]{1,0:T(8,128)(2,1)} %shard_map.128.after), channel_id=1, source_target_pairs={{0,192},{1,193},{2,194},{3,195},{4,200},{5,201},{6,202},{7,203},{8... | collective-permute-start | bytes 983048 | tf_op jit(solution)/shard_map/ppermute | solution.py:363
  19.7 2.5 %shard_map.129 = (bf16[208,768]{1,0:T(8,128)(2,1)}, bf16[208,768]{1,0:T(8,128)(2,1)}, s32[8]{0:T(128)}) custom-call(s32[1]{0:T(128)} %bitcast.place, s32[192]{0:T(256)} %lengths.1, s32[192]{0:T(256)} %source.1, bf16[1064,512]{1,0:T(8,128)(2,1)} %q.3, bf16[1064,128]{1,0:T(8,128)(2,1)} %k.3, bf16[1064,128]{1,0:T(8,128)(2,1)} %v.3, ...), custom_call_target="tpu_custom_call" | custom-call | flops 1 | bytes 1 | tf_op jit(solution)/shard_map/pallas_call | solution.py:81
  22.3 1.9 %collective-permute-start.1 = (bf16[208,768]{1,0:T(8,128)(2,1)}, bf16[208,768]{1,0:T(8,128)(2,1)S(1)}, u32[]{:S(2)}, u32[]{:S(2)}) collective-permute-start(bf16[208,768]{1,0:T(8,128)(2,1)} %get-tuple-element.17), channel_id=1, source_target_pairs={{0,8},{8,16},{16,24},{24,32},{32,40},{40,48},{48,56},{56,64},{64,7... | collective-permute-start | bytes 958472 | tf_op jit(solution)/shard_map/ppermute | solution.py:369
  24.2 2.4 %collective-permute-start.2 = (bf16[208,768]{1,0:T(8,128)(2,1)}, bf16[208,768]{1,0:T(8,128)(2,1)}, u32[]{:S(2)}, u32[]{:S(2)}) collective-permute-start(bf16[208,768]{1,0:T(8,128)(2,1)} %get-tuple-element.18), channel_id=1, source_target_pairs={{8,0},{16,8},{24,16},{32,24},{40,32},{48,40},{56,48},{64,56},{72,6... | collective-permute-start | bytes 958472 | tf_op jit(solution)/shard_map/ppermute | solution.py:370
  30.2 2.2 %collective-permute-done.1.left = bf16[208,768]{1,0:T(8,128)(2,1)S(1)} collective-permute-done((bf16[208,768]{1,0:T(8,128)(2,1)}, bf16[208,768]{1,0:T(8,128)(2,1)S(1)}, u32[]{:S(2)}, u32[]{:S(2)}) %collective-permute-start.1) | collective-permute-done | bytes 319520 | tf_op jit(solution)/shard_map/ppermute | solution.py:369
  33.1 7.2 %shard_map.130 = (bf16[672,768]{1,0:T(8,128)(2,1)}, f32[6,448,384]{2,1,0:T(8,128)}, bf16[672,512]{1,0:T(8,128)(2,1)}) custom-call(s32[8]{0:T(128)} %get-tuple-element.16.sc, bf16[208,768]{1,0:T(8,128)(2,1)} %copy-done.9, bf16[1064,512]{1,0:T(8,128)(2,1)} %q.3, bf16[1064,128]{1,0:T(8,128)(2,1)} %k.3, bf16[1064,128]{1,0:T(8,128)(2,1)} %v.3, ...), custom_call_target="tpu_custom_call" | custom-call | flops 30000001024 | bytes 9000000 | tf_op jit(solution)/shard_map/pallas_call | solution.py:147
  40.4 2.1 %collective-permute-start.3 = (bf16[672,512]{1,0:T(8,128)(2,1)}, bf16[672,512]{1,0:T(8,128)(2,1)}, u32[]{:S(2)}, u32[]{:S(2)}) collective-permute-start(bf16[672,512]{1,0:T(8,128)(2,1)} %get-tuple-element.19), channel_id=1, source_target_pairs={{0,4},{4,0},{1,5},{5,1},{2,6},{6,2},{3,7},{7,3},{8,12},{12,8},{9,1... | collective-permute-start | bytes 2064392 | tf_op jit(solution)/shard_map/ppermute | solution.py:319
  43.7 5.3 %collective-permute-done.11 = bf16[672,640]{1,0:T(8,128)(2,1)S(1)} collective-permute-done((bf16[672,640]{1,0:T(8,128)(2,1)S(1)}, bf16[672,640]{1,0:T(8,128)(2,1)S(1)}, u32[]{:S(2)}, u32[]{:S(2)}) %collective-permute-start.11) | collective-permute-done | bytes 860192 | tf_op jit(solution)/shard_map/ppermute | solution.py:319
  49.2 2.9 %collective-permute-start.12 = (bf16[336,640]{1,0:T(8,128)(2,1)S(1)}, bf16[336,640]{1,0:T(8,128)(2,1)S(1)}, u32[]{:S(2)}, u32[]{:S(2)}) collective-permute-start(bf16[336,640]{1,0:T(8,128)(2,1)S(1)} %slice.26), channel_id=1, source_target_pairs={{0,3},{1,0},{2,1},{3,2},{4,7},{5,4},{6,5},{7,6},{8,11},{9,8},{10,9... | collective-permute-start | bytes 1290248 | tf_op jit(solution)/shard_map/ppermute | solution.py:319
  52.4 5.3 %collective-permute-done.3 = bf16[672,512]{1,0:T(8,128)(2,1)} collective-permute-done((bf16[672,512]{1,0:T(8,128)(2,1)}, bf16[672,512]{1,0:T(8,128)(2,1)}, u32[]{:S(2)}, u32[]{:S(2)}) %collective-permute-start.3) | collective-permute-done | bytes 688160 | tf_op jit(solution)/shard_map/ppermute | solution.py:319
  59.0 1.9 %collective-permute-done.12 = bf16[336,640]{1,0:T(8,128)(2,1)S(1)} collective-permute-done((bf16[336,640]{1,0:T(8,128)(2,1)S(1)}, bf16[336,640]{1,0:T(8,128)(2,1)S(1)}, u32[]{:S(2)}, u32[]{:S(2)}) %collective-permute-start.12) | collective-permute-done | bytes 430112 | tf_op jit(solution)/shard_map/ppermute | solution.py:319
  61.9 3.7 %multiply_convert_fusion = bf16[1280,1024]{1,0:T(8,128)(2,1)} fusion(bf16[672,1024]{1,0:T(8,128)(2,1)S(1)} %get-tuple-element.33, bf16[672,2560]{1,0:T(8,128)(2,1)S(1)} %constant_dynamic-update-slice_fusion.6, s32[]{:T(128)S(6)} %select_n.112), kind=kOutput, calls=%fused_computation.1 | convolution fusion | flops 1764229120 | bytes 5718020 | tf_op jit(solution)/shard_map/dot_general | solution.py:314
  66.5 5.6 %multiply_convert_fusion.1 = bf16[1280,1024]{1,0:T(8,128)(2,1)} fusion(bf16[672,1024]{1,0:T(8,128)(2,1)} %copy-done.6, bf16[672,2560]{1,0:T(8,128)(2,1)} %copy-done.2, s32[]{:T(128)S(6)} %select_n.111), kind=kOutput, calls=%fused_computation.2 | convolution fusion | flops 1764229120 | bytes 5718020 | tf_op jit(solution)/shard_map/dot_general | solution.py:314
  72.4 3.8 %add_convert_fusion = bf16[1280,1024]{1,0:T(8,128)(2,1)S(1)} fusion(bf16[1280,1024]{1,0:T(8,128)(2,1)} %shard_map.133, bf16[1280,1024]{1,0:T(8,128)(2,1)} %multiply_convert_fusion.1), kind=kLoop, calls=%fused_computation | loop fusion | flops 5242880 | bytes 7864320 | tf_op jit(solution)/shard_map/convert_element_type | solution.py:402
  76.3 1.8 %pad_maximum_fusion = bf16[2560,512]{1,0:T(8,128)(2,1)} fusion(bf16[1280,512]{1,0:T(8,128)(2,1)S(1)} %get-tuple-element.28, bf16[1280,512]{1,0:T(8,128)(2,1)S(1)} %get-tuple-element.27), kind=kLoop, calls=%fused_computation.3 | loop fusion | flops 5242880 | bytes 5242880 | tf_op jit(solution)/shard_map/concatenate | solution.py:403
  78.1 4.9 %convolution_convert_fusion.1.gm = bf16[672,512]{1,0:T(8,128)(2,1)S(1)} fusion(bf16[672,2560]{1,0:T(8,128)(2,1)} %copy-done.2, bf16[2560,512]{1,0:T(8,128)(2,1)} %all-gather.2.cloned.1.call-done.refs_1_), kind=kOutput, calls=%fused_computation.12 | convolution fusion | flops 1761951744 | bytes 6750208 | tf_op jit(solution)/shard_map/dot_general | solution.py:314
  83.0 5.0 %broadcast_select_fusion = (bf16[672,512]{1,0:T(8,128)(2,1)}, bf16[672,512]{1,0:T(8,128)(2,1)}) fusion(bf16[672,512]{1,0:T(8,128)(2,1)S(1)} %convolution_convert_fusion.1.gm, pred[]{:T(512)S(6)} %eq.12, bf16[672,2560]{1,0:T(8,128)(2,1)S(1)} %copy-done.3, bf16[2560,512]{1,0:T(8,128)(2,1)} %collective-permute-done.5), kind=kOutput, calls=%fused_computation.13 | convolution fusion | flops 1762295808 | bytes 8126465 | tf_op jit(solution)/shard_map/dot_general | solution.py:314
  88.0 2.7 %collective-permute-start.14 = (bf16[672,512]{1,0:T(8,128)(2,1)}, bf16[672,512]{1,0:T(8,128)(2,1)}, u32[]{:S(2)}, u32[]{:S(2)}) collective-permute-start(bf16[672,512]{1,0:T(8,128)(2,1)} %get-tuple-element.34), channel_id=1, source_target_pairs={{0,4},{4,0},{1,5},{5,1},{2,6},{6,2},{3,7},{7,3},{8,12},{12,8},{9,1... | collective-permute-start | bytes 2064392 | tf_op jit(solution)/shard_map/ppermute | solution.py:319
  90.8 1.8 %fusion.8 = f32[672,640]{1,0:T(8,128)S(1)} fusion(bf16[672,512]{1,0:T(8,128)(2,1)S(1)} %get-tuple-element.30, bf16[2560,512]{1,0:T(8,128)(2,1)} %collective-permute-done.5, s32[]{:T(128)S(6)} %select_n.105), kind=kOutput, calls=%fused_computation.20 | convolution fusion | flops 440401920 | bytes 3063812 | tf_op jit(solution)/shard_map/dot_general | solution.py:314
  96.2 1.8 %fusion.17 = f32[672,640]{1,0:T(8,128)S(1)} fusion(bf16[672,512]{1,0:T(8,128)(2,1)S(1)} %get-tuple-element.30, bf16[2560,512]{1,0:T(8,128)(2,1)} %collective-permute-done.5, s32[]{:T(128)S(6)} %select_n.96), kind=kOutput, calls=%fused_computation.27 | convolution fusion | flops 440401920 | bytes 3063812 | tf_op jit(solution)/shard_map/dot_general | solution.py:314
  98.0 2.0 %convolution_add_fusion.refs_1_ = f32[672,640]{1,0:T(8,128)} fusion(f32[672,640]{1,0:T(8,128)S(1)} %fusion.17, bf16[672,512]{1,0:T(8,128)(2,1)S(1)} %get-tuple-element.29, bf16[2560,512]{1,0:T(8,128)(2,1)S(1)} %copy-done.1, s32[]{:T(128)S(6)} %select_n.96), kind=kOutput, calls=%fused_computation.10 | convolution fusion | flops 440832000 | bytes 4784132 | tf_op jit(solution)/shard_map/dot_general | solution.py:314
  100.0 1.8 %fusion.2 = f32[672,640]{1,0:T(8,128)S(1)} fusion(bf16[672,512]{1,0:T(8,128)(2,1)S(1)} %get-tuple-element.30, bf16[2560,512]{1,0:T(8,128)(2,1)} %collective-permute-done.5, s32[]{:T(128)S(6)} %select_n.109), kind=kOutput, calls=%fused_computation.16 | convolution fusion | flops 440401920 | bytes 3063812 | tf_op jit(solution)/shard_map/dot_general | solution.py:314
  101.9 1.8 %fusion.11 = f32[672,640]{1,0:T(8,128)S(1)} fusion(bf16[672,512]{1,0:T(8,128)(2,1)S(1)} %get-tuple-element.30, bf16[2560,512]{1,0:T(8,128)(2,1)} %collective-permute-done.5, s32[]{:T(128)S(6)} %select_n.101), kind=kOutput, calls=%fused_computation.23 | convolution fusion | flops 440401920 | bytes 3063812 | tf_op jit(solution)/shard_map/dot_general | solution.py:314
  103.7 2.0 %collective-permute-done.8 = bf16[336,640]{1,0:T(8,128)(2,1)S(1)} collective-permute-done((bf16[336,640]{1,0:T(8,128)(2,1)S(1)}, bf16[336,640]{1,0:T(8,128)(2,1)S(1)}, u32[]{:S(2)}, u32[]{:S(2)}) %collective-permute-start.8) | collective-permute-done | bytes 430112 | tf_op jit(solution)/shard_map/ppermute | solution.py:319
  107.4 2.8 %collective-permute-start.9 = (bf16[672,640]{1,0:T(8,128)(2,1)}, bf16[672,640]{1,0:T(8,128)(2,1)}, u32[]{:S(2)}, u32[]{:S(2)}) collective-permute-start(bf16[672,640]{1,0:T(8,128)(2,1)} %add_convert_fusion.2.after), channel_id=1, source_target_pairs={{0,3},{1,0},{2,1},{3,2},{4,7},{5,4},{6,5},{7,6},{8,11},{9,8},{10,9... | collective-permute-start | bytes 2580488 | tf_op jit(solution)/shard_map/ppermute | solution.py:319
  110.2 2.9 %add_convert_fusion.3 = bf16[672,640]{1,0:T(8,128)(2,1)} fusion(f32[672,640]{1,0:T(8,128)S(1)} %fusion.11, bf16[336,640]{1,0:T(8,128)(2,1)} %shard_map.131, bf16[672,512]{1,0:T(8,128)(2,1)S(1)} %get-tuple-element.29, bf16[2560,512]{1,0:T(8,128)(2,1)} %all-gather.2.cloned.1.call-done.refs_1_, s32[]{:T(128)S(6)} %select_n.101), kind=kOutput, calls=%fused_computation.8 | convolution fusion | flops 442122240 | bytes 4354052 | tf_op jit(solution)/shard_map/dot_general | solution.py:314
  113.1 8.6 %shard_map.132 = (bf16[672,512]{1,0:T(8,128)(2,1)}, bf16[672,128]{1,0:T(8,128)(2,1)}, bf16[672,128]{1,0:T(8,128)(2,1)}) custom-call(s32[1]{0:T(128)} %bitcast.4.sel, bf16[672,512]{1,0:T(8,128)(2,1)} %copy-done.10, bf16[672,512]{1,0:T(8,128)(2,1)} %get-tuple-element.35.go, bf16[672,512]{1,0:T(8,128)(2,1)} %collective-permute-done.14.got, ...), custom_call_target="tpu_custom_call" | custom-call | flops 6000000000 | bytes 9000000 | tf_op jit(solution)/shard_map/pallas_call | solution.py:231
  123.4 3.9 %collective-permute-start.16 = (bf16[160,512]{1,0:T(8,128)(2,1)}, bf16[160,512]{1,0:T(8,128)(2,1)S(1)}, u32[]{:S(2)}, u32[]{:S(2)}) collective-permute-start(bf16[160,512]{1,0:T(8,128)(2,1)} %get-tuple-element.25), channel_id=1, source_target_pairs={{72,0},{64,32},{0,64},{8,96},{73,1},{65,33},{1,65},{9,97},{74,2},{... | collective-permute-start | bytes 491528 | tf_op jit(solution)/shard_map/ppermute | solution.py:432
  128.2 5.3 %collective-permute-done.7 = bf16[672,640]{1,0:T(8,128)(2,1)S(1)} collective-permute-done((bf16[672,640]{1,0:T(8,128)(2,1)}, bf16[672,640]{1,0:T(8,128)(2,1)S(1)}, u32[]{:S(2)}, u32[]{:S(2)}) %collective-permute-start.7) | collective-permute-done | bytes 860192 | tf_op jit(solution)/shard_map/ppermute | solution.py:319
  133.5 2.3 %add_convert_fusion.1 = bf16[672,640]{1,0:T(8,128)(2,1)} fusion(bf16[672,640]{1,0:T(8,128)(2,1)} %collective-permute-done.9, f32[672,640]{1,0:T(8,128)S(1)} %copy-done, bf16[672,640]{1,0:T(8,128)(2,1)S(1)} %collective-permute-done.7), kind=kLoop, calls=%fused_computation.6 | loop fusion | flops 2150400 | bytes 4300800 | tf_op jit(solution)/shard_map/convert_element_type | solution.py:426
  135.9 6.0 %collective-permute-done.17 = bf16[160,512]{1,0:T(8,128)(2,1)S(1)} collective-permute-done((bf16[160,512]{1,0:T(8,128)(2,1)}, bf16[160,512]{1,0:T(8,128)(2,1)S(1)}, u32[]{:S(2)}, u32[]{:S(2)}) %collective-permute-start.17) | collective-permute-done | bytes 163872 | tf_op jit(solution)/shard_map/ppermute | solution.py:432
  (67 shorter events, 21.9 us)
Async XLA Ops:
  7.2 19.5 %copy-start.5 = (bf16[672,640]{1,0:T(8,128)(2,1)S(1)}, bf16[672,640]{1,0:T(8,128)(2,1)}, u32[]{:S(2)}) copy-start(bf16[672,640]{1,0:T(8,128)(2,1)} %param.15) | copy-start | bytes 2580484
  7.2 64.9 %all-gather.2.cloned.1.call-start = ((), (), s32[]{:S(2)}) async-start(), calls=%async_computation.1 | async-start | bytes 2949120 | tf_op jit(solution)/shard_map/all_gather | solution.py:389
  7.2 4.6 %collective-permute-start = (bf16[160,512]{1,0:T(8,128)(2,1)}, bf16[160,512]{1,0:T(8,128)(2,1)S(1)}, u32[]{:S(2)}, u32[]{:S(2)}) collective-permute-start(bf16[160,512]{1,0:T(8,128)(2,1)} %here.1), channel_id=1, source_target_pairs={{0,8},{8,0},{1,9},{9,1},{2,10},{10,2},{3,11},{11,3},{4,12},{12,4},... | collective-permute-start | bytes 491528 | tf_op jit(solution)/shard_map/ppermute | solution.py:319
  11.8 0.7 copy-start.8
  14.2 15.2 %collective-permute-start.4 = (bf16[320,512]{1,0:T(8,128)(2,1)}, bf16[320,512]{1,0:T(8,128)(2,1)S(1)}, u32[]{:S(2)}, u32[]{:S(2)}) collective-permute-start(bf16[320,512]{1,0:T(8,128)(2,1)} %shard_map.128.after), channel_id=1, source_target_pairs={{0,192},{1,193},{2,194},{3,195},{4,200},{5,201},{6,202},{7,203},{8... | collective-permute-start | bytes 983048 | tf_op jit(solution)/shard_map/ppermute | solution.py:363
  22.3 10.1 %collective-permute-start.1 = (bf16[208,768]{1,0:T(8,128)(2,1)}, bf16[208,768]{1,0:T(8,128)(2,1)S(1)}, u32[]{:S(2)}, u32[]{:S(2)}) collective-permute-start(bf16[208,768]{1,0:T(8,128)(2,1)} %get-tuple-element.17), channel_id=1, source_target_pairs={{0,8},{8,16},{16,24},{24,32},{32,40},{40,48},{48,56},{56,64},{64,7... | collective-permute-start | bytes 958472 | tf_op jit(solution)/shard_map/ppermute | solution.py:369
  24.2 8.8 %collective-permute-start.2 = (bf16[208,768]{1,0:T(8,128)(2,1)}, bf16[208,768]{1,0:T(8,128)(2,1)}, u32[]{:S(2)}, u32[]{:S(2)}) collective-permute-start(bf16[208,768]{1,0:T(8,128)(2,1)} %get-tuple-element.18), channel_id=1, source_target_pairs={{8,0},{16,8},{24,16},{32,24},{40,32},{48,40},{56,48},{64,56},{72,6... | collective-permute-start | bytes 958472 | tf_op jit(solution)/shard_map/ppermute | solution.py:370
  26.6 22.4 %collective-permute-start.11 = (bf16[672,640]{1,0:T(8,128)(2,1)S(1)}, bf16[672,640]{1,0:T(8,128)(2,1)S(1)}, u32[]{:S(2)}, u32[]{:S(2)}) collective-permute-start(bf16[672,640]{1,0:T(8,128)(2,1)S(1)} %copy-done.5), channel_id=1, source_target_pairs={{0,1},{1,2},{2,3},{3,0},{4,5},{5,6},{6,7},{7,4},{8,9},{9,10},{10,1... | collective-permute-start | bytes 2580488 | tf_op jit(solution)/shard_map/ppermute | solution.py:319
  27.9 21.2 %collective-permute-start.10 = (bf16[672,640]{1,0:T(8,128)(2,1)S(1)}, bf16[672,640]{1,0:T(8,128)(2,1)S(1)}, u32[]{:S(2)}, u32[]{:S(2)}) collective-permute-start(bf16[672,640]{1,0:T(8,128)(2,1)S(1)} %copy-done.5), channel_id=1, source_target_pairs={{0,3},{1,0},{2,1},{3,2},{4,7},{5,4},{6,5},{7,6},{8,11},{9,8},{10,9... | collective-permute-start | bytes 2580488 | tf_op jit(solution)/shard_map/ppermute | solution.py:319
  29.4 0.7 copy-start.7
  30.2 91.5 %reduce-scatter.2.cloned.1.call-start = ((), (), s32[]{:S(2)}) async-start(), calls=%async_computation.2 | async-start | bytes 2949120 | tf_op jit(solution)/shard_map/reduce_scatter | solution.py:404
  32.4 0.7 copy-start.9
  40.4 17.3 %collective-permute-start.3 = (bf16[672,512]{1,0:T(8,128)(2,1)}, bf16[672,512]{1,0:T(8,128)(2,1)}, u32[]{:S(2)}, u32[]{:S(2)}) collective-permute-start(bf16[672,512]{1,0:T(8,128)(2,1)} %get-tuple-element.19), channel_id=1, source_target_pairs={{0,4},{4,0},{1,5},{5,1},{2,6},{6,2},{3,7},{7,3},{8,12},{12,8},{9,1... | collective-permute-start | bytes 2064392 | tf_op jit(solution)/shard_map/ppermute | solution.py:319
  42.5 1.1 copy-start.4
  49.1 12.8 %collective-permute-start.13 = (bf16[336,640]{1,0:T(8,128)(2,1)S(1)}, bf16[336,640]{1,0:T(8,128)(2,1)S(1)}, u32[]{:S(2)}, u32[]{:S(2)}) collective-permute-start(bf16[336,640]{1,0:T(8,128)(2,1)S(1)} %slice.27), channel_id=1, source_target_pairs={{0,1},{1,2},{2,3},{3,0},{4,5},{5,6},{6,7},{7,4},{8,9},{9,10},{10,1... | collective-permute-start | bytes 1290248 | tf_op jit(solution)/shard_map/ppermute | solution.py:319
  49.2 11.8 %collective-permute-start.12 = (bf16[336,640]{1,0:T(8,128)(2,1)S(1)}, bf16[336,640]{1,0:T(8,128)(2,1)S(1)}, u32[]{:S(2)}, u32[]{:S(2)}) collective-permute-start(bf16[336,640]{1,0:T(8,128)(2,1)S(1)} %slice.26), channel_id=1, source_target_pairs={{0,3},{1,0},{2,1},{3,2},{4,7},{5,4},{6,5},{7,6},{8,11},{9,8},{10,9... | collective-permute-start | bytes 1290248 | tf_op jit(solution)/shard_map/ppermute | solution.py:319
  59.0 6.6 %copy-start.6 = (bf16[672,1024]{1,0:T(8,128)(2,1)}, bf16[672,1024]{1,0:T(8,128)(2,1)S(1)}, u32[]{:S(2)}) copy-start(bf16[672,1024]{1,0:T(8,128)(2,1)S(1)} %get-tuple-element.33) | copy-start | bytes 4128772
  61.9 3.7 %copy-start.2 = (bf16[672,2560]{1,0:T(8,128)(2,1)}, bf16[672,2560]{1,0:T(8,128)(2,1)S(1)}, u32[]{:S(2)}) copy-start(bf16[672,2560]{1,0:T(8,128)(2,1)S(1)} %constant_dynamic-update-slice_fusion.6) | copy-start | bytes 10321924
  65.6 6.8 %collective-permute-start.15 = (bf16[1280,1024]{1,0:T(8,128)(2,1)}, bf16[1280,1024]{1,0:T(8,128)(2,1)}, u32[]{:S(2)}, u32[]{:S(2)}) collective-permute-start(bf16[1280,1024]{1,0:T(8,128)(2,1)} %multiply_convert_fusion), channel_id=1, source_target_pairs={{0,8},{8,0},{1,9},{9,1},{2,10},{10,2},{3,11},{11,3},{4,12},{12,4},... | collective-permute-start | bytes 7864328 | tf_op jit(solution)/shard_map/ppermute | solution.py:319
  72.1 10.9 %collective-permute-start.5 = (bf16[2560,512]{1,0:T(8,128)(2,1)}, bf16[2560,512]{1,0:T(8,128)(2,1)}, u32[]{:S(2)}, u32[]{:S(2)}) collective-permute-start(bf16[2560,512]{1,0:T(8,128)(2,1)} %all-gather.2.cloned.1.call-done.refs_1_), channel_id=1, source_target_pairs={{0,8},{8,0},{1,9},{9,1},{2,10},{10,2},{3,11},{11,3},{4,12},{12,4},... | collective-permute-start | bytes 7864328 | tf_op jit(solution)/shard_map/ppermute | solution.py:319
  78.1 4.9 %copy-start.3 = (bf16[672,2560]{1,0:T(8,128)(2,1)S(1)}, bf16[672,2560]{1,0:T(8,128)(2,1)}, u32[]{:S(2)}) copy-start(bf16[672,2560]{1,0:T(8,128)(2,1)} %copy-done.2) | copy-start | bytes 10321924
  83.0 5.0 %copy-start.10 = (bf16[672,512]{1,0:T(8,128)(2,1)}, bf16[672,512]{1,0:T(8,128)(2,1)S(1)}, u32[]{:S(2)}) copy-start(bf16[672,512]{1,0:T(8,128)(2,1)S(1)} %convolution_convert_fusion.1.gm) | copy-start | bytes 2064388
  88.0 4.6 %copy-start.1 = (bf16[2560,512]{1,0:T(8,128)(2,1)S(1)}, bf16[2560,512]{1,0:T(8,128)(2,1)}, u32[]{:S(2)}) copy-start(bf16[2560,512]{1,0:T(8,128)(2,1)} %all-gather.2.cloned.1.call-done.refs_1_) | copy-start | bytes 7864324
  88.0 25.0 %collective-permute-start.14 = (bf16[672,512]{1,0:T(8,128)(2,1)}, bf16[672,512]{1,0:T(8,128)(2,1)}, u32[]{:S(2)}, u32[]{:S(2)}) collective-permute-start(bf16[672,512]{1,0:T(8,128)(2,1)} %get-tuple-element.34), channel_id=1, source_target_pairs={{0,4},{4,0},{1,5},{5,1},{2,6},{6,2},{3,7},{7,3},{8,12},{12,8},{9,1... | collective-permute-start | bytes 2064392 | tf_op jit(solution)/shard_map/ppermute | solution.py:319
  93.4 16.7 %collective-permute-start.6 = (bf16[336,640]{1,0:T(8,128)(2,1)S(1)}, bf16[336,640]{1,0:T(8,128)(2,1)}, u32[]{:S(2)}, u32[]{:S(2)}) collective-permute-start(bf16[336,640]{1,0:T(8,128)(2,1)S(1)} %get-tuple-element.31), channel_id=1, source_target_pairs={{0,1},{1,2},{2,3},{3,0},{4,5},{5,6},{6,7},{7,4},{8,9},{9,10},{10,1... | collective-permute-start | bytes 1290248 | tf_op jit(solution)/shard_map/ppermute | solution.py:319
  94.7 11.0 %collective-permute-start.8 = (bf16[336,640]{1,0:T(8,128)(2,1)S(1)}, bf16[336,640]{1,0:T(8,128)(2,1)S(1)}, u32[]{:S(2)}, u32[]{:S(2)}) collective-permute-start(bf16[336,640]{1,0:T(8,128)(2,1)S(1)} %get-tuple-element.32), channel_id=1, source_target_pairs={{0,3},{1,0},{2,1},{3,2},{4,7},{5,4},{6,5},{7,6},{8,11},{9,8},{10,9... | collective-permute-start | bytes 1290248 | tf_op jit(solution)/shard_map/ppermute | solution.py:319
  107.4 20.8 %collective-permute-start.9 = (bf16[672,640]{1,0:T(8,128)(2,1)}, bf16[672,640]{1,0:T(8,128)(2,1)}, u32[]{:S(2)}, u32[]{:S(2)}) collective-permute-start(bf16[672,640]{1,0:T(8,128)(2,1)} %add_convert_fusion.2.after), channel_id=1, source_target_pairs={{0,3},{1,0},{2,1},{3,2},{4,7},{5,4},{6,5},{7,6},{8,11},{9,8},{10,9... | collective-permute-start | bytes 2580488 | tf_op jit(solution)/shard_map/ppermute | solution.py:319
  113.0 20.5 %collective-permute-start.7 = (bf16[672,640]{1,0:T(8,128)(2,1)}, bf16[672,640]{1,0:T(8,128)(2,1)S(1)}, u32[]{:S(2)}, u32[]{:S(2)}) collective-permute-start(bf16[672,640]{1,0:T(8,128)(2,1)} %add_convert_fusion.3), channel_id=1, source_target_pairs={{0,1},{1,2},{2,3},{3,0},{4,5},{5,6},{6,7},{7,4},{8,9},{9,10},{10,1... | collective-permute-start | bytes 2580488 | tf_op jit(solution)/shard_map/ppermute | solution.py:319
  113.0 20.5 %copy-start = (f32[672,640]{1,0:T(8,128)S(1)}, f32[672,640]{1,0:T(8,128)}, u32[]{:S(2)}) copy-start(f32[672,640]{1,0:T(8,128)} %convolution_add_fusion.refs_1_) | copy-start | bytes 5160964
  123.4 12.5 %collective-permute-start.16 = (bf16[160,512]{1,0:T(8,128)(2,1)}, bf16[160,512]{1,0:T(8,128)(2,1)S(1)}, u32[]{:S(2)}, u32[]{:S(2)}) collective-permute-start(bf16[160,512]{1,0:T(8,128)(2,1)} %get-tuple-element.25), channel_id=1, source_target_pairs={{72,0},{64,32},{0,64},{8,96},{73,1},{65,33},{1,65},{9,97},{74,2},{... | collective-permute-start | bytes 491528 | tf_op jit(solution)/shard_map/ppermute | solution.py:432
  127.3 14.6 %collective-permute-start.17 = (bf16[160,512]{1,0:T(8,128)(2,1)}, bf16[160,512]{1,0:T(8,128)(2,1)S(1)}, u32[]{:S(2)}, u32[]{:S(2)}) collective-permute-start(bf16[160,512]{1,0:T(8,128)(2,1)} %get-tuple-element.26), channel_id=1, source_target_pairs={{88,0},{80,32},{16,64},{24,96},{89,1},{81,33},{17,65},{25,97},{90,... | collective-permute-start | bytes 491528 | tf_op jit(solution)/shard_map/ppermute | solution.py:432
Sparse Core Ops, SparseCore 0:
  30.3 38.4 all-gather.1
  78.2 38.6 reduce-scatter.1

commit v5 on v4

--- a/solution.py
+++ b/solution.py
@@ -173,11 +173,10 @@
 
 
 def bwd_kernel(
-    sel, gm, go, got, pk, p_in, qg, kg, dq, dk, dv, qn, kn, do, dk_acc, dv_acc, p_buf, sems
+    mine, got, pk, p_in, qg, kg, dq, dk, dv, qn, kn, do, dk_acc, dv_acc, p_buf, sems
 ):
     for i in range(NBLK):
         pltpu.make_async_copy(p_in.at[i], p_buf.at[i], sems.at[i]).start()
-    first = sel[0] == 1
     for i in range(NBLK):
         r = slice(BLK * i, BLK * (i + 1))
         for h in range(HEADS + 1):
@@ -188,8 +187,7 @@
             n = (e * lax.rsqrt(ms + EPS) * gain).astype(BF)
             if h < HEADS:
                 qn[r, c] = n
-                own = jnp.where(first, gm[r, c].astype(F32), go[r, c].astype(F32))
-                do[r, c] = (own + got[r, c].astype(F32)).astype(BF)
+                do[r, c] = (mine[r, c].astype(F32) + got[r, c].astype(F32)).astype(BF)
             else:
                 kn[r, :] = n
     dk_acc[...] = jnp.zeros_like(dk_acc)
@@ -226,7 +224,7 @@
         dv[r, :] = dv_acc[r, :].astype(BF)
 
 
-def backward(sel, gm, go, got, pk, p, qg, kg):
+def backward(mine, got, pk, p, qg, kg):
     vm = pl.BlockSpec(memory_space=pltpu.VMEM)
     return pl.pallas_call(
         bwd_kernel,
@@ -235,9 +233,7 @@
             jax.ShapeDtypeStruct((TOK, HEAD), BF),
             jax.ShapeDtypeStruct((TOK, HEAD), BF),
         ),
-        in_specs=[pl.BlockSpec(memory_space=pltpu.SMEM)]
-        + [vm] * 4
-        + [pl.BlockSpec(memory_space=pl.ANY), vm, vm],
+        in_specs=[vm] * 3 + [pl.BlockSpec(memory_space=pl.ANY), vm, vm],
         out_specs=(vm, vm, vm),
         scratch_shapes=[
             pltpu.VMEM((TOK, 512), BF),
@@ -250,7 +246,7 @@
         ],
         compiler_params=params(),
         cost_estimate=cost(6e9, 9e6),
-    )(sel, gm, go, got, pk, p, qg, kg)
+    )(mine, got, pk, p, qg, kg)
 
 
 def halves_kernel(swap, rows, after, out0, out1):
@@ -277,24 +273,6 @@
     )(swap, rows, after)
 
 
-def pair_kernel(swap, here, pair, out):
-    first = swap[0] == 0
-    out[0:160, :] = jnp.where(first, here[...], pair[...])
-    out[160:320, :] = jnp.where(first, pair[...], here[...])
-
-
-def pair_of(swap, here, pair):
-    vm = pl.BlockSpec(memory_space=pltpu.VMEM)
-    return pl.pallas_call(
-        pair_kernel,
-        out_shape=jax.ShapeDtypeStruct((320, 512), BF),
-        in_specs=[pl.BlockSpec(memory_space=pltpu.SMEM), vm, vm],
-        out_specs=vm,
-        compiler_params=params(),
-        cost_estimate=cost(1, 1),
-    )(swap, here, pair)
-
-
 def hold_kernel(*refs):
     pass
 
@@ -357,8 +335,12 @@
     dp = (z * 2 + yl) * 2 + c
     shards = 32
 
-    core = c.astype(jnp.int32)[None]
-    w_chip = pair_of(core, out_weight, shift(out_weight, "c", 1))
+    w_pair = shift(out_weight, "c", 1)
+    w_chip = jnp.where(
+        c == 0,
+        jnp.concatenate([out_weight, w_pair], axis=0),
+        jnp.concatenate([w_pair, out_weight], axis=0),
+    )
 
     w_moved = lax.ppermute(w_chip, ALL, weight_moves())
 
@@ -427,7 +409,7 @@
 
     ready = halves_of(yl.astype(jnp.int32)[None], summed, last)
     query_grad, key_grad, value_grad = backward(
-        same.astype(jnp.int32)[None], part_m, part_o, got_yh, packed, probs, qg, kg
+        jnp.where(same, part_m, part_o), got_yh, packed, probs, qg, kg
     )
     landed = [lax.ppermute(ready[flip], ALL, final_moves(flip)) for flip in (0, 1)]
     weight_grad = landed[0].astype(F32) + landed[1].astype(F32)

time: 151 us -> 149 us (0.987)
  Pallas kernels: 21.8 us -> 19.9 us
    pallas_call x1 -> x0, Pallas kernels: 1.74 us -> none  [pair_of(): pl.pallas_call(pair_kernel, out_shape=jax.ShapeDtypeStruct((320, 512), BF...]
  transfers between devices with their start and end apart: 20 -> 20, of which waited for: 10 -> 11; matrix products, arithmetic and copies ran while one was open for 29% -> 30% of each run, Pallas kernels for 13% -> 13%
where the time goes in v5:
time: 149 us; the launch traced here: 148 us
  starting transfers between devices  35.3 us (24%)
  matrix products  33.5 us (22%)
  waiting for transfers between devices  30.9 us (21%)
  Pallas kernels  19.9 us (13%)
  between operations  14.3 us (10%)
  other arithmetic  11.1 us (7%)
  local copies, waits for them, and re-layouts  2.64 us (2%)
    dot_general x12, matrix products, product(): lax.dot_general(a, b, (((ca,), (cb,)), ((), ())), preferred_element_type=...  33.5 us
    ppermute x13, waiting for transfers between devices, shift(): return lax.ppermute(value, axis, [(i, (i + k) % n) for i in range(n)])  22.4 us
    ppermute x13, starting transfers between devices, shift(): return lax.ppermute(value, axis, [(i, (i + k) % n) for i in range(n)])  19.6 us
    pallas_call x1, Pallas kernels, backward(): pl.pallas_call(bwd_kernel, out_shape=(jax.ShapeDtypeStruct((TOK, 512), BF...  8.42 us
    pallas_call x1, Pallas kernels, forward(): pl.pallas_call(fwd_kernel, out_shape=(jax.ShapeDtypeStruct((TOK, 768), BF...  7.25 us
    ppermute x2, waiting for transfers between devices, body(): lax.ppermute(ready[flip], ALL, final_moves(flip))  6.31 us
    ppermute x1, starting transfers between devices, body(): w_moved = lax.ppermute(w_chip, ALL, weight_moves())  5.63 us
    ppermute x2, starting transfers between devices, body(): lax.ppermute(ready[flip], ALL, final_moves(flip))  4.95 us
  transfers between devices with their start and end apart: 20, of which 11 were waited for; matrix products, arithmetic and copies ran while one was open for 30% of the time, Pallas kernels for 13%

profile of v5, /device:TPU:1, one launch (start us, length us, event | category | flops | bytes accessed | tf_op | source)
XLA Modules:
  0.0 147.7 jit_solution(14297139390083205961)
XLA Ops:
  7.2 3.3 %collective-permute-start = (bf16[160,512]{1,0:T(8,128)(2,1)}, bf16[160,512]{1,0:T(8,128)(2,1)S(1)}, u32[]{:S(2)}, u32[]{:S(2)}) collective-permute-start(bf16[160,512]{1,0:T(8,128)(2,1)} %param.14), channel_id=1, source_target_pairs={{0,8},{8,0},{1,9},{9,1},{2,10},{10,2},{3,11},{11,3},{4,12},{12,4},... | collective-permute-start | bytes 491528 | tf_op jit(solution)/shard_map/ppermute | solution.py:297
  12.9 5.6 %collective-permute-start.4 = (bf16[320,512]{1,0:T(8,128)(2,1)S(1)}, bf16[320,512]{1,0:T(8,128)(2,1)S(1)}, u32[]{:S(2)}, u32[]{:S(2)}) collective-permute-start(bf16[320,512]{1,0:T(8,128)(2,1)S(1)} %maximum_select_fusion.after), channel_id=1, source_target_pairs={{0,192},{1,193},{2,194},{3,195},{4,200},{5,201},{6,202},{7,203},{8... | collective-permute-start | bytes 983048 | tf_op jit(solution)/shard_map/ppermute | solution.py:345
  18.5 2.5 %shard_map.128 = (bf16[208,768]{1,0:T(8,128)(2,1)}, bf16[208,768]{1,0:T(8,128)(2,1)}, s32[8]{0:T(128)}) custom-call(s32[1]{0:T(128)} %bitcast.place, s32[192]{0:T(256)} %lengths.1, s32[192]{0:T(256)} %source.1, bf16[1064,512]{1,0:T(8,128)(2,1)} %q.3, bf16[1064,128]{1,0:T(8,128)(2,1)} %k.3, bf16[1064,128]{1,0:T(8,128)(2,1)} %v.3, bf16[320,512]{1,0:T(8,128)(2,1)} %copy-done.5), custom_call_target="tpu_custom_call" | custom-call | flops 1 | bytes 1 | tf_op jit(solution)/shard_map/pallas_call | solution.py:81
  21.1 1.9 %collective-permute-start.1 = (bf16[208,768]{1,0:T(8,128)(2,1)}, bf16[208,768]{1,0:T(8,128)(2,1)}, u32[]{:S(2)}, u32[]{:S(2)}) collective-permute-start(bf16[208,768]{1,0:T(8,128)(2,1)} %get-tuple-element.17), channel_id=1, source_target_pairs={{0,8},{8,16},{16,24},{24,32},{32,40},{40,48},{48,56},{56,64},{64,7... | collective-permute-start | bytes 958472 | tf_op jit(solution)/shard_map/ppermute | solution.py:351
  23.0 3.1 %collective-permute-start.2 = (bf16[208,768]{1,0:T(8,128)(2,1)}, bf16[208,768]{1,0:T(8,128)(2,1)}, u32[]{:S(2)}, u32[]{:S(2)}) collective-permute-start(bf16[208,768]{1,0:T(8,128)(2,1)} %get-tuple-element.18), channel_id=1, source_target_pairs={{8,0},{16,8},{24,16},{32,24},{40,32},{48,40},{56,48},{64,56},{72,6... | collective-permute-start | bytes 958472 | tf_op jit(solution)/shard_map/ppermute | solution.py:352
  31.8 7.3 %shard_map.129 = (bf16[672,768]{1,0:T(8,128)(2,1)}, f32[6,448,384]{2,1,0:T(8,128)}, bf16[672,512]{1,0:T(8,128)(2,1)}) custom-call(s32[8]{0:T(128)} %get-tuple-element.16.sc, bf16[208,768]{1,0:T(8,128)(2,1)} %collective-permute-done.1.left, bf16[1064,512]{1,0:T(8,128)(2,1)} %q.3, bf16[1064,128]{1,0:T(8,128)(2,1)} %k.3, bf16[1064,128]{1,0:T(8,128)(2,1)} %v.3, ...), custom_call_target="tpu_custom_call" | custom-call | flops 30000001024 | bytes 9000000 | tf_op jit(solution)/shard_map/pallas_call | solution.py:147
  39.1 2.2 %collective-permute-start.3 = (bf16[672,512]{1,0:T(8,128)(2,1)}, bf16[672,512]{1,0:T(8,128)(2,1)}, u32[]{:S(2)}, u32[]{:S(2)}) collective-permute-start(bf16[672,512]{1,0:T(8,128)(2,1)} %get-tuple-element.19), channel_id=1, source_target_pairs={{0,4},{4,0},{1,5},{5,1},{2,6},{6,2},{3,7},{7,3},{8,12},{12,8},{9,1... | collective-permute-start | bytes 2064392 | tf_op jit(solution)/shard_map/ppermute | solution.py:297
  42.5 6.0 %collective-permute-done.11 = bf16[672,640]{1,0:T(8,128)(2,1)S(1)} collective-permute-done((bf16[672,640]{1,0:T(8,128)(2,1)S(1)}, bf16[672,640]{1,0:T(8,128)(2,1)S(1)}, u32[]{:S(2)}, u32[]{:S(2)}) %collective-permute-start.11) | collective-permute-done | bytes 860192 | tf_op jit(solution)/shard_map/ppermute | solution.py:297
  48.7 2.9 %collective-permute-start.12 = (bf16[336,640]{1,0:T(8,128)(2,1)S(1)}, bf16[336,640]{1,0:T(8,128)(2,1)S(1)}, u32[]{:S(2)}, u32[]{:S(2)}) collective-permute-start(bf16[336,640]{1,0:T(8,128)(2,1)S(1)} %slice.26), channel_id=1, source_target_pairs={{0,3},{1,0},{2,1},{3,2},{4,7},{5,4},{6,5},{7,6},{8,11},{9,8},{10,9... | collective-permute-start | bytes 1290248 | tf_op jit(solution)/shard_map/ppermute | solution.py:297
  51.9 4.5 %collective-permute-done.3 = bf16[672,512]{1,0:T(8,128)(2,1)} collective-permute-done((bf16[672,512]{1,0:T(8,128)(2,1)}, bf16[672,512]{1,0:T(8,128)(2,1)}, u32[]{:S(2)}, u32[]{:S(2)}) %collective-permute-start.3) | collective-permute-done | bytes 688160 | tf_op jit(solution)/shard_map/ppermute | solution.py:297
  57.8 2.7 %collective-permute-done.12 = bf16[336,640]{1,0:T(8,128)(2,1)S(1)} collective-permute-done((bf16[336,640]{1,0:T(8,128)(2,1)S(1)}, bf16[336,640]{1,0:T(8,128)(2,1)S(1)}, u32[]{:S(2)}, u32[]{:S(2)}) %collective-permute-start.12) | collective-permute-done | bytes 430112 | tf_op jit(solution)/shard_map/ppermute | solution.py:297
  61.4 3.7 %multiply_convert_fusion = bf16[1280,1024]{1,0:T(8,128)(2,1)} fusion(bf16[672,1024]{1,0:T(8,128)(2,1)S(1)} %get-tuple-element.35, bf16[672,2560]{1,0:T(8,128)(2,1)S(1)} %constant_dynamic-update-slice_fusion.6, s32[]{:T(128)S(6)} %select_n.127), kind=kOutput, calls=%fused_computation.1 | convolution fusion | flops 1764229120 | bytes 5718020 | tf_op jit(solution)/shard_map/dot_general | solution.py:292
  66.0 5.6 %multiply_convert_fusion.1 = bf16[1280,1024]{1,0:T(8,128)(2,1)} fusion(bf16[672,1024]{1,0:T(8,128)(2,1)} %copy-done.7, bf16[672,2560]{1,0:T(8,128)(2,1)} %copy-done.2, s32[]{:T(128)S(6)} %select_n.126), kind=kOutput, calls=%fused_computation.2 | convolution fusion | flops 1764229120 | bytes 5718020 | tf_op jit(solution)/shard_map/dot_general | solution.py:292
  71.6 3.8 %add_convert_fusion = bf16[1280,1024]{1,0:T(8,128)(2,1)S(1)} fusion(bf16[1280,1024]{1,0:T(8,128)(2,1)} %shard_map.132, bf16[1280,1024]{1,0:T(8,128)(2,1)} %multiply_convert_fusion.1), kind=kLoop, calls=%fused_computation | loop fusion | flops 5242880 | bytes 7864320 | tf_op jit(solution)/shard_map/convert_element_type | solution.py:384
  75.6 1.7 %pad_maximum_fusion = bf16[2560,512]{1,0:T(8,128)(2,1)} fusion(bf16[1280,512]{1,0:T(8,128)(2,1)S(1)} %get-tuple-element.28, bf16[1280,512]{1,0:T(8,128)(2,1)S(1)} %get-tuple-element.27), kind=kLoop, calls=%fused_computation.3 | loop fusion | flops 5242880 | bytes 5242880 | tf_op jit(solution)/shard_map/concatenate | solution.py:385
  77.4 4.9 %convolution_convert_fusion.1 = bf16[672,512]{1,0:T(8,128)(2,1)S(1)} fusion(bf16[672,2560]{1,0:T(8,128)(2,1)} %copy-done.2, bf16[2560,512]{1,0:T(8,128)(2,1)} %all-gather.2.cloned.1.call-done.refs_1_), kind=kOutput, calls=%fused_computation.12 | convolution fusion | flops 1761951744 | bytes 6750208 | tf_op jit(solution)/shard_map/dot_general | solution.py:292
  82.2 4.8 %broadcast_select_fusion = (bf16[672,512]{1,0:T(8,128)(2,1)}, bf16[672,512]{1,0:T(8,128)(2,1)}) fusion(bf16[672,512]{1,0:T(8,128)(2,1)S(1)} %convolution_convert_fusion.1, pred[]{:T(512)S(6)} %eq.15, bf16[672,2560]{1,0:T(8,128)(2,1)S(1)} %copy-done.3, bf16[2560,512]{1,0:T(8,128)(2,1)} %collective-permute-done.5), kind=kOutput, calls=%fused_computation.13 | convolution fusion | flops 1762639872 | bytes 8126465 | tf_op jit(solution)/shard_map/dot_general | solution.py:292
  87.0 2.1 %collective-permute-start.14 = (bf16[672,512]{1,0:T(8,128)(2,1)}, bf16[672,512]{1,0:T(8,128)(2,1)}, u32[]{:S(2)}, u32[]{:S(2)}) collective-permute-start(bf16[672,512]{1,0:T(8,128)(2,1)} %get-tuple-element.29), channel_id=1, source_target_pairs={{0,4},{4,0},{1,5},{5,1},{2,6},{6,2},{3,7},{7,3},{8,12},{12,8},{9,1... | collective-permute-start | bytes 2064392 | tf_op jit(solution)/shard_map/ppermute | solution.py:297
  89.1 1.8 %fusion.8 = f32[672,640]{1,0:T(8,128)S(1)} fusion(bf16[672,512]{1,0:T(8,128)(2,1)S(1)} %get-tuple-element.32, bf16[2560,512]{1,0:T(8,128)(2,1)} %collective-permute-done.5, s32[]{:T(128)S(6)} %select_n.119), kind=kOutput, calls=%fused_computation.21 | convolution fusion | flops 440401920 | bytes 3063812 | tf_op jit(solution)/shard_map/dot_general | solution.py:292
  94.5 1.8 %fusion.17 = f32[672,640]{1,0:T(8,128)S(1)} fusion(bf16[672,512]{1,0:T(8,128)(2,1)S(1)} %get-tuple-element.32, bf16[2560,512]{1,0:T(8,128)(2,1)} %collective-permute-done.5, s32[]{:T(128)S(6)} %select_n.110), kind=kOutput, calls=%fused_computation.28 | convolution fusion | flops 440401920 | bytes 3063812 | tf_op jit(solution)/shard_map/dot_general | solution.py:292
  96.4 2.0 %convolution_add_fusion.refs_1_ = f32[672,640]{1,0:T(8,128)} fusion(f32[672,640]{1,0:T(8,128)S(1)} %fusion.17, bf16[672,512]{1,0:T(8,128)(2,1)S(1)} %get-tuple-element.31, bf16[2560,512]{1,0:T(8,128)(2,1)S(1)} %copy-done.1, s32[]{:T(128)S(6)} %select_n.110), kind=kOutput, calls=%fused_computation.10 | convolution fusion | flops 440832000 | bytes 4784132 | tf_op jit(solution)/shard_map/dot_general | solution.py:292
  98.3 1.8 %fusion.2 = f32[672,640]{1,0:T(8,128)S(1)} fusion(bf16[672,512]{1,0:T(8,128)(2,1)S(1)} %get-tuple-element.32, bf16[2560,512]{1,0:T(8,128)(2,1)} %collective-permute-done.5, s32[]{:T(128)S(6)} %select_n.123), kind=kOutput, calls=%fused_computation.17 | convolution fusion | flops 440401920 | bytes 3063812 | tf_op jit(solution)/shard_map/dot_general | solution.py:292
  100.2 1.8 %fusion.11 = f32[672,640]{1,0:T(8,128)S(1)} fusion(bf16[672,512]{1,0:T(8,128)(2,1)S(1)} %get-tuple-element.32, bf16[2560,512]{1,0:T(8,128)(2,1)} %collective-permute-done.5, s32[]{:T(128)S(6)} %select_n.115), kind=kOutput, calls=%fused_computation.24 | convolution fusion | flops 440401920 | bytes 3063812 | tf_op jit(solution)/shard_map/dot_general | solution.py:292
  102.0 2.0 %collective-permute-done.8 = bf16[336,640]{1,0:T(8,128)(2,1)S(1)} collective-permute-done((bf16[336,640]{1,0:T(8,128)(2,1)S(1)}, bf16[336,640]{1,0:T(8,128)(2,1)S(1)}, u32[]{:S(2)}, u32[]{:S(2)}) %collective-permute-start.8) | collective-permute-done | bytes 430112 | tf_op jit(solution)/shard_map/ppermute | solution.py:297
  105.7 2.6 %collective-permute-start.9 = (bf16[672,640]{1,0:T(8,128)(2,1)}, bf16[672,640]{1,0:T(8,128)(2,1)}, u32[]{:S(2)}, u32[]{:S(2)}) collective-permute-start(bf16[672,640]{1,0:T(8,128)(2,1)} %add_convert_fusion.2.after), channel_id=1, source_target_pairs={{0,3},{1,0},{2,1},{3,2},{4,7},{5,4},{6,5},{7,6},{8,11},{9,8},{10,9... | collective-permute-start | bytes 2580488 | tf_op jit(solution)/shard_map/ppermute | solution.py:297
  108.3 2.9 %add_convert_fusion.3 = bf16[672,640]{1,0:T(8,128)(2,1)} fusion(f32[672,640]{1,0:T(8,128)S(1)} %fusion.11, bf16[336,640]{1,0:T(8,128)(2,1)} %shard_map.130, bf16[672,512]{1,0:T(8,128)(2,1)S(1)} %get-tuple-element.31, bf16[2560,512]{1,0:T(8,128)(2,1)} %all-gather.2.cloned.1.call-done.refs_1_, s32[]{:T(128)S(6)} %select_n.115), kind=kOutput, calls=%fused_computation.8 | convolution fusion | flops 442122240 | bytes 4354052 | tf_op jit(solution)/shard_map/dot_general | solution.py:292
  111.2 8.4 %shard_map.131 = (bf16[672,512]{1,0:T(8,128)(2,1)}, bf16[672,128]{1,0:T(8,128)(2,1)}, bf16[672,128]{1,0:T(8,128)(2,1)}) custom-call(bf16[672,512]{1,0:T(8,128)(2,1)} %get-tuple-element.30.mine, bf16[672,512]{1,0:T(8,128)(2,1)} %collective-permute-done.14.got, bf16[672,768]{1,0:T(8,128)(2,1)} %get-tuple-element.20.pk, f32[6,448,384]{2,1,0:T(8,128)} %get-tuple-element.21.p_in, ...), custom_call_target="tpu_custom_call" | custom-call | flops 6000000000 | bytes 9000000 | tf_op jit(solution)/shard_map/pallas_call | solution.py:229
  119.6 1.7 %shard_map.133 = (bf16[160,512]{1,0:T(8,128)(2,1)}, bf16[160,512]{1,0:T(8,128)(2,1)}) custom-call(s32[1]{0:T(128)} %bitcast.3.swap, bf16[320,512]{1,0:T(8,128)(2,1)} %reduce-scatter.2.cloned.1.call-done.rows, bf16[672,640]{1,0:T(8,128)(2,1)} %add_convert_fusion.2.after), custom_call_target="tpu_custom_call" | custom-call | flops 81920 | bytes 1000000 | tf_op jit(solution)/shard_map/pallas_call | solution.py:262
  121.3 4.1 %collective-permute-start.16 = (bf16[160,512]{1,0:T(8,128)(2,1)}, bf16[160,512]{1,0:T(8,128)(2,1)S(1)}, u32[]{:S(2)}, u32[]{:S(2)}) collective-permute-start(bf16[160,512]{1,0:T(8,128)(2,1)} %get-tuple-element.25), channel_id=1, source_target_pairs={{72,0},{64,32},{0,64},{8,96},{73,1},{65,33},{1,65},{9,97},{74,2},{... | collective-permute-start | bytes 491528 | tf_op jit(solution)/shard_map/ppermute | solution.py:414
  126.3 5.1 %collective-permute-done.7 = bf16[672,640]{1,0:T(8,128)(2,1)S(1)} collective-permute-done((bf16[672,640]{1,0:T(8,128)(2,1)}, bf16[672,640]{1,0:T(8,128)(2,1)S(1)}, u32[]{:S(2)}, u32[]{:S(2)}) %collective-permute-start.7) | collective-permute-done | bytes 860192 | tf_op jit(solution)/shard_map/ppermute | solution.py:297
  131.4 2.3 %add_convert_fusion.1 = bf16[672,640]{1,0:T(8,128)(2,1)} fusion(bf16[672,640]{1,0:T(8,128)(2,1)} %collective-permute-done.9, f32[672,640]{1,0:T(8,128)S(1)} %copy-done, bf16[672,640]{1,0:T(8,128)(2,1)S(1)} %collective-permute-done.7), kind=kLoop, calls=%fused_computation.6 | loop fusion | flops 2150400 | bytes 4300800 | tf_op jit(solution)/shard_map/convert_element_type | solution.py:408
  134.1 6.0 %collective-permute-done.17 = bf16[160,512]{1,0:T(8,128)(2,1)S(1)} collective-permute-done((bf16[160,512]{1,0:T(8,128)(2,1)}, bf16[160,512]{1,0:T(8,128)(2,1)S(1)}, u32[]{:S(2)}, u32[]{:S(2)}) %collective-permute-start.17) | collective-permute-done | bytes 163872 | tf_op jit(solution)/shard_map/ppermute | solution.py:414
  (63 shorter events, 20.3 us)
Async XLA Ops:
  7.2 19.0 %copy-start.6 = (bf16[672,640]{1,0:T(8,128)(2,1)S(1)}, bf16[672,640]{1,0:T(8,128)(2,1)}, u32[]{:S(2)}) copy-start(bf16[672,640]{1,0:T(8,128)(2,1)} %param.15) | copy-start | bytes 2580484
  7.2 64.4 %all-gather.2.cloned.1.call-start = ((), (), s32[]{:S(2)}) async-start(), calls=%async_computation.1 | async-start | bytes 2949120 | tf_op jit(solution)/shard_map/all_gather | solution.py:371
  7.2 4.6 %collective-permute-start = (bf16[160,512]{1,0:T(8,128)(2,1)}, bf16[160,512]{1,0:T(8,128)(2,1)S(1)}, u32[]{:S(2)}, u32[]{:S(2)}) collective-permute-start(bf16[160,512]{1,0:T(8,128)(2,1)} %param.14), channel_id=1, source_target_pairs={{0,8},{8,0},{1,9},{9,1},{2,10},{10,2},{3,11},{11,3},{4,12},{12,4},... | collective-permute-start | bytes 491528 | tf_op jit(solution)/shard_map/ppermute | solution.py:297
  12.9 5.6 %copy-start.5 = (bf16[320,512]{1,0:T(8,128)(2,1)}, bf16[320,512]{1,0:T(8,128)(2,1)S(1)}, u32[]{:S(2)}) copy-start(bf16[320,512]{1,0:T(8,128)(2,1)S(1)} %maximum_select_fusion.after) | copy-start | bytes 983044
  12.9 16.0 %collective-permute-start.4 = (bf16[320,512]{1,0:T(8,128)(2,1)S(1)}, bf16[320,512]{1,0:T(8,128)(2,1)S(1)}, u32[]{:S(2)}, u32[]{:S(2)}) collective-permute-start(bf16[320,512]{1,0:T(8,128)(2,1)S(1)} %maximum_select_fusion.after), channel_id=1, source_target_pairs={{0,192},{1,193},{2,194},{3,195},{4,200},{5,201},{6,202},{7,203},{8... | collective-permute-start | bytes 983048 | tf_op jit(solution)/shard_map/ppermute | solution.py:345
  21.1 10.0 %collective-permute-start.1 = (bf16[208,768]{1,0:T(8,128)(2,1)}, bf16[208,768]{1,0:T(8,128)(2,1)}, u32[]{:S(2)}, u32[]{:S(2)}) collective-permute-start(bf16[208,768]{1,0:T(8,128)(2,1)} %get-tuple-element.17), channel_id=1, source_target_pairs={{0,8},{8,16},{16,24},{24,32},{32,40},{40,48},{48,56},{56,64},{64,7... | collective-permute-start | bytes 958472 | tf_op jit(solution)/shard_map/ppermute | solution.py:351
  23.0 8.8 %collective-permute-start.2 = (bf16[208,768]{1,0:T(8,128)(2,1)}, bf16[208,768]{1,0:T(8,128)(2,1)}, u32[]{:S(2)}, u32[]{:S(2)}) collective-permute-start(bf16[208,768]{1,0:T(8,128)(2,1)} %get-tuple-element.18), channel_id=1, source_target_pairs={{8,0},{16,8},{24,16},{32,24},{40,32},{48,40},{56,48},{64,56},{72,6... | collective-permute-start | bytes 958472 | tf_op jit(solution)/shard_map/ppermute | solution.py:352
  26.1 22.4 %collective-permute-start.11 = (bf16[672,640]{1,0:T(8,128)(2,1)S(1)}, bf16[672,640]{1,0:T(8,128)(2,1)S(1)}, u32[]{:S(2)}, u32[]{:S(2)}) collective-permute-start(bf16[672,640]{1,0:T(8,128)(2,1)S(1)} %copy-done.6), channel_id=1, source_target_pairs={{0,1},{1,2},{2,3},{3,0},{4,5},{5,6},{6,7},{7,4},{8,9},{9,10},{10,1... | collective-permute-start | bytes 2580488 | tf_op jit(solution)/shard_map/ppermute | solution.py:297
  27.4 21.2 %collective-permute-start.10 = (bf16[672,640]{1,0:T(8,128)(2,1)S(1)}, bf16[672,640]{1,0:T(8,128)(2,1)S(1)}, u32[]{:S(2)}, u32[]{:S(2)}) collective-permute-start(bf16[672,640]{1,0:T(8,128)(2,1)S(1)} %copy-done.6), channel_id=1, source_target_pairs={{0,3},{1,0},{2,1},{3,2},{4,7},{5,4},{6,5},{7,6},{8,11},{9,8},{10,9... | collective-permute-start | bytes 2580488 | tf_op jit(solution)/shard_map/ppermute | solution.py:297
  28.9 0.7 copy-start.8
  29.6 90.0 %reduce-scatter.2.cloned.1.call-start = ((), (), s32[]{:S(2)}) async-start(), calls=%async_computation.2 | async-start | bytes 2949120 | tf_op jit(solution)/shard_map/reduce_scatter | solution.py:386
  39.1 17.4 %collective-permute-start.3 = (bf16[672,512]{1,0:T(8,128)(2,1)}, bf16[672,512]{1,0:T(8,128)(2,1)}, u32[]{:S(2)}, u32[]{:S(2)}) collective-permute-start(bf16[672,512]{1,0:T(8,128)(2,1)} %get-tuple-element.19), channel_id=1, source_target_pairs={{0,4},{4,0},{1,5},{5,1},{2,6},{6,2},{3,7},{7,3},{8,12},{12,8},{9,1... | collective-permute-start | bytes 2064392 | tf_op jit(solution)/shard_map/ppermute | solution.py:297
  41.3 1.1 copy-start.4
  48.5 12.8 %collective-permute-start.13 = (bf16[336,640]{1,0:T(8,128)(2,1)S(1)}, bf16[336,640]{1,0:T(8,128)(2,1)S(1)}, u32[]{:S(2)}, u32[]{:S(2)}) collective-permute-start(bf16[336,640]{1,0:T(8,128)(2,1)S(1)} %slice.27), channel_id=1, source_target_pairs={{0,1},{1,2},{2,3},{3,0},{4,5},{5,6},{6,7},{7,4},{8,9},{9,10},{10,1... | collective-permute-start | bytes 1290248 | tf_op jit(solution)/shard_map/ppermute | solution.py:297
  48.7 11.8 %collective-permute-start.12 = (bf16[336,640]{1,0:T(8,128)(2,1)S(1)}, bf16[336,640]{1,0:T(8,128)(2,1)S(1)}, u32[]{:S(2)}, u32[]{:S(2)}) collective-permute-start(bf16[336,640]{1,0:T(8,128)(2,1)S(1)} %slice.26), channel_id=1, source_target_pairs={{0,3},{1,0},{2,1},{3,2},{4,7},{5,4},{6,5},{7,6},{8,11},{9,8},{10,9... | collective-permute-start | bytes 1290248 | tf_op jit(solution)/shard_map/ppermute | solution.py:297
  57.8 7.3 %copy-start.7 = (bf16[672,1024]{1,0:T(8,128)(2,1)}, bf16[672,1024]{1,0:T(8,128)(2,1)S(1)}, u32[]{:S(2)}) copy-start(bf16[672,1024]{1,0:T(8,128)(2,1)S(1)} %get-tuple-element.35) | copy-start | bytes 4128772
  61.4 3.7 %copy-start.2 = (bf16[672,2560]{1,0:T(8,128)(2,1)}, bf16[672,2560]{1,0:T(8,128)(2,1)S(1)}, u32[]{:S(2)}) copy-start(bf16[672,2560]{1,0:T(8,128)(2,1)S(1)} %constant_dynamic-update-slice_fusion.6) | copy-start | bytes 10321924
  65.1 6.5 %collective-permute-start.15 = (bf16[1280,1024]{1,0:T(8,128)(2,1)}, bf16[1280,1024]{1,0:T(8,128)(2,1)}, u32[]{:S(2)}, u32[]{:S(2)}) collective-permute-start(bf16[1280,1024]{1,0:T(8,128)(2,1)} %multiply_convert_fusion), channel_id=1, source_target_pairs={{0,8},{8,0},{1,9},{9,1},{2,10},{10,2},{3,11},{11,3},{4,12},{12,4},... | collective-permute-start | bytes 7864328 | tf_op jit(solution)/shard_map/ppermute | solution.py:297
  71.6 10.7 %collective-permute-start.5 = (bf16[2560,512]{1,0:T(8,128)(2,1)}, bf16[2560,512]{1,0:T(8,128)(2,1)}, u32[]{:S(2)}, u32[]{:S(2)}) collective-permute-start(bf16[2560,512]{1,0:T(8,128)(2,1)} %all-gather.2.cloned.1.call-done.refs_1_), channel_id=1, source_target_pairs={{0,8},{8,0},{1,9},{9,1},{2,10},{10,2},{3,11},{11,3},{4,12},{12,4},... | collective-permute-start | bytes 7864328 | tf_op jit(solution)/shard_map/ppermute | solution.py:297
  77.3 4.9 %copy-start.3 = (bf16[672,2560]{1,0:T(8,128)(2,1)S(1)}, bf16[672,2560]{1,0:T(8,128)(2,1)}, u32[]{:S(2)}) copy-start(bf16[672,2560]{1,0:T(8,128)(2,1)} %copy-done.2) | copy-start | bytes 10321924
  87.0 3.9 %copy-start.1 = (bf16[2560,512]{1,0:T(8,128)(2,1)S(1)}, bf16[2560,512]{1,0:T(8,128)(2,1)}, u32[]{:S(2)}) copy-start(bf16[2560,512]{1,0:T(8,128)(2,1)} %all-gather.2.cloned.1.call-done.refs_1_) | copy-start | bytes 7864324
  87.0 24.2 %collective-permute-start.14 = (bf16[672,512]{1,0:T(8,128)(2,1)}, bf16[672,512]{1,0:T(8,128)(2,1)}, u32[]{:S(2)}, u32[]{:S(2)}) collective-permute-start(bf16[672,512]{1,0:T(8,128)(2,1)} %get-tuple-element.29), channel_id=1, source_target_pairs={{0,4},{4,0},{1,5},{5,1},{2,6},{6,2},{3,7},{7,3},{8,12},{12,8},{9,1... | collective-permute-start | bytes 2064392 | tf_op jit(solution)/shard_map/ppermute | solution.py:297
  91.7 16.5 %collective-permute-start.6 = (bf16[336,640]{1,0:T(8,128)(2,1)S(1)}, bf16[336,640]{1,0:T(8,128)(2,1)}, u32[]{:S(2)}, u32[]{:S(2)}) collective-permute-start(bf16[336,640]{1,0:T(8,128)(2,1)S(1)} %get-tuple-element.33), channel_id=1, source_target_pairs={{0,1},{1,2},{2,3},{3,0},{4,5},{5,6},{6,7},{7,4},{8,9},{9,10},{10,1... | collective-permute-start | bytes 1290248 | tf_op jit(solution)/shard_map/ppermute | solution.py:297
  93.0 11.0 %collective-permute-start.8 = (bf16[336,640]{1,0:T(8,128)(2,1)S(1)}, bf16[336,640]{1,0:T(8,128)(2,1)S(1)}, u32[]{:S(2)}, u32[]{:S(2)}) collective-permute-start(bf16[336,640]{1,0:T(8,128)(2,1)S(1)} %get-tuple-element.34), channel_id=1, source_target_pairs={{0,3},{1,0},{2,1},{3,2},{4,7},{5,4},{6,5},{7,6},{8,11},{9,8},{10,9... | collective-permute-start | bytes 1290248 | tf_op jit(solution)/shard_map/ppermute | solution.py:297
  105.7 20.6 %collective-permute-start.9 = (bf16[672,640]{1,0:T(8,128)(2,1)}, bf16[672,640]{1,0:T(8,128)(2,1)}, u32[]{:S(2)}, u32[]{:S(2)}) collective-permute-start(bf16[672,640]{1,0:T(8,128)(2,1)} %add_convert_fusion.2.after), channel_id=1, source_target_pairs={{0,3},{1,0},{2,1},{3,2},{4,7},{5,4},{6,5},{7,6},{8,11},{9,8},{10,9... | collective-permute-start | bytes 2580488 | tf_op jit(solution)/shard_map/ppermute | solution.py:297
  111.2 20.3 %collective-permute-start.7 = (bf16[672,640]{1,0:T(8,128)(2,1)}, bf16[672,640]{1,0:T(8,128)(2,1)S(1)}, u32[]{:S(2)}, u32[]{:S(2)}) collective-permute-start(bf16[672,640]{1,0:T(8,128)(2,1)} %add_convert_fusion.3), channel_id=1, source_target_pairs={{0,1},{1,2},{2,3},{3,0},{4,5},{5,6},{6,7},{7,4},{8,9},{9,10},{10,1... | collective-permute-start | bytes 2580488 | tf_op jit(solution)/shard_map/ppermute | solution.py:297
  111.2 20.3 %copy-start = (f32[672,640]{1,0:T(8,128)S(1)}, f32[672,640]{1,0:T(8,128)}, u32[]{:S(2)}) copy-start(f32[672,640]{1,0:T(8,128)} %convolution_add_fusion.refs_1_) | copy-start | bytes 5160964
  121.3 12.7 %collective-permute-start.16 = (bf16[160,512]{1,0:T(8,128)(2,1)}, bf16[160,512]{1,0:T(8,128)(2,1)S(1)}, u32[]{:S(2)}, u32[]{:S(2)}) collective-permute-start(bf16[160,512]{1,0:T(8,128)(2,1)} %get-tuple-element.25), channel_id=1, source_target_pairs={{72,0},{64,32},{0,64},{8,96},{73,1},{65,33},{1,65},{9,97},{74,2},{... | collective-permute-start | bytes 491528 | tf_op jit(solution)/shard_map/ppermute | solution.py:414
  125.5 14.6 %collective-permute-start.17 = (bf16[160,512]{1,0:T(8,128)(2,1)}, bf16[160,512]{1,0:T(8,128)(2,1)S(1)}, u32[]{:S(2)}, u32[]{:S(2)}) collective-permute-start(bf16[160,512]{1,0:T(8,128)(2,1)} %get-tuple-element.26), channel_id=1, source_target_pairs={{88,0},{80,32},{16,64},{24,96},{89,1},{81,33},{17,65},{25,97},{90,... | collective-permute-start | bytes 491528 | tf_op jit(solution)/shard_map/ppermute | solution.py:414
Sparse Core Ops, SparseCore 0:
  29.8 37.7 all-gather.1
  77.5 37.7 reduce-scatter.1
